TPU v7x, 32 devices: a whole 2x2x4 slice. The times are simulated.
32 devices in a mesh: dp: 8 (over y, x, core), expert: 4 (over z).
Axes of the slice: x: 2, y: 2, z: 4, core: 2. Of those that a mesh axis runs over, the one named last changes fastest.
Arguments:
- tokens: bfloat16 [4096, 4096], P(('dp', 'expert')), may hold values from -6 to 6
- out_grad: bfloat16 [4096, 4096], P(('dp', 'expert')), may hold values from -6 to 6
- routes: int32 [4096, 2], P(('dp', 'expert')), may hold values from 0 to 3, all different within a row; in each aligned block of 128 rows (0 to 127, 128 to 255, ...) at most 64 rows name the same one
- gate_probs: bfloat16 [4096, 2], P(('dp', 'expert')), may hold values from 0.19921875 to 1
- w_gate: bfloat16 [4, 4096, 768], P('expert'), may hold values from -0.09375 to 0.09375
- w_up: bfloat16 [4, 4096, 768], P('expert'), may hold values from -0.09375 to 0.09375
- w_down: bfloat16 [4, 768, 4096], P('expert'), may hold values from -0.21875 to 0.21875
Outputs:
- x_grad: bfloat16 [4096, 4096], P(('dp', 'expert'))
- prob_grad: bfloat16 [4096, 2], P(('dp', 'expert'))
- gate_grad: float32 [4, 4096, 768], P('expert', 'dp')
- up_grad: float32 [4, 4096, 768], P('expert', 'dp')
- down_grad: float32 [4, 768, 4096], P('expert', None, 'dp')
Inputs may be any that keep to these rules, and one draw needn't show every extreme that they name: `routes`: each token names 2 different experts; the 128 tokens of one device (aligned blocks of rows) name one expert at most 64 times, a bound that some block reaches.
All inputs are finite; a program needn't handle non-finite values.
Results may differ from a plain program's by a relative error of at most 0.013.
Values may be sent and summed in bfloat16 or wider, within the bound.
No kernel may reach another device: no remote copies, remote signals or barrier semaphores. Data moves between devices by JAX's collectives and lax.ppermute only.
A program may use at most 192 MiB of HBM per device.

v0:
```python
import math

import jax
import jax.numpy as jnp
from jax import lax
from jax.sharding import PartitionSpec as P

CAP = 64


def contract_rows(left, right):
    return lax.dot_general(
        left, right, (((0,), (0,)), ((), ())), preferred_element_type=jnp.float32
    )


def body(tokens, out_grad, routes, gate_probs, w_gate, w_up, w_down):
    tok_count, width = tokens.shape
    top_count = routes.shape[1]
    experts = lax.axis_size("expert")
    replicas = lax.axis_size("dp")
    hidden = w_gate.shape[2]
    routed = tok_count * top_count
    row_total = experts * CAP
    grad_scale = 1.0 / math.sqrt(tok_count * replicas * experts)
    prob_scale = 1.0 / math.sqrt(width)
    flat_route = routes.reshape(routed)
    onehot = (flat_route[:, None] == jnp.arange(experts, dtype=jnp.int32)[None, :]).astype(
        jnp.int32
    )
    position = jnp.sum((jnp.cumsum(onehot, axis=0) - 1) * onehot, axis=1)
    target = flat_route * CAP + position
    slot_source = (
        jnp.full((row_total,), routed, jnp.int32)
        .at[target]
        .set(jnp.arange(routed, dtype=jnp.int32))
    )
    filled = slot_source < routed
    source = jnp.minimum(slot_source, routed - 1)
    token_index = source // top_count
    zero_value = jnp.zeros((), jnp.bfloat16)
    tok_send = jnp.where(filled[:, None], tokens[token_index], zero_value).reshape(
        experts, CAP, width
    )
    cot_send = jnp.where(filled[:, None], out_grad[token_index], zero_value).reshape(
        experts, CAP, width
    )
    prob_send = jnp.where(filled, gate_probs.reshape(routed)[source], zero_value).reshape(
        experts, CAP
    )
    tok_recv, cot_recv, prob_recv = (
        lax.all_to_all(tok_send, "expert", split_axis=0, concat_axis=0, tiled=True),
        lax.all_to_all(cot_send, "expert", split_axis=0, concat_axis=0, tiled=True),
        lax.all_to_all(prob_send, "expert", split_axis=0, concat_axis=0, tiled=True),
    )
    x_rows = tok_recv.reshape(row_total, width)
    g_rows = cot_recv.reshape(row_total, width)
    prob_rows = prob_recv.reshape(row_total).astype(jnp.float32)[:, None]
    gate_matrix = w_gate[0]
    up_matrix = w_up[0]
    down_matrix = w_down[0]
    gate_pre = jnp.dot(x_rows, gate_matrix, preferred_element_type=jnp.float32)
    up_pre = jnp.dot(x_rows, up_matrix, preferred_element_type=jnp.float32)
    sigmoid_gate = jax.nn.sigmoid(gate_pre)
    activation = (gate_pre * sigmoid_gate * up_pre).astype(jnp.bfloat16)
    back_hidden = lax.dot_general(
        g_rows, down_matrix, (((1,), (1,)), ((), ())), preferred_element_type=jnp.float32
    )
    hidden_grad = prob_rows * back_hidden
    gate_delta = (
        hidden_grad * up_pre * sigmoid_gate * (1.0 + gate_pre * (1.0 - sigmoid_gate))
    ).astype(jnp.bfloat16)
    up_delta = (hidden_grad * gate_pre * sigmoid_gate).astype(jnp.bfloat16)
    out_delta = (prob_rows * g_rows.astype(jnp.float32)).astype(jnp.bfloat16)
    row_grad = (
        lax.dot_general(
            gate_delta, gate_matrix, (((1,), (1,)), ((), ())), preferred_element_type=jnp.float32
        )
        + lax.dot_general(
            up_delta, up_matrix, (((1,), (1,)), ((), ())), preferred_element_type=jnp.float32
        )
    ).astype(jnp.bfloat16)
    outputs = jnp.dot(activation, down_matrix, preferred_element_type=jnp.float32)
    prob_rows_grad = jnp.sum(g_rows.astype(jnp.float32) * outputs, axis=1) * prob_scale
    back_rows, back_probs = (
        lax.all_to_all(
            row_grad.reshape(experts, CAP, width), "expert", split_axis=0, concat_axis=0, tiled=True
        ),
        lax.all_to_all(
            prob_rows_grad.astype(jnp.bfloat16).reshape(experts, CAP),
            "expert",
            split_axis=0,
            concat_axis=0,
            tiled=True,
        ),
    )
    picked_rows = back_rows.reshape(row_total, width)[target].reshape(tok_count, top_count, width)
    x_grad = jnp.sum(picked_rows.astype(jnp.float32), axis=1).astype(jnp.bfloat16)
    prob_grad = back_probs.reshape(row_total)[target].reshape(tok_count, top_count)
    hidden_pair = jnp.concatenate([gate_delta, up_delta], axis=1)
    paired = contract_rows(x_rows, hidden_pair)
    downward = contract_rows(out_delta, activation)
    summed = lax.psum_scatter(
        (jnp.concatenate([paired, downward], axis=1) * grad_scale).astype(jnp.bfloat16),
        "dp",
        scatter_dimension=0,
        tiled=True,
    ).astype(jnp.float32)
    gate_grad = summed[:, :hidden][None]
    up_grad = summed[:, hidden : 2 * hidden][None]
    down_grad = summed[:, 2 * hidden :].T[None]
    return (x_grad, prob_grad, gate_grad, up_grad, down_grad)


def solution(mesh):
    return jax.shard_map(
        body,
        mesh=mesh,
        in_specs=(
            P(("dp", "expert"), None),
            P(("dp", "expert"), None),
            P(("dp", "expert"), None),
            P(("dp", "expert"), None),
            P("expert", None, None),
            P("expert", None, None),
            P("expert", None, None),
        ),
        out_specs=(
            P(("dp", "expert"), None),
            P(("dp", "expert"), None),
            P("expert", "dp", None),
            P("expert", "dp", None),
            P("expert", None, "dp"),
        ),
        check_vma=False,
    )
```

profile of v0, /device:TPU:0, one launch (start us, length us, event | category | flops | bytes accessed | tf_op | source)
XLA Modules:
  0.0 326.9 jit_solution(14643023157458716303)
XLA Ops:
  9.0 0.8 copy.30
  10.2 1.2 reduce-window.6
  11.9 1.4 scatter_custom_fusion
  13.3 1.9 gather_fusion
  15.9 6.3 %all-to-all-start = ((bf16[4,1,64]{2,1,0:T(2,128)(2,1)}), bf16[4,1,64]{2,1,0:T(2,128)(2,1)S(1)}, u32[]{:S(2)}, u32[]{:S(2)}) async-start(bf16[4,1,64]{2,1,0:T(2,128)(2,1)} %all_to_all.25), calls=%async_computation | async-start | bytes 4096 | tf_op jit(solution)/shard_map/all_to_all | solution.py:54
  22.3 3.2 gather_fusion.2
  25.5 3.1 gather_fusion.1
  28.6 4.6 %broadcast_select_fusion.1 = (bf16[4,64,4096]{2,1,0:T(8,128)(2,1)}, bf16[4,64,4096]{2,1,0:T(8,128)(2,1)}) fusion(bf16[4,64,4096]{2,1,0:T(8,128)(2,1)} %bitcast.73, pred[4,64]{1,0:T(4,128)(4,1)S(1)} %broadcast_in_dim.47, bf16[4,64,4096]{2,1,0:T(8,128)(2,1)} %bitcast.72), kind=kLoop, calls=%fused_computation.28 | loop fusion | flops 2097152 | bytes 8388864 | tf_op jit(solution)/shard_map/jit(_where)/select_n | solution.py:45
  33.2 52.8 %all_to_all.31 = bf16[4,64,4096]{2,1,0:T(8,128)(2,1)S(1)} all-to-all(bf16[4,64,4096]{2,1,0:T(8,128)(2,1)} %get-tuple-element.31), channel_id=1, replica_groups=mesh['dp'=8,'expert'=4] {'expert'}, dimensions={0} | all-to-all | bytes 4194304 | tf_op jit(solution)/shard_map/all_to_all | solution.py:52
  86.0 4.5 %all-to-all-start.1 = ((bf16[4,64,4096]{2,1,0:T(8,128)(2,1)}), bf16[4,64,4096]{2,1,0:T(8,128)(2,1)}, u32[]{:S(2)}, u32[]{:S(2)}) async-start(bf16[4,64,4096]{2,1,0:T(8,128)(2,1)} %get-tuple-element.30), calls=%async_computation.1 | async-start | bytes 4194304 | tf_op jit(solution)/shard_map/all_to_all | solution.py:53
  90.8 5.4 %fusion.3 = f32[256,768]{1,0:T(8,128)} fusion(bf16[256,4096]{1,0:T(8,128)(2,1)S(1)} %bitcast.68, bf16[1,4096,768]{2,1,0:T(8,128)(2,1)} %param.11), kind=kOutput, calls=%fused_computation.10 | convolution fusion | flops 1610612736 | bytes 9175040 | tf_op jit(solution)/shard_map/dot_general | solution.py:62
  96.2 41.5 %all-to-all-done.1 = bf16[4,64,4096]{2,1,0:T(8,128)(2,1)} async-done(((bf16[4,64,4096]{2,1,0:T(8,128)(2,1)}), bf16[4,64,4096]{2,1,0:T(8,128)(2,1)}, u32[]{:S(2)}, u32[]{:S(2)}) %all-to-all-start.1) | async-done | bytes 2097184 | tf_op jit(solution)/shard_map/all_to_all | solution.py:53
  137.8 5.3 %fusion.29 = f32[256,768]{1,0:T(8,128)S(1)} fusion(bf16[256,4096]{1,0:T(8,128)(2,1)} %bitcast.5, bf16[1,768,4096]{2,1,0:T(8,128)(2,1)} %param.13, f32[256]{0:T(256)S(1)} %reshape.139), kind=kOutput, calls=%fused_computation.33 | convolution fusion | flops 1610809344 | bytes 9176064 | tf_op jit(solution)/shard_map/dot_general | solution.py:66
  143.1 4.8 %multiply_convert_fusion = (bf16[256,768]{1,0:T(8,128)(2,1)S(1)}, bf16[256,768]{1,0:T(8,128)(2,1)S(1)}, bf16[256,768]{1,0:T(8,128)(2,1)S(1)}) fusion(f32[256,768]{1,0:T(8,128)S(1)} %copy-done.3, f32[256,768]{1,0:T(8,128)S(1)} %fusion.29, bf16[256,4096]{1,0:T(8,128)(2,1)S(1)} %bitcast.69, bf16[1,4096,768]{2,1,0:T(8,128)(2,1)} %param.12), kind=kOutput, calls=%fused_computation.38 | convolution fusion | flops 1613758464 | bytes 11141120 | tf_op jit(solution)/shard_map/dot_general | solution.py:63
  147.9 8.0 %fusion.23 = f32[4096,768]{0,1:T(8,128)} fusion(bf16[256,768]{1,0:T(8,128)(2,1)S(1)} %get-tuple-element.25, bf16[256,4096]{1,0:T(8,128)(2,1)} %bitcast.5, f32[256]{0:T(256)S(1)} %reshape.139), kind=kOutput, calls=%fused_computation.25 | convolution fusion | flops 1613758464 | bytes 15074304 | tf_op jit(solution)/shard_map/dot_general | solution.py:12
  155.9 10.1 %fusion.32 = f32[4096,1536]{0,1:T(8,128)} fusion(bf16[256,4096]{1,0:T(8,128)(2,1)S(1)} %bitcast.70, bf16[256,768]{1,0:T(8,128)(2,1)S(1)} %get-tuple-element.27, bf16[256,768]{1,0:T(8,128)(2,1)S(1)} %get-tuple-element.26), kind=kOutput, calls=%fused_computation.34 | convolution fusion | flops 3222798336 | bytes 28049408 | tf_op jit(solution)/shard_map/dot_general | solution.py:12
  166.0 19.5 %fusion = bf16[4096,2304]{0,1:T(8,128)(2,1)} fusion(f32[4096,768]{0,1:T(8,128)} %fusion.23, f32[4096,1536]{0,1:T(8,128)} %fusion.32), kind=kLoop, calls=%fused_computation.7 | loop fusion | flops 28311552 | bytes 56623104 | tf_op jit(solution)/shard_map/convert_element_type | solution.py:104
  185.5 5.4 %fusion.26 = f32[256]{0:T(256)S(1)} fusion(bf16[256,768]{1,0:T(8,128)(2,1)S(1)} %get-tuple-element.25, bf16[1,768,4096]{2,1,0:T(8,128)(2,1)} %param.13, bf16[256,4096]{1,0:T(8,128)(2,1)} %bitcast.5), kind=kOutput, calls=%fused_computation.32 | convolution fusion | flops 1613758208 | bytes 8782848 | tf_op jit(solution)/shard_map/dot_general | solution.py:83
  191.6 3.5 %all-to-all-start.4 = ((bf16[4,1,64]{2,1,0:T(2,128)(2,1)}), bf16[4,1,64]{2,1,0:T(2,128)(2,1)S(1)}, u32[]{:S(2)}, u32[]{:S(2)}) async-start(bf16[4,1,64]{2,1,0:T(2,128)(2,1)} %convert_element_type.70), calls=%async_computation.4 | async-start | bytes 4096 | tf_op jit(solution)/shard_map/all_to_all | solution.py:89
  195.0 6.0 %fusion.1 = f32[256,4096]{1,0:T(8,128)S(1)} fusion(bf16[256,768]{1,0:T(8,128)(2,1)S(1)} %get-tuple-element.26, bf16[1,4096,768]{2,1,0:T(8,128)(2,1)} %param.11), kind=kOutput, calls=%fused_computation.8 | convolution fusion | flops 1610612736 | bytes 10878976 | tf_op jit(solution)/shard_map/dot_general | solution.py:76
  201.2 3.1 fusion.19
  204.3 4.8 %all-to-all-start.3 = ((bf16[4,64,4096]{2,1,0:T(8,128)(2,1)}), bf16[4,64,4096]{2,1,0:T(8,128)(2,1)S(1)}, u32[]{:S(2)}, u32[]{:S(2)}) async-start(bf16[4,64,4096]{2,1,0:T(8,128)(2,1)} %bitcast.71), calls=%async_computation.3 | async-start | bytes 4194304 | tf_op jit(solution)/shard_map/all_to_all | solution.py:86
  209.3 1.9 gather_fusion.4
  211.9 44.4 %all-to-all-done.3 = bf16[4,64,4096]{2,1,0:T(8,128)(2,1)S(1)} async-done(((bf16[4,64,4096]{2,1,0:T(8,128)(2,1)}), bf16[4,64,4096]{2,1,0:T(8,128)(2,1)S(1)}, u32[]{:S(2)}, u32[]{:S(2)}) %all-to-all-start.3) | async-done | bytes 2097184 | tf_op jit(solution)/shard_map/all_to_all | solution.py:86
  256.3 3.2 gather_fusion.3
  259.5 3.2 reshape.136
  262.6 7.2 %reduce_sum.34 = bf16[128,4096]{1,0:T(8,128)(2,1)} reduce(bf16[128,2,4096]{2,1,0:T(2,128)(2,1)S(1)} %reshape.136, bf16[]{:T(256)} %constant.34.clone.1), dimensions={1}, to_apply=%region_4.5 | reduce | flops 524288 | bytes 3145730 | tf_op jit(solution)/shard_map/reduce_sum | solution.py:98
  269.8 41.0 %reduce-scatter.2.cloned.1.call-done = bf16[512,2304]{0,1:T(8,128)(2,1)} async-done(((bf16[4096,2304]{0,1:T(8,128)(2,1)}), bf16[512,2304]{0,1:T(8,128)(2,1)}) %reduce-scatter.2.cloned.1.call-update) | async-done | bytes 2359312 | tf_op jit(solution)/shard_map/reduce_scatter | solution.py:103
  310.8 2.3 convert_element_type.68
  313.1 2.2 slice_bitcast_fusion
  315.3 3.1 copy.35
  318.4 1.6 copy.34
  (48 shorter events, 5.5 us)
Async XLA Ops:
  7.2 15.1 %copy-start = (bf16[128,4096]{1,0:T(8,128)(2,1)S(1)}, bf16[128,4096]{1,0:T(8,128)(2,1)}, u32[]{:S(2)}) copy-start(bf16[128,4096]{1,0:T(8,128)(2,1)} %param.7) | copy-start | bytes 3145732
  15.9 17.3 %all-to-all-start = ((bf16[4,1,64]{2,1,0:T(2,128)(2,1)}), bf16[4,1,64]{2,1,0:T(2,128)(2,1)S(1)}, u32[]{:S(2)}, u32[]{:S(2)}) async-start(bf16[4,1,64]{2,1,0:T(2,128)(2,1)} %all_to_all.25), calls=%async_computation | async-start | bytes 4096 | tf_op jit(solution)/shard_map/all_to_all | solution.py:54
  22.3 3.2 copy-start.2
  86.0 51.8 %all-to-all-start.1 = ((bf16[4,64,4096]{2,1,0:T(8,128)(2,1)}), bf16[4,64,4096]{2,1,0:T(8,128)(2,1)}, u32[]{:S(2)}, u32[]{:S(2)}) async-start(bf16[4,64,4096]{2,1,0:T(8,128)(2,1)} %get-tuple-element.30), calls=%async_computation.1 | async-start | bytes 4194304 | tf_op jit(solution)/shard_map/all_to_all | solution.py:53
  90.4 220.4 %reduce-scatter.2.cloned.1.call-start = ((), (), s32[]{:S(2)}) async-start(), calls=%async_computation.6 | async-start | bytes 21233664 | tf_op jit(solution)/shard_map/reduce_scatter | solution.py:103
  137.8 5.3 %copy-start.3 = (f32[256,768]{1,0:T(8,128)S(1)}, f32[256,768]{1,0:T(8,128)}, u32[]{:S(2)}) copy-start(f32[256,768]{1,0:T(8,128)} %fusion.3) | copy-start | bytes 2359300
  185.4 15.6 %slice-start = ((s8[6291456]{0:T(1024)(128)(4,1)}), s8[2097152]{0:T(1024)(128)(4,1)S(1)}, s32[]{:S(2)}) async-start(s8[6291456]{0:T(1024)(128)(4,1)} %bitcast.74), calls=%async_computation.7 | async-start | bytes 4194304
  191.6 12.7 %all-to-all-start.4 = ((bf16[4,1,64]{2,1,0:T(2,128)(2,1)}), bf16[4,1,64]{2,1,0:T(2,128)(2,1)S(1)}, u32[]{:S(2)}, u32[]{:S(2)}) async-start(bf16[4,1,64]{2,1,0:T(2,128)(2,1)} %convert_element_type.70), calls=%async_computation.4 | async-start | bytes 4096 | tf_op jit(solution)/shard_map/all_to_all | solution.py:89
  195.0 6.1 %slice-start.1 = ((s8[6291456]{0:T(1024)(128)(4,1)}), s8[4194304]{0:T(1024)(128)(4,1)S(1)}, s32[]{:S(2)}) async-start(s8[6291456]{0:T(1024)(128)(4,1)} %bitcast.74), calls=%async_computation.8 | async-start | bytes 8388608
  204.3 52.0 %all-to-all-start.3 = ((bf16[4,64,4096]{2,1,0:T(8,128)(2,1)}), bf16[4,64,4096]{2,1,0:T(8,128)(2,1)S(1)}, u32[]{:S(2)}, u32[]{:S(2)}) async-start(bf16[4,64,4096]{2,1,0:T(8,128)(2,1)} %bitcast.71), calls=%async_computation.3 | async-start | bytes 4194304 | tf_op jit(solution)/shard_map/all_to_all | solution.py:86
  315.3 4.7 %copy-start.1 = (bf16[128,4096]{1,0:T(8,128)(2,1)S(1)}, bf16[128,4096]{1,0:T(8,128)(2,1)}, u32[]{:S(2)}) copy-start(bf16[128,4096]{1,0:T(8,128)(2,1)} %param.7) | copy-start | bytes 3145732
Sparse Core Ops, SparseCore 0:
  185.6 125.1 reduce-scatter.1
where the time goes:
time: 328 us; the launch traced here: 327 us
  waiting for transfers between devices  127 us (39%)
  blocking collectives  52.8 us (16%)
  matrix products  48.2 us (15%)
  other arithmetic  35.8 us (11%)
  local copies, waits for them, and re-layouts  29.7 us (9%)
  starting transfers between devices  19.3 us (6%)
  between operations  14.2 us (4%)
    all_to_all x1, blocking collectives, body(): lax.all_to_all(tok_send, 'expert', split_axis=0, concat_axis=0, tiled=True)  52.8 us
    all_to_all x1, waiting for transfers between devices, body(): lax.all_to_all(row_grad.reshape(experts, CAP, width), 'expert', split_axi...  44.4 us
    all_to_all x1, waiting for transfers between devices, body(): lax.all_to_all(cot_send, 'expert', split_axis=0, concat_axis=0, tiled=True)  41.5 us
    reduce_scatter x1, waiting for transfers between devices, body(): lax.psum_scatter((jnp.concatenate([paired, downward], axis=1) * grad_scal...  41 us
    convert_element_type x1, other arithmetic, body(): (jnp.concatenate([paired, downward], axis=1) * grad_scale).astype(jnp.bfl...  19.5 us
    dot_general x2, matrix products, contract_rows(): lax.dot_general(left, right, (((0,), (0,)), ((), ())), preferred_element_...  18.1 us
    reduce_sum x1, other arithmetic, body(): jnp.sum(picked_rows.astype(jnp.float32), axis=1).astype(jnp.bfloat16)  7.19 us
    unnamed x17, local copies, waits for them, and re-layouts  7.05 us
  transfers between devices with their start and end apart: 5, of which 3 were waited for; matrix products, arithmetic and copies ran while one was open for 15% of the time, Pallas kernels for 0%

commit v1 on v0

v1 whole, which is shorter than its diff:
```python
import functools
import math

import jax
import jax.numpy as jnp
from jax import lax
from jax.experimental import pallas as pl
from jax.experimental.pallas import tpu as pltpu
from jax.sharding import PartitionSpec as P

CAP = 64
CHUNKS = 2
EXTRA = 128
F32 = jnp.float32
BF16 = jnp.bfloat16
VMEM_LIMIT = 48 * 1024 * 1024


def whole(shape):
    return pl.BlockSpec(shape, lambda i, pos: (0,) * len(shape))


def call(kernel, grid, in_specs, out_specs, out_shape, pos, args, flops=0, scratch=()):
    moved = sum(a.size * a.dtype.itemsize for a in args)
    moved += sum(math.prod(o.shape) * o.dtype.itemsize for o in jax.tree.leaves(out_shape))
    return pl.pallas_call(
        kernel,
        grid_spec=pltpu.PrefetchScalarGridSpec(
            num_scalar_prefetch=1,
            grid=grid,
            in_specs=in_specs,
            out_specs=out_specs,
            scratch_shapes=list(scratch),
        ),
        out_shape=out_shape,
        compiler_params=pltpu.CompilerParams(vmem_limit_bytes=VMEM_LIMIT),
        cost_estimate=pl.CostEstimate(flops=flops, bytes_accessed=moved, transcendentals=0),
    )(pos, *args)


def shape_of(shape, dtype=BF16):
    return jax.ShapeDtypeStruct(shape, dtype)


def dot(left, right):
    return jnp.dot(left, right, preferred_element_type=F32)


def dot_t(left, right):
    return lax.dot_general(left, right, (((1,), (1,)), ((), ())), preferred_element_type=F32)


def shard_at(i, me, replicas):
    half = replicas // 2
    return jnp.where(i < half, 2 * i + 1, 2 * i - replicas) ^ me


def slot_expert(rows, cols, my_expert):
    return (lax.broadcasted_iota(jnp.int32, (rows, cols), 1) // CAP) ^ my_expert


def slot_matrix(routes_ref, my_expert, slots):
    tok = routes_ref.shape[0]
    expert = slot_expert(tok, slots, my_expert)
    hit = jnp.zeros((tok, slots), jnp.bool_)
    for k in range(routes_ref.shape[1]):
        hit = hit | (routes_ref[:, k : k + 1] == expert)
    named = jnp.where(hit, 1.0, 0.0)
    before = lax.broadcasted_iota(jnp.int32, (tok, tok), 1) < lax.broadcasted_iota(
        jnp.int32, (tok, tok), 0
    )
    rank = dot(jnp.where(before, 1.0, 0.0).astype(BF16), named.astype(BF16))
    place = (lax.broadcasted_iota(jnp.int32, (tok, slots), 1) % CAP).astype(F32)
    return jnp.where(rank == place, named, 0.0), expert


def send_tokens_kernel(experts, pos_ref, routes_ref, tok_ref, *rest):
    outs, place_ref, pt_ref = rest[:experts], rest[experts], rest[experts + 1]

    @pl.when(pl.program_id(0) == 0)
    def _():
        place, _ = slot_matrix(routes_ref, pos_ref[1], experts * CAP)
        place_ref[...] = place.astype(BF16)
        pt_ref[...] = place.T.astype(BF16)

    rows = dot(pt_ref[...], tok_ref[...]).astype(BF16)
    for j in range(experts):
        outs[j][...] = rows[j * CAP : (j + 1) * CAP]


def send_cot_kernel(experts, pos_ref, routes_ref, probs_ref, cot_ref, dep_ref, *rest):
    outs, pt_ref = rest[:experts], rest[experts]

    @pl.when(pl.program_id(0) == 0)
    def _():
        place, expert = slot_matrix(routes_ref, pos_ref[1], experts * CAP)
        probs = probs_ref[...].astype(F32)
        weight = jnp.zeros_like(place)
        for k in range(routes_ref.shape[1]):
            weight += jnp.where(routes_ref[:, k : k + 1] == expert, probs[:, k : k + 1], 0.0)
        pt_ref[...] = (place * weight).T.astype(BF16)

    rows = dot(pt_ref[...], cot_ref[...]).astype(BF16)
    for j in range(experts):
        outs[j][...] = rows[j * CAP : (j + 1) * CAP]


def forward_kernel(experts, replicas, pos_ref, *rest):
    xs, (wg_ref, wu_ref), outs, x_ref = (
        rest[:experts],
        rest[experts : experts + 2],
        rest[experts + 2 : -1],
        rest[-1],
    )
    act_ref, act_t_ref, for_gate_ref, for_up_ref = outs

    @pl.when(pl.program_id(0) == 0)
    def _():
        for j in range(experts):
            x_ref[j * CAP : (j + 1) * CAP, :] = xs[j][...]

    width = wg_ref.shape[1] // replicas
    gate = jnp.zeros(act_ref.shape, F32)
    up = jnp.zeros(act_ref.shape, F32)
    for i in range(replicas):
        at = pl.ds(pl.multiple_of(shard_at(i, pos_ref[0], replicas) * width, width), width)
        part = x_ref[:, i * width : (i + 1) * width]
        gate += dot(part, wg_ref[0, at, :])
        up += dot(part, wu_ref[0, at, :])
    sig = jax.nn.sigmoid(gate)
    silu = gate * sig
    act = silu * up
    act_ref[...] = act.astype(BF16)
    act_t_ref[...] = act.T.astype(BF16)
    for_gate_ref[...] = up * sig * (1.0 + gate * (1.0 - sig))
    for_up_ref[...] = silu


def transpose_kernel(experts, pos_ref, *rest):
    rows = jnp.concatenate([ref[...] for ref in rest[:experts]], axis=0)
    rest[experts][...] = rows.T


def down_far_kernel(experts, scale, pos_ref, act_t_ref, *rest):
    rows = jnp.concatenate([ref[...] for ref in rest[:experts]], axis=0)
    rest[experts][...] = (dot(act_t_ref[...], rows) * scale).astype(BF16)


def scatter_pieces(part, q, outs):
    low_send, low_keep, high_send, high_keep = outs
    pieces = pl.num_programs(0)
    half = part.shape[0] // 2

    @pl.when(q % 2 == 1)
    def _():
        low_send[0] = part[:half].astype(BF16)

    @pl.when(q % 2 == 0)
    def _():
        low_keep[0] = part[:half]

    @pl.when(q >= pieces // 2)
    def _():
        high_send[0] = part[half:].astype(BF16)

    @pl.when(q < pieces // 2)
    def _():
        high_keep[0] = part[half:]


def scatter_specs(pieces, rows, cols):
    block = (1, rows // 2, cols)
    half = pieces // 2
    specs = [
        pl.BlockSpec(block, lambda q, pos: (q // 2, 0, 0)),
        pl.BlockSpec(block, lambda q, pos: (q // 2, 0, 0)),
        pl.BlockSpec(block, lambda q, pos: (jnp.maximum(q - half, 0), 0, 0)),
        pl.BlockSpec(block, lambda q, pos: (jnp.minimum(q, half - 1), 0, 0)),
    ]
    shapes = [shape_of((half, rows // 2, cols), t) for t in (BF16, F32, BF16, F32)]
    return specs, shapes


def down_near_kernel(experts, scale, pos_ref, act_t_ref, other_ref, *rest):
    rows = jnp.concatenate([ref[...] for ref in rest[:experts]], axis=0)
    part = dot(act_t_ref[...], rows) * scale + other_ref[...].astype(F32)
    scatter_pieces(part, pl.program_id(0), rest[experts:])


def back_hidden_kernel(experts, last, pos_ref, wd_ref, *rest):
    i = pl.program_id(0)
    rows = jnp.concatenate([ref[...] for ref in rest[:experts]], axis=0)
    rest = rest[experts:]
    if last:
        prev_ref, act_ref, for_gate_ref, for_up_ref, dh_ref, du_ref, prob_ref, sum_ref = rest
    else:
        (sum_ref,) = rest
    term = dot_t(rows, wd_ref[0])

    @pl.when(i == 0)
    def _():
        sum_ref[...] = term + prev_ref[...] if last else term

    @pl.when(i > 0)
    def _():
        sum_ref[...] += term

    if last:

        @pl.when(i == pl.num_programs(0) - 1)
        def _():
            back = sum_ref[...]
            dh_ref[...] = (back * for_gate_ref[...]).astype(BF16)
            du_ref[...] = (back * for_up_ref[...]).astype(BF16)
            prob_ref[...] = jnp.sum(act_ref[...].astype(F32) * back, axis=1, keepdims=True)


def grad_far_kernel(scale, pos_ref, xt_ref, delta_ref, out_ref):
    out_ref[...] = (dot(xt_ref[...], delta_ref[...]) * scale).astype(BF16)


def grad_near_kernel(scale, pos_ref, xt_ref, delta_ref, other_ref, *outs):
    part = dot(xt_ref[...], delta_ref[...]) * scale + other_ref[...].astype(F32)
    scatter_pieces(part, pl.program_id(0), outs)


def row_grad_kernel(experts, pos_ref, dh_ref, du_ref, prob_ref, wg_ref, wu_ref, *outs):
    i = pl.program_id(0)
    width = wg_ref.shape[1]
    rows = (dot_t(dh_ref[...], wg_ref[0]) + dot_t(du_ref[...], wu_ref[0])).astype(BF16)
    at = pl.ds(pl.multiple_of(i * width, width), width)
    for j in range(experts):
        outs[j][:, at] = rows[j * CAP : (j + 1) * CAP]

    @pl.when(i == 0)
    def _():
        full = prob_ref[...]
        high = full.astype(BF16).astype(F32)
        lane = lax.broadcasted_iota(jnp.int32, (full.shape[0], EXTRA), 1)
        both = jnp.where(lane == 0, high, jnp.where(lane == 1, full - high, 0.0)).astype(BF16)
        for j in range(experts):
            outs[j][:, outs[j].shape[1] - EXTRA :] = both[j * CAP : (j + 1) * CAP]


def combine_kernel(experts, scale, pos_ref, place_ref, routes_ref, probs_ref, *rest):
    backs, extras = rest[:experts], rest[experts : 2 * experts]
    x_ref, prob_ref = rest[2 * experts :]
    rows = jnp.concatenate([ref[...] for ref in backs], axis=0)
    x_ref[...] = dot(place_ref[...], rows).astype(BF16)

    @pl.when(pl.program_id(0) == 0)
    def _():
        place = place_ref[...].astype(F32)
        extra = jnp.concatenate([ref[...] for ref in extras], axis=0)
        expert = slot_expert(place.shape[0], place.shape[1], pos_ref[1])
        probs = probs_ref[...].astype(F32)
        lane = lax.broadcasted_iota(jnp.int32, probs.shape, 1)
        result = jnp.zeros(probs.shape, F32)
        for k in range(routes_ref.shape[1]):
            mine = jnp.where(routes_ref[:, k : k + 1] == expert, place, 0.0).astype(BF16)
            found = jnp.sum(dot(mine, extra), axis=1, keepdims=True)
            result += jnp.where(lane == k, found, 0.0)
        prob_ref[...] = (result * scale / probs).astype(BF16)


def flip(x, axis, bit):
    count = lax.axis_size(axis)
    return lax.ppermute(x, axis, [(i, i ^ bit) for i in range(count)])


def halve(send, keep, bits, low):
    for at, bit in enumerate(bits):
        total = keep + flip(send, "dp", bit).astype(F32)
        if at + 1 == len(bits):
            return total[0]
        if low:
            pairs = total.reshape(total.shape[0] // 2, 2, *total.shape[1:])
            send, keep = pairs[:, 1].astype(BF16), pairs[:, 0]
        else:
            half = total.shape[0] // 2
            send, keep = total[half:].astype(BF16), total[:half]


def body(tokens, out_grad, routes, gate_probs, w_gate, w_up, w_down):
    tok, width = tokens.shape
    experts = lax.axis_size("expert")
    replicas = lax.axis_size("dp")
    hidden = w_gate.shape[2]
    slots = experts * CAP
    shard = width // replicas
    pieces = replicas // 2
    grad_scale = 1.0 / math.sqrt(tok * replicas * experts)
    prob_scale = 1.0 / math.sqrt(width)
    pos = jnp.stack([lax.axis_index("dp"), lax.axis_index("expert")]).astype(jnp.int32)
    bits = [1 << (b + 1) for b in range(pieces.bit_length() - 1)]

    def exchange(blocks):
        return [blocks[0]] + [flip(blocks[j], "expert", j) for j in range(experts - 1, 0, -1)][::-1]

    def block_specs(cols, at):
        return [pl.BlockSpec((CAP, cols), at) for _ in range(experts)]

    *x_out, place = call(
        functools.partial(send_tokens_kernel, experts),
        (replicas,),
        [
            whole(routes.shape),
            pl.BlockSpec((tok, shard), lambda i, pos: (0, shard_at(i, pos[0], replicas))),
        ],
        block_specs(shard, lambda i, pos: (0, i)) + [whole((tok, slots))],
        [shape_of((CAP, width)) for _ in range(experts)] + [shape_of((tok, slots))],
        pos,
        [routes, tokens],
        flops=2 * tok * slots * width,
        scratch=[pltpu.VMEM((slots, tok), BF16)],
    )
    x_in = exchange(x_out)

    part = shard // CHUNKS
    cols = width // CHUNKS

    def send_cot(c, dep):
        out = call(
            functools.partial(send_cot_kernel, experts),
            (replicas,),
            [
                whole(routes.shape),
                whole(gate_probs.shape),
                pl.BlockSpec(
                    (tok, part), lambda i, pos: (0, shard_at(i, pos[0], replicas) * CHUNKS + c)
                ),
                pl.BlockSpec(memory_space=pl.ANY),
            ],
            block_specs(part, lambda i, pos: (0, i)),
            [shape_of((CAP, cols)) for _ in range(experts)],
            pos,
            [routes, gate_probs, out_grad, dep],
            flops=2 * tok * slots * cols,
            scratch=[pltpu.VMEM((slots, tok), BF16)],
        )
        return exchange(out)

    dy = [send_cot(0, place)]
    for c in range(1, CHUNKS):
        dy.append(send_cot(c, dy[c - 1][1] if c > 1 else x_in[1]))

    hid = hidden // 3
    act, act_t, for_gate, for_up = call(
        functools.partial(forward_kernel, experts, replicas),
        (3,),
        [whole((CAP, width)) for _ in range(experts)]
        + [pl.BlockSpec((1, width, hid), lambda i, pos: (0, 0, i)) for _ in range(2)],
        [
            pl.BlockSpec((slots, hid), lambda i, pos: (0, i)),
            pl.BlockSpec((hid, slots), lambda i, pos: (i, 0)),
            pl.BlockSpec((slots, hid), lambda i, pos: (0, i)),
            pl.BlockSpec((slots, hid), lambda i, pos: (0, i)),
        ],
        [
            shape_of((slots, hidden)),
            shape_of((hidden, slots)),
            shape_of((slots, hidden), F32),
            shape_of((slots, hidden), F32),
        ],
        pos,
        [*x_in, w_gate, w_up],
        flops=4 * slots * width * hidden,
        scratch=[pltpu.VMEM((slots, width), BF16)],
    )
    (x_t,) = call(
        functools.partial(transpose_kernel, experts),
        (replicas,),
        block_specs(shard, lambda i, pos: (0, i)),
        [pl.BlockSpec((shard, slots), lambda i, pos: (i, 0))],
        [shape_of((width, slots))],
        pos,
        x_in,
    )

    down_parts = []
    back = None
    for c in range(CHUNKS):
        (far,) = call(
            functools.partial(down_far_kernel, experts, grad_scale),
            (pieces,),
            [whole((hidden, slots))] + block_specs(part, lambda i, pos: (0, i)),
            [pl.BlockSpec((hidden, part), lambda i, pos: (0, i))],
            [shape_of((hidden, pieces * part))],
            pos,
            [act_t, *dy[c]],
            flops=hidden * slots * cols,
        )
        other = flip(far, "dp", 1)
        last = c + 1 == CHUNKS
        specs = [
            pl.BlockSpec(
                (1, hidden, part),
                lambda i, pos, c=c: (0, 0, shard_at(i, pos[0], replicas) * CHUNKS + c),
            )
        ] + block_specs(part, lambda i, pos: (0, i))
        full = whole((slots, hidden))
        if last:
            dh, du, prob = call(
                functools.partial(back_hidden_kernel, experts, True),
                (replicas,),
                specs + [full] * 4,
                [full, full, whole((slots, 1))],
                [
                    shape_of((slots, hidden)),
                    shape_of((slots, hidden)),
                    shape_of((slots, 1), F32),
                ],
                pos,
                [w_down, *dy[c], back, act, for_gate, for_up],
                flops=2 * slots * hidden * cols,
                scratch=[pltpu.VMEM((slots, hidden), F32)],
            )
        else:
            (back,) = call(
                functools.partial(back_hidden_kernel, experts, False),
                (replicas,),
                specs,
                [full],
                [shape_of((slots, hidden), F32)],
                pos,
                [w_down, *dy[c]],
                flops=2 * slots * hidden * cols,
            )
        out_specs, out_shapes = scatter_specs(pieces, hidden, part)
        low_send, low_keep, high_send, high_keep = call(
            functools.partial(down_near_kernel, experts, grad_scale),
            (pieces,),
            [whole((hidden, slots)), pl.BlockSpec((hidden, part), lambda i, pos: (0, i))]
            + block_specs(part, lambda i, pos: (0, i + pieces)),
            out_specs,
            out_shapes,
            pos,
            [act_t, other, *dy[c]],
            flops=hidden * slots * cols,
        )
        low = halve(low_send, low_keep, bits, True)
        high = halve(high_send, high_keep, bits[::-1], False)
        down_parts.append(jnp.concatenate([low, high], axis=0))
    down_grad = jnp.concatenate(down_parts, axis=1)[None]

    fars = []
    for delta in (dh, du):
        (far,) = call(
            functools.partial(grad_far_kernel, grad_scale),
            (pieces,),
            [pl.BlockSpec((shard, slots), lambda i, pos: (i, 0)), whole((slots, hidden))],
            [pl.BlockSpec((shard, hidden), lambda i, pos: (i, 0))],
            [shape_of((pieces * shard, hidden))],
            pos,
            [x_t, delta],
            flops=width * slots * hidden,
        )
        fars.append(flip(far, "dp", 1))

    back_out = call(
        functools.partial(row_grad_kernel, experts),
        (8,),
        [whole((slots, hidden)), whole((slots, hidden)), whole((slots, 1))]
        + [pl.BlockSpec((1, width // 8, hidden), lambda i, pos: (0, i, 0)) for _ in range(2)],
        [whole((CAP, width + EXTRA)) for _ in range(experts)],
        [shape_of((CAP, width + EXTRA)) for _ in range(experts)],
        pos,
        [dh, du, prob, w_gate, w_up],
        flops=4 * slots * width * hidden,
    )
    back_in = exchange(back_out)

    grads = []
    for delta, other in zip((dh, du), fars):
        out_specs, out_shapes = scatter_specs(pieces, shard, hidden)
        low_send, low_keep, high_send, high_keep = call(
            functools.partial(grad_near_kernel, grad_scale),
            (pieces,),
            [
                pl.BlockSpec((shard, slots), lambda i, pos: (i + pieces, 0)),
                whole((slots, hidden)),
                pl.BlockSpec((shard, hidden), lambda i, pos: (i, 0)),
            ],
            out_specs,
            out_shapes,
            pos,
            [x_t, delta, other],
            flops=width * slots * hidden,
        )
        low = halve(low_send, low_keep, bits, True)
        high = halve(high_send, high_keep, bits[::-1], False)
        grads.append(jnp.concatenate([low, high], axis=0)[None])

    step = width // 8
    x_grad, prob_grad = call(
        functools.partial(combine_kernel, experts, prob_scale),
        (8,),
        [whole((tok, slots)), whole(routes.shape), whole(gate_probs.shape)]
        + block_specs(step, lambda i, pos: (0, i))
        + block_specs(EXTRA, lambda i, pos: (0, width // EXTRA)),
        [pl.BlockSpec((tok, step), lambda i, pos: (0, i)), whole(gate_probs.shape)],
        [shape_of((tok, width)), shape_of(gate_probs.shape)],
        pos,
        [place, routes, gate_probs, *back_in, *back_in],
        flops=2 * tok * slots * width,
    )
    return (x_grad, prob_grad, grads[0], grads[1], down_grad)


def solution(mesh):
    return jax.shard_map(
        body,
        mesh=mesh,
        in_specs=(
            P(("dp", "expert"), None),
            P(("dp", "expert"), None),
            P(("dp", "expert"), None),
            P(("dp", "expert"), None),
            P("expert", None, None),
            P("expert", None, None),
            P("expert", None, None),
        ),
        out_specs=(
            P(("dp", "expert"), None),
            P(("dp", "expert"), None),
            P("expert", "dp", None),
            P("expert", "dp", None),
            P("expert", None, "dp"),
        ),
        check_vma=False,
    )
```

time: 328 us -> 310 us (0.945); the launches traced: 327 us -> 305 us
  Pallas kernels: 0 us -> 76.1 us
  blocking collectives: 52.8 us -> 0 us
  matrix products: 48.2 us -> 0 us
  waiting for transfers between devices: 127 us -> 171 us
  other arithmetic: 35.8 us -> 6.56 us
  starting transfers between devices: 19.3 us -> 46.4 us
  local copies, waits for them, and re-layouts: 29.7 us -> 4.7 us
  between operations: 14.2 us -> 1.16 us
    ppermute x0 -> x32, waiting for transfers between devices: none -> 171 us  [flip(): return lax.ppermute(x, axis, [(i, i ^ bit) for i in range(count)])]
    all_to_all x4 -> x0, waiting for transfers between devices: 85.9 us -> none  [the longest x1 44.4 us: body(): lax.all_to_all(row_grad.reshape(experts, CAP, width), 'expert', split_axi...]
    pallas_call x0 -> x17, Pallas kernels: none -> 76.1 us  [call(): pl.pallas_call(kernel, grid_spec=pltpu.PrefetchScalarGridSpec(num_scalar_...]
    all_to_all x1 -> x0, blocking collectives: 52.8 us -> none  [body(): lax.all_to_all(tok_send, 'expert', split_axis=0, concat_axis=0, tiled=True)]
    dot_general x8 -> x0, matrix products: 48.2 us -> none  [the longest x2 18.1 us: contract_rows(): lax.dot_general(left, right, (((0,), (0,)), ((), ())), preferred_element_...]
    ppermute x0 -> x32, starting transfers between devices: none -> 46.4 us  [flip(): return lax.ppermute(x, axis, [(i, i ^ bit) for i in range(count)])]
    reduce_scatter x1 -> x0, waiting for transfers between devices: 41 us -> none  [body(): lax.psum_scatter((jnp.concatenate([paired, downward], axis=1) * grad_scal...]
    convert_element_type x5 -> x0, other arithmetic: 21.8 us -> none  [the longest x1 19.5 us: body(): (jnp.concatenate([paired, downward], axis=1) * grad_scale).astype(jnp.bfl...]
  transfers between devices with their start and end apart: 5 -> 32, of which waited for: 3 -> 15; matrix products, arithmetic and copies ran while one was open for 15% -> 2% of each run, Pallas kernels for 0% -> 23%
where the time goes in v1:
time: 310 us; the launch traced here: 305 us
  waiting for transfers between devices  171 us (55%)
  Pallas kernels  76.1 us (25%)
  starting transfers between devices  46.4 us (15%)
  other arithmetic  6.56 us (2%)
  local copies, waits for them, and re-layouts  4.7 us (2%)
    ppermute x32, waiting for transfers between devices, flip(): return lax.ppermute(x, axis, [(i, i ^ bit) for i in range(count)])  171 us
    pallas_call x17, Pallas kernels, call(): pl.pallas_call(kernel, grid_spec=pltpu.PrefetchScalarGridSpec(num_scalar_...  76.1 us
    ppermute x32, starting transfers between devices, flip(): return lax.ppermute(x, axis, [(i, i ^ bit) for i in range(count)])  46.4 us
  transfers between devices with their start and end apart: 32, of which 15 were waited for; matrix products, arithmetic and copies ran while one was open for 2% of the time, Pallas kernels for 23%

profile of v1, /device:TPU:0, one launch (start us, length us, event | category | flops | bytes accessed | tf_op | source)
XLA Modules:
  0.0 305.4 jit_solution(14788985355102176045)
XLA Ops:
  2.8 4.8 %shard_map.110 = (bf16[64,4096]{1,0:T(8,128)(2,1)S(1)}, bf16[64,4096]{1,0:T(8,128)(2,1)}, bf16[64,4096]{1,0:T(8,128)(2,1)}, bf16[64,4096]{1,0:T(8,128)(2,1)}, bf16[128,256]{1,0:T(8,128)(2,1)S(1)}) custom-call(s32[2]{0:T(128)S(1)} %pad_add_fusion.pos_ref, s32[128,2]{1,0:T(8,128)S(1)} %copy.12.routes_ref, bf16[128,4096]{1,0:T(8,128)(2,1)S(1)} %copy-done.16), custom_call_target="tpu_custom_call" | custom-call | flops 268435456 | bytes 3212288 | tf_op jit(solution)/shard_map/pallas_call | solution.py:26
  7.6 3.1 %collective-permute-start = (bf16[64,4096]{1,0:T(8,128)(2,1)}, bf16[64,4096]{1,0:T(8,128)(2,1)S(1)}, u32[]{:S(2)}, u32[]{:S(2)}) collective-permute-start(bf16[64,4096]{1,0:T(8,128)(2,1)} %get-tuple-element.48), channel_id=1, source_target_pairs={{0,1},{1,0},{2,3},{3,2},{4,5},{5,4},{6,7},{7,6},{8,9},{9,8},{10,11... | collective-permute-start | bytes 1572872 | tf_op jit(solution)/shard_map/ppermute | solution.py:268
  17.7 3.5 %collective-permute-start.5 = (bf16[64,2048]{1,0:T(8,128)(2,1)S(1)}, bf16[64,2048]{1,0:T(8,128)(2,1)S(1)}, u32[]{:S(2)}, u32[]{:S(2)}) collective-permute-start(bf16[64,2048]{1,0:T(8,128)(2,1)S(1)} %get-tuple-element.55), channel_id=1, source_target_pairs={{0,2},{1,3},{2,0},{3,1},{4,6},{5,7},{6,4},{7,5},{8,10},{9,11},{10,... | collective-permute-start | bytes 786440 | tf_op jit(solution)/shard_map/ppermute | solution.py:268
  21.2 12.9 %collective-permute-done.dep_ref.rest_1_ = bf16[64,4096]{1,0:T(8,128)(2,1)S(1)} collective-permute-done((bf16[64,4096]{1,0:T(8,128)(2,1)}, bf16[64,4096]{1,0:T(8,128)(2,1)S(1)}, u32[]{:S(2)}, u32[]{:S(2)}) %collective-permute-start) | collective-permute-done | bytes 524320 | tf_op jit(solution)/shard_map/ppermute | solution.py:268
  34.1 4.6 %collective-permute-start.6 = (bf16[64,2048]{1,0:T(8,128)(2,1)S(1)}, bf16[64,2048]{1,0:T(8,128)(2,1)S(1)}, u32[]{:S(2)}, u32[]{:S(2)}) collective-permute-start(bf16[64,2048]{1,0:T(8,128)(2,1)S(1)} %get-tuple-element.56), channel_id=1, source_target_pairs={{0,3},{1,2},{2,1},{3,0},{4,7},{5,6},{6,5},{7,4},{8,11},{9,10},{10,... | collective-permute-start | bytes 786440 | tf_op jit(solution)/shard_map/ppermute | solution.py:268
  38.7 10.5 %collective-permute-done.7.rest_2_ = bf16[64,4096]{1,0:T(8,128)(2,1)S(1)} collective-permute-done((bf16[64,4096]{1,0:T(8,128)(2,1)}, bf16[64,4096]{1,0:T(8,128)(2,1)S(1)}, u32[]{:S(2)}, u32[]{:S(2)}) %collective-permute-start.7) | collective-permute-done | bytes 524320 | tf_op jit(solution)/shard_map/ppermute | solution.py:268
  49.2 8.0 %shard_map.114 = (bf16[256,768]{1,0:T(8,128)(2,1)S(1)}, bf16[768,256]{1,0:T(8,128)(2,1)S(1)}, f32[256,768]{1,0:T(8,128)S(1)}, f32[256,768]{1,0:T(8,128)S(1)}) custom-call(s32[2]{0:T(128)S(1)} %pad_add_fusion.pos_ref, bf16[64,4096]{1,0:T(8,128)(2,1)S(1)} %get-tuple-element.57.rest_0_, bf16[64,4096]{1,0:T(8,128)(2,1)S(1)} %collective-permute-done.dep_ref.rest_1_, ...), custom_call_target="tpu_custom_call" | custom-call | flops 3221225472 | bytes 17039360 | tf_op jit(solution)/shard_map/pallas_call | solution.py:26
  57.3 20.0 %collective-permute-done.5.rest_2_ = bf16[64,2048]{1,0:T(8,128)(2,1)S(1)} collective-permute-done((bf16[64,2048]{1,0:T(8,128)(2,1)S(1)}, bf16[64,2048]{1,0:T(8,128)(2,1)S(1)}, u32[]{:S(2)}, u32[]{:S(2)}) %collective-permute-start.5) | collective-permute-done | bytes 262176 | tf_op jit(solution)/shard_map/ppermute | solution.py:268
  81.9 4.8 %collective-permute-start.1 = (bf16[64,2048]{1,0:T(8,128)(2,1)S(1)}, bf16[64,2048]{1,0:T(8,128)(2,1)S(1)}, u32[]{:S(2)}, u32[]{:S(2)}) collective-permute-start(bf16[64,2048]{1,0:T(8,128)(2,1)S(1)} %get-tuple-element.50), channel_id=1, source_target_pairs={{0,1},{1,0},{2,3},{3,2},{4,5},{5,4},{6,7},{7,6},{8,9},{9,8},{10,11... | collective-permute-start | bytes 786440 | tf_op jit(solution)/shard_map/ppermute | solution.py:268
  89.2 9.7 %collective-permute-done.1.rest_1_ = bf16[64,2048]{1,0:T(8,128)(2,1)S(1)} collective-permute-done((bf16[64,2048]{1,0:T(8,128)(2,1)S(1)}, bf16[64,2048]{1,0:T(8,128)(2,1)S(1)}, u32[]{:S(2)}, u32[]{:S(2)}) %collective-permute-start.1) | collective-permute-done | bytes 262176 | tf_op jit(solution)/shard_map/ppermute | solution.py:268
  98.9 9.2 %collective-permute-done.2.rest_2_ = bf16[64,2048]{1,0:T(8,128)(2,1)S(1)} collective-permute-done((bf16[64,2048]{1,0:T(8,128)(2,1)S(1)}, bf16[64,2048]{1,0:T(8,128)(2,1)S(1)}, u32[]{:S(2)}, u32[]{:S(2)}) %collective-permute-start.2) | collective-permute-done | bytes 262176 | tf_op jit(solution)/shard_map/ppermute | solution.py:268
  111.0 6.6 %shard_map.113.rest_4_ = f32[256,768]{1,0:T(8,128)S(1)} custom-call(s32[2]{0:T(128)S(1)} %pad_add_fusion.pos_ref, bf16[1,768,4096]{2,1,0:T(8,128)(2,1)} %wd_ref.3, bf16[64,2048]{1,0:T(8,128)(2,1)S(1)} %get-tuple-element.53.rest_0_, bf16[64,2048]{1,0:T(8,128)(2,1)S(1)} %collective-permute-done.4.rest_1_, bf16[64,2048]{1,0:T(8,128)(2,1)S(1)} %collective-permute-done.5.rest_2_, ...), custom_call_target="tpu_custom_call" | custom-call | flops 805306368 | bytes 8126464 | tf_op jit(solution)/shard_map/pallas_call | solution.py:26
  119.5 7.0 %shard_map.115 = (bf16[256,768]{1,0:T(8,128)(2,1)S(1)}, bf16[256,768]{1,0:T(8,128)(2,1)S(1)}, f32[256,1]{1,0:T(8,128)S(1)}) custom-call(s32[2]{0:T(128)S(1)} %pad_add_fusion.pos_ref, bf16[1,768,4096]{2,1,0:T(8,128)(2,1)} %wd_ref.3, bf16[64,2048]{1,0:T(8,128)(2,1)S(1)} %get-tuple-element.49.rest_0_, bf16[64,2048]{1,0:T(8,128)(2,1)S(1)} %collective-permute-done.1.rest_1_, ...), custom_call_target="tpu_custom_call" | custom-call | flops 805306368 | bytes 10880000 | tf_op jit(solution)/shard_map/pallas_call | solution.py:26
  126.5 3.5 %shard_map.121 = bf16[2048,768]{1,0:T(8,128)(2,1)} custom-call(s32[2]{0:T(128)S(1)} %pad_add_fusion.pos_ref, bf16[4096,256]{1,0:T(8,128)(2,1)S(1)} %shard_map.118.xt_ref, bf16[256,768]{1,0:T(8,128)(2,1)S(1)} %get-tuple-element.64.du_ref.delta_ref), custom_call_target="tpu_custom_call" | custom-call | flops 805306368 | bytes 5636096 | tf_op jit(solution)/shard_map/pallas_call | solution.py:26
  130.5 9.6 %shard_map.116 = (bf16[64,4224]{1,0:T(8,128)(2,1)S(1)}, bf16[64,4224]{1,0:T(8,128)(2,1)S(1)}, bf16[64,4224]{1,0:T(8,128)(2,1)S(1)}, bf16[64,4224]{1,0:T(8,128)(2,1)S(1)}) custom-call(s32[2]{0:T(128)S(1)} %pad_add_fusion.pos_ref, bf16[256,768]{1,0:T(8,128)(2,1)S(1)} %get-tuple-element.63.dh_ref.delta_ref, ...), custom_call_target="tpu_custom_call" | custom-call | flops 3221225472 | bytes 15533056 | tf_op jit(solution)/shard_map/pallas_call | solution.py:26
  140.1 6.5 %collective-permute-start.10 = (bf16[64,4224]{1,0:T(8,128)(2,1)S(1)}, bf16[64,4224]{1,0:T(8,128)(2,1)S(1)}, u32[]{:S(2)}, u32[]{:S(2)}) collective-permute-start(bf16[64,4224]{1,0:T(8,128)(2,1)S(1)} %get-tuple-element.68), channel_id=1, source_target_pairs={{0,2},{1,3},{2,0},{3,1},{4,6},{5,7},{6,4},{7,5},{8,10},{9,11},{10,... | collective-permute-start | bytes 1622024 | tf_op jit(solution)/shard_map/ppermute | solution.py:268
  148.0 3.3 %shard_map.124 = (bf16[2,384,256]{2,1,0:T(8,128)(2,1)}, f32[2,384,256]{2,1,0:T(8,128)S(1)}, bf16[2,384,256]{2,1,0:T(8,128)(2,1)}, f32[2,384,256]{2,1,0:T(8,128)S(1)}) custom-call(s32[2]{0:T(128)S(1)} %pad_add_fusion.pos_ref, bf16[768,256]{1,0:T(8,128)(2,1)S(1)} %get-tuple-element.80.act_t_ref, bf16[768,1024]{1,0:T(8,128)(2,1)S(1)} %collective-permute-done.22.other_ref, ...), custom_call_target="tpu_custom_call" | custom-call | flops 402653184 | bytes 5373952 | tf_op jit(solution)/shard_map/pallas_call | solution.py:26
  152.2 30.8 %collective-permute-done.10.rest_2_.rest_6_ = bf16[64,4224]{1,0:T(8,128)(2,1)S(1)} collective-permute-done((bf16[64,4224]{1,0:T(8,128)(2,1)S(1)}, bf16[64,4224]{1,0:T(8,128)(2,1)S(1)}, u32[]{:S(2)}, u32[]{:S(2)}) %collective-permute-start.10) | collective-permute-done | bytes 540704 | tf_op jit(solution)/shard_map/ppermute | solution.py:268
  184.4 3.5 %shard_map.119 = bf16[2048,768]{1,0:T(8,128)(2,1)} custom-call(s32[2]{0:T(128)S(1)} %pad_add_fusion.pos_ref, bf16[4096,256]{1,0:T(8,128)(2,1)S(1)} %shard_map.118.xt_ref, bf16[256,768]{1,0:T(8,128)(2,1)S(1)} %get-tuple-element.63.dh_ref.delta_ref), custom_call_target="tpu_custom_call" | custom-call | flops 805306368 | bytes 5636096 | tf_op jit(solution)/shard_map/pallas_call | solution.py:26
  188.0 5.1 %shard_map.117 = (bf16[128,4096]{1,0:T(8,128)(2,1)}, bf16[128,2]{1,0:T(8,128)(2,1)S(1)}) custom-call(s32[2]{0:T(128)S(1)} %pad_add_fusion.pos_ref, bf16[128,256]{1,0:T(8,128)(2,1)S(1)} %copy-done.23, s32[128,2]{1,0:T(8,128)S(1)} %copy-done.15, bf16[128,2]{1,0:T(8,128)(2,1)S(1)} %copy-done.21, bf16[64,4224]{1,0:T(8,128)(2,1)S(1)} %get-tuple-element.66.rest_0_.rest_4_, ...), custom_call_target="tpu_custom_call" | custom-call | flops 268435456 | bytes 5441536 | tf_op jit(solution)/shard_map/pallas_call | solution.py:26
  195.3 3.6 %shard_map.126 = (bf16[2,384,256]{2,1,0:T(8,128)(2,1)S(1)}, f32[2,384,256]{2,1,0:T(8,128)S(1)}, bf16[2,384,256]{2,1,0:T(8,128)(2,1)S(1)}, f32[2,384,256]{2,1,0:T(8,128)S(1)}) custom-call(s32[2]{0:T(128)S(1)} %pad_add_fusion.pos_ref, bf16[768,256]{1,0:T(8,128)(2,1)S(1)} %get-tuple-element.80.act_t_ref, bf16[768,1024]{1,0:T(8,128)(2,1)} %collective-permute-done.27.other_ref, ...), custom_call_target="tpu_custom_call" | custom-call | flops 402653184 | bytes 5373952 | tf_op jit(solution)/shard_map/pallas_call | solution.py:26
  201.3 4.5 %collective-permute-done.25 = bf16[2,384,256]{2,1,0:T(8,128)(2,1)S(1)} collective-permute-done((bf16[2,384,256]{2,1,0:T(8,128)(2,1)}, bf16[2,384,256]{2,1,0:T(8,128)(2,1)S(1)}, u32[]{:S(2)}, u32[]{:S(2)}) %collective-permute-start.25) | collective-permute-done | bytes 393248 | tf_op jit(solution)/shard_map/ppermute | solution.py:268
  207.5 10.6 %collective-permute-done.24 = bf16[1,384,256]{2,1,0:T(8,128)(2,1)S(1)} collective-permute-done((bf16[1,384,256]{2,1,0:T(8,128)(2,1)S(1)}, bf16[1,384,256]{2,1,0:T(8,128)(2,1)S(1)}, u32[]{:S(2)}, u32[]{:S(2)}) %collective-permute-start.24) | collective-permute-done | bytes 196640 | tf_op jit(solution)/shard_map/ppermute | solution.py:268
  218.6 5.9 %collective-permute-done.26 = bf16[1,384,256]{2,1,0:T(8,128)(2,1)S(1)} collective-permute-done((bf16[1,384,256]{2,1,0:T(8,128)(2,1)S(1)}, bf16[1,384,256]{2,1,0:T(8,128)(2,1)S(1)}, u32[]{:S(2)}, u32[]{:S(2)}) %collective-permute-start.26) | collective-permute-done | bytes 196640 | tf_op jit(solution)/shard_map/ppermute | solution.py:268
  226.4 4.5 %shard_map.122 = (bf16[2,256,768]{2,1,0:T(8,128)(2,1)S(1)}, f32[2,256,768]{2,1,0:T(8,128)S(1)}, bf16[2,256,768]{2,1,0:T(8,128)(2,1)S(1)}, f32[2,256,768]{2,1,0:T(8,128)S(1)}) custom-call(s32[2]{0:T(128)S(1)} %pad_add_fusion.pos_ref, bf16[4096,256]{1,0:T(8,128)(2,1)} %copy-done, bf16[256,768]{1,0:T(8,128)(2,1)S(1)} %get-tuple-element.64.du_ref.delta_ref, ...), custom_call_target="tpu_custom_call" | custom-call | flops 805306368 | bytes 10354688 | tf_op jit(solution)/shard_map/pallas_call | solution.py:26
  233.2 19.9 %collective-permute-done.31 = bf16[1,384,256]{2,1,0:T(8,128)(2,1)S(1)} collective-permute-done((bf16[1,384,256]{2,1,0:T(8,128)(2,1)S(1)}, bf16[1,384,256]{2,1,0:T(8,128)(2,1)S(1)}, u32[]{:S(2)}, u32[]{:S(2)}) %collective-permute-start.31) | collective-permute-done | bytes 196640 | tf_op jit(solution)/shard_map/ppermute | solution.py:268
  255.1 4.5 %shard_map.120 = (bf16[2,256,768]{2,1,0:T(8,128)(2,1)S(1)}, f32[2,256,768]{2,1,0:T(8,128)S(1)}, bf16[2,256,768]{2,1,0:T(8,128)(2,1)S(1)}, f32[2,256,768]{2,1,0:T(8,128)S(1)}) custom-call(s32[2]{0:T(128)S(1)} %pad_add_fusion.pos_ref, bf16[4096,256]{1,0:T(8,128)(2,1)} %copy-done, bf16[256,768]{1,0:T(8,128)(2,1)S(1)} %get-tuple-element.63.dh_ref.delta_ref, ...), custom_call_target="tpu_custom_call" | custom-call | flops 805306368 | bytes 10354688 | tf_op jit(solution)/shard_map/pallas_call | solution.py:26
  262.5 11.2 %collective-permute-done.20 = bf16[2,256,768]{2,1,0:T(8,128)(2,1)S(1)} collective-permute-done((bf16[2,256,768]{2,1,0:T(8,128)(2,1)S(1)}, bf16[2,256,768]{2,1,0:T(8,128)(2,1)S(1)}, u32[]{:S(2)}, u32[]{:S(2)}) %collective-permute-start.20) | collective-permute-done | bytes 786464 | tf_op jit(solution)/shard_map/ppermute | solution.py:268
  274.5 5.7 %collective-permute-done.13 = bf16[2,256,768]{2,1,0:T(8,128)(2,1)S(1)} collective-permute-done((bf16[2,256,768]{2,1,0:T(8,128)(2,1)S(1)}, bf16[2,256,768]{2,1,0:T(8,128)(2,1)S(1)}, u32[]{:S(2)}, u32[]{:S(2)}) %collective-permute-start.13) | collective-permute-done | bytes 786464 | tf_op jit(solution)/shard_map/ppermute | solution.py:268
  282.0 8.6 %collective-permute-done.15 = bf16[2,256,768]{2,1,0:T(8,128)(2,1)S(1)} collective-permute-done((bf16[2,256,768]{2,1,0:T(8,128)(2,1)S(1)}, bf16[2,256,768]{2,1,0:T(8,128)(2,1)S(1)}, u32[]{:S(2)}, u32[]{:S(2)}) %collective-permute-start.15) | collective-permute-done | bytes 786464 | tf_op jit(solution)/shard_map/ppermute | solution.py:268
  291.4 7.6 %collective-permute-done.19 = bf16[1,256,768]{2,1,0:T(8,128)(2,1)S(1)} collective-permute-done((bf16[1,256,768]{2,1,0:T(8,128)(2,1)S(1)}, bf16[1,256,768]{2,1,0:T(8,128)(2,1)S(1)}, u32[]{:S(2)}, u32[]{:S(2)}) %collective-permute-start.19) | collective-permute-done | bytes 393248 | tf_op jit(solution)/shard_map/ppermute | solution.py:268
  300.4 3.6 %collective-permute-done.14 = bf16[1,256,768]{2,1,0:T(8,128)(2,1)S(1)} collective-permute-done((bf16[1,256,768]{2,1,0:T(8,128)(2,1)S(1)}, bf16[1,256,768]{2,1,0:T(8,128)(2,1)S(1)}, u32[]{:S(2)}, u32[]{:S(2)}) %collective-permute-start.14) | collective-permute-done | bytes 393248 | tf_op jit(solution)/shard_map/ppermute | solution.py:268
  (128 shorter events, 47.3 us)
Async XLA Ops:
  7.6 26.5 %collective-permute-start = (bf16[64,4096]{1,0:T(8,128)(2,1)}, bf16[64,4096]{1,0:T(8,128)(2,1)S(1)}, u32[]{:S(2)}, u32[]{:S(2)}) collective-permute-start(bf16[64,4096]{1,0:T(8,128)(2,1)} %get-tuple-element.48), channel_id=1, source_target_pairs={{0,1},{1,0},{2,3},{3,2},{4,5},{5,4},{6,7},{7,6},{8,9},{9,8},{10,11... | collective-permute-start | bytes 1572872 | tf_op jit(solution)/shard_map/ppermute | solution.py:268
  10.7 38.5 %collective-permute-start.7 = (bf16[64,4096]{1,0:T(8,128)(2,1)}, bf16[64,4096]{1,0:T(8,128)(2,1)S(1)}, u32[]{:S(2)}, u32[]{:S(2)}) collective-permute-start(bf16[64,4096]{1,0:T(8,128)(2,1)} %get-tuple-element.58), channel_id=1, source_target_pairs={{0,2},{1,3},{2,0},{3,1},{4,6},{5,7},{6,4},{7,5},{8,10},{9,11},{10,... | collective-permute-start | bytes 1572872 | tf_op jit(solution)/shard_map/ppermute | solution.py:268
  13.2 35.9 %collective-permute-start.8 = (bf16[64,4096]{1,0:T(8,128)(2,1)}, bf16[64,4096]{1,0:T(8,128)(2,1)S(1)}, u32[]{:S(2)}, u32[]{:S(2)}) collective-permute-start(bf16[64,4096]{1,0:T(8,128)(2,1)} %get-tuple-element.59), channel_id=1, source_target_pairs={{0,3},{1,2},{2,1},{3,0},{4,7},{5,6},{6,5},{7,4},{8,11},{9,10},{10,... | collective-permute-start | bytes 1572872 | tf_op jit(solution)/shard_map/ppermute | solution.py:268
  16.7 40.5 %collective-permute-start.4 = (bf16[64,2048]{1,0:T(8,128)(2,1)S(1)}, bf16[64,2048]{1,0:T(8,128)(2,1)S(1)}, u32[]{:S(2)}, u32[]{:S(2)}) collective-permute-start(bf16[64,2048]{1,0:T(8,128)(2,1)S(1)} %get-tuple-element.54), channel_id=1, source_target_pairs={{0,1},{1,0},{2,3},{3,2},{4,5},{5,4},{6,7},{7,6},{8,9},{9,8},{10,11... | collective-permute-start | bytes 786440 | tf_op jit(solution)/shard_map/ppermute | solution.py:268
  17.7 59.5 %collective-permute-start.5 = (bf16[64,2048]{1,0:T(8,128)(2,1)S(1)}, bf16[64,2048]{1,0:T(8,128)(2,1)S(1)}, u32[]{:S(2)}, u32[]{:S(2)}) collective-permute-start(bf16[64,2048]{1,0:T(8,128)(2,1)S(1)} %get-tuple-element.55), channel_id=1, source_target_pairs={{0,2},{1,3},{2,0},{3,1},{4,6},{5,7},{6,4},{7,5},{8,10},{9,11},{10,... | collective-permute-start | bytes 786440 | tf_op jit(solution)/shard_map/ppermute | solution.py:268
  34.1 43.1 %collective-permute-start.6 = (bf16[64,2048]{1,0:T(8,128)(2,1)S(1)}, bf16[64,2048]{1,0:T(8,128)(2,1)S(1)}, u32[]{:S(2)}, u32[]{:S(2)}) collective-permute-start(bf16[64,2048]{1,0:T(8,128)(2,1)S(1)} %get-tuple-element.56), channel_id=1, source_target_pairs={{0,3},{1,2},{2,1},{3,0},{4,7},{5,6},{6,5},{7,4},{8,11},{9,10},{10,... | collective-permute-start | bytes 786440 | tf_op jit(solution)/shard_map/ppermute | solution.py:268
  79.1 68.8 %collective-permute-start.22 = (bf16[768,1024]{1,0:T(8,128)(2,1)S(1)}, bf16[768,1024]{1,0:T(8,128)(2,1)S(1)}, u32[]{:S(2)}, u32[]{:S(2)}) collective-permute-start(bf16[768,1024]{1,0:T(8,128)(2,1)S(1)} %shard_map.123), channel_id=1, source_target_pairs={{0,4},{4,0},{8,12},{12,8},{16,20},{20,16},{24,28},{28,24},{1,5},{5... | collective-permute-start | bytes 4718600 | tf_op jit(solution)/shard_map/ppermute | solution.py:268
  81.9 17.0 %collective-permute-start.1 = (bf16[64,2048]{1,0:T(8,128)(2,1)S(1)}, bf16[64,2048]{1,0:T(8,128)(2,1)S(1)}, u32[]{:S(2)}, u32[]{:S(2)}) collective-permute-start(bf16[64,2048]{1,0:T(8,128)(2,1)S(1)} %get-tuple-element.50), channel_id=1, source_target_pairs={{0,1},{1,0},{2,3},{3,2},{4,5},{5,4},{6,7},{7,6},{8,9},{9,8},{10,11... | collective-permute-start | bytes 786440 | tf_op jit(solution)/shard_map/ppermute | solution.py:268
  86.7 21.3 %collective-permute-start.2 = (bf16[64,2048]{1,0:T(8,128)(2,1)S(1)}, bf16[64,2048]{1,0:T(8,128)(2,1)S(1)}, u32[]{:S(2)}, u32[]{:S(2)}) collective-permute-start(bf16[64,2048]{1,0:T(8,128)(2,1)S(1)} %get-tuple-element.51), channel_id=1, source_target_pairs={{0,2},{1,3},{2,0},{3,1},{4,6},{5,7},{6,4},{7,5},{8,10},{9,11},{10,... | collective-permute-start | bytes 786440 | tf_op jit(solution)/shard_map/ppermute | solution.py:268
  87.8 20.2 %collective-permute-start.3 = (bf16[64,2048]{1,0:T(8,128)(2,1)S(1)}, bf16[64,2048]{1,0:T(8,128)(2,1)S(1)}, u32[]{:S(2)}, u32[]{:S(2)}) collective-permute-start(bf16[64,2048]{1,0:T(8,128)(2,1)S(1)} %get-tuple-element.52), channel_id=1, source_target_pairs={{0,3},{1,2},{2,1},{3,0},{4,7},{5,6},{6,5},{7,4},{8,11},{9,10},{10,... | collective-permute-start | bytes 786440 | tf_op jit(solution)/shard_map/ppermute | solution.py:268
  111.0 84.2 %collective-permute-start.27 = (bf16[768,1024]{1,0:T(8,128)(2,1)}, bf16[768,1024]{1,0:T(8,128)(2,1)}, u32[]{:S(2)}, u32[]{:S(2)}) collective-permute-start(bf16[768,1024]{1,0:T(8,128)(2,1)} %shard_map.125), channel_id=1, source_target_pairs={{0,4},{4,0},{8,12},{12,8},{16,20},{20,16},{24,28},{28,24},{1,5},{5... | collective-permute-start | bytes 4718600 | tf_op jit(solution)/shard_map/ppermute | solution.py:268
  130.0 96.3 %collective-permute-start.17 = (bf16[2048,768]{1,0:T(8,128)(2,1)}, bf16[2048,768]{1,0:T(8,128)(2,1)}, u32[]{:S(2)}, u32[]{:S(2)}) collective-permute-start(bf16[2048,768]{1,0:T(8,128)(2,1)} %shard_map.121), channel_id=1, source_target_pairs={{0,4},{4,0},{8,12},{12,8},{16,20},{20,16},{24,28},{28,24},{1,5},{5... | collective-permute-start | bytes 9437192 | tf_op jit(solution)/shard_map/ppermute | solution.py:268
  140.1 42.8 %collective-permute-start.10 = (bf16[64,4224]{1,0:T(8,128)(2,1)S(1)}, bf16[64,4224]{1,0:T(8,128)(2,1)S(1)}, u32[]{:S(2)}, u32[]{:S(2)}) collective-permute-start(bf16[64,4224]{1,0:T(8,128)(2,1)S(1)} %get-tuple-element.68), channel_id=1, source_target_pairs={{0,2},{1,3},{2,0},{3,1},{4,6},{5,7},{6,4},{7,5},{8,10},{9,11},{10,... | collective-permute-start | bytes 1622024 | tf_op jit(solution)/shard_map/ppermute | solution.py:268
  146.6 41.3 %collective-permute-start.11 = (bf16[64,4224]{1,0:T(8,128)(2,1)S(1)}, bf16[64,4224]{1,0:T(8,128)(2,1)S(1)}, u32[]{:S(2)}, u32[]{:S(2)}) collective-permute-start(bf16[64,4224]{1,0:T(8,128)(2,1)S(1)} %get-tuple-element.69), channel_id=1, source_target_pairs={{0,3},{1,2},{2,1},{3,0},{4,7},{5,6},{6,5},{7,4},{8,11},{9,10},{10,... | collective-permute-start | bytes 1622024 | tf_op jit(solution)/shard_map/ppermute | solution.py:268
  148.0 40.0 %collective-permute-start.9 = (bf16[64,4224]{1,0:T(8,128)(2,1)S(1)}, bf16[64,4224]{1,0:T(8,128)(2,1)S(1)}, u32[]{:S(2)}, u32[]{:S(2)}) collective-permute-start(bf16[64,4224]{1,0:T(8,128)(2,1)S(1)} %get-tuple-element.67), channel_id=1, source_target_pairs={{0,1},{1,0},{2,3},{3,2},{4,5},{5,4},{6,7},{7,6},{8,9},{9,8},{10,11... | collective-permute-start | bytes 1622024 | tf_op jit(solution)/shard_map/ppermute | solution.py:268
  182.9 16.6 %collective-permute-start.23 = (bf16[2,384,256]{2,1,0:T(8,128)(2,1)}, bf16[2,384,256]{2,1,0:T(8,128)(2,1)}, u32[]{:S(2)}, u32[]{:S(2)}) collective-permute-start(bf16[2,384,256]{2,1,0:T(8,128)(2,1)} %get-tuple-element.82), channel_id=1, source_target_pairs={{0,8},{4,12},{8,0},{12,4},{16,24},{20,28},{24,16},{28,20},{1,9},{5... | collective-permute-start | bytes 1179656 | tf_op jit(solution)/shard_map/ppermute | solution.py:268
  187.9 67.2 %collective-permute-start.12 = (bf16[2048,768]{1,0:T(8,128)(2,1)}, bf16[2048,768]{1,0:T(8,128)(2,1)}, u32[]{:S(2)}, u32[]{:S(2)}) collective-permute-start(bf16[2048,768]{1,0:T(8,128)(2,1)} %shard_map.119), channel_id=1, source_target_pairs={{0,4},{4,0},{8,12},{12,8},{16,20},{20,16},{24,28},{28,24},{1,5},{5... | collective-permute-start | bytes 9437192 | tf_op jit(solution)/shard_map/ppermute | solution.py:268
  193.7 12.1 %collective-permute-start.25 = (bf16[2,384,256]{2,1,0:T(8,128)(2,1)}, bf16[2,384,256]{2,1,0:T(8,128)(2,1)S(1)}, u32[]{:S(2)}, u32[]{:S(2)}) collective-permute-start(bf16[2,384,256]{2,1,0:T(8,128)(2,1)} %get-tuple-element.84), channel_id=1, source_target_pairs={{0,16},{4,20},{8,24},{12,28},{16,0},{20,4},{24,8},{28,12},{1,17},{... | collective-permute-start | bytes 1179656 | tf_op jit(solution)/shard_map/ppermute | solution.py:268
  198.9 25.7 %collective-permute-start.28 = (bf16[2,384,256]{2,1,0:T(8,128)(2,1)S(1)}, bf16[2,384,256]{2,1,0:T(8,128)(2,1)S(1)}, u32[]{:S(2)}, u32[]{:S(2)}) collective-permute-start(bf16[2,384,256]{2,1,0:T(8,128)(2,1)S(1)} %get-tuple-element.86), channel_id=1, source_target_pairs={{0,8},{4,12},{8,0},{12,4},{16,24},{20,28},{24,16},{28,20},{1,9},{5... | collective-permute-start | bytes 1179656 | tf_op jit(solution)/shard_map/ppermute | solution.py:268
  199.5 32.0 %collective-permute-start.30 = (bf16[2,384,256]{2,1,0:T(8,128)(2,1)S(1)}, bf16[2,384,256]{2,1,0:T(8,128)(2,1)S(1)}, u32[]{:S(2)}, u32[]{:S(2)}) collective-permute-start(bf16[2,384,256]{2,1,0:T(8,128)(2,1)S(1)} %get-tuple-element.88), channel_id=1, source_target_pairs={{0,16},{4,20},{8,24},{12,28},{16,0},{20,4},{24,8},{28,12},{1,17},{... | collective-permute-start | bytes 1179656 | tf_op jit(solution)/shard_map/ppermute | solution.py:268
  205.8 12.2 %collective-permute-start.24 = (bf16[1,384,256]{2,1,0:T(8,128)(2,1)S(1)}, bf16[1,384,256]{2,1,0:T(8,128)(2,1)S(1)}, u32[]{:S(2)}, u32[]{:S(2)}) collective-permute-start(bf16[1,384,256]{2,1,0:T(8,128)(2,1)S(1)} %fusion.14), channel_id=1, source_target_pairs={{0,16},{4,20},{8,24},{12,28},{16,0},{20,4},{24,8},{28,12},{1,17},{... | collective-permute-start | bytes 589832 | tf_op jit(solution)/shard_map/ppermute | solution.py:268
  218.1 6.5 %collective-permute-start.26 = (bf16[1,384,256]{2,1,0:T(8,128)(2,1)S(1)}, bf16[1,384,256]{2,1,0:T(8,128)(2,1)S(1)}, u32[]{:S(2)}, u32[]{:S(2)}) collective-permute-start(bf16[1,384,256]{2,1,0:T(8,128)(2,1)S(1)} %slice.139), channel_id=1, source_target_pairs={{0,8},{4,12},{8,0},{12,4},{16,24},{20,28},{24,16},{28,20},{1,9},{5... | collective-permute-start | bytes 589832 | tf_op jit(solution)/shard_map/ppermute | solution.py:268
  224.7 8.4 %collective-permute-start.29 = (bf16[1,384,256]{2,1,0:T(8,128)(2,1)S(1)}, bf16[1,384,256]{2,1,0:T(8,128)(2,1)S(1)}, u32[]{:S(2)}, u32[]{:S(2)}) collective-permute-start(bf16[1,384,256]{2,1,0:T(8,128)(2,1)S(1)} %fusion.15), channel_id=1, source_target_pairs={{0,16},{4,20},{8,24},{12,28},{16,0},{20,4},{24,8},{28,12},{1,17},{... | collective-permute-start | bytes 589832 | tf_op jit(solution)/shard_map/ppermute | solution.py:268
  230.9 30.9 %collective-permute-start.18 = (bf16[2,256,768]{2,1,0:T(8,128)(2,1)S(1)}, bf16[2,256,768]{2,1,0:T(8,128)(2,1)S(1)}, u32[]{:S(2)}, u32[]{:S(2)}) collective-permute-start(bf16[2,256,768]{2,1,0:T(8,128)(2,1)S(1)} %get-tuple-element.77), channel_id=1, source_target_pairs={{0,8},{4,12},{8,0},{12,4},{16,24},{20,28},{24,16},{28,20},{1,9},{5... | collective-permute-start | bytes 2359304 | tf_op jit(solution)/shard_map/ppermute | solution.py:268
  231.6 21.5 %collective-permute-start.31 = (bf16[1,384,256]{2,1,0:T(8,128)(2,1)S(1)}, bf16[1,384,256]{2,1,0:T(8,128)(2,1)S(1)}, u32[]{:S(2)}, u32[]{:S(2)}) collective-permute-start(bf16[1,384,256]{2,1,0:T(8,128)(2,1)S(1)} %slice.138), channel_id=1, source_target_pairs={{0,8},{4,12},{8,0},{12,4},{16,24},{20,28},{24,16},{28,20},{1,9},{5... | collective-permute-start | bytes 589832 | tf_op jit(solution)/shard_map/ppermute | solution.py:268
  253.2 20.5 %collective-permute-start.20 = (bf16[2,256,768]{2,1,0:T(8,128)(2,1)S(1)}, bf16[2,256,768]{2,1,0:T(8,128)(2,1)S(1)}, u32[]{:S(2)}, u32[]{:S(2)}) collective-permute-start(bf16[2,256,768]{2,1,0:T(8,128)(2,1)S(1)} %get-tuple-element.79), channel_id=1, source_target_pairs={{0,16},{4,20},{8,24},{12,28},{16,0},{20,4},{24,8},{28,12},{1,17},{... | collective-permute-start | bytes 2359304 | tf_op jit(solution)/shard_map/ppermute | solution.py:268
  259.6 20.5 %collective-permute-start.13 = (bf16[2,256,768]{2,1,0:T(8,128)(2,1)S(1)}, bf16[2,256,768]{2,1,0:T(8,128)(2,1)S(1)}, u32[]{:S(2)}, u32[]{:S(2)}) collective-permute-start(bf16[2,256,768]{2,1,0:T(8,128)(2,1)S(1)} %get-tuple-element.73), channel_id=1, source_target_pairs={{0,8},{4,12},{8,0},{12,4},{16,24},{20,28},{24,16},{28,20},{1,9},{5... | collective-permute-start | bytes 2359304 | tf_op jit(solution)/shard_map/ppermute | solution.py:268
  260.2 30.3 %collective-permute-start.15 = (bf16[2,256,768]{2,1,0:T(8,128)(2,1)S(1)}, bf16[2,256,768]{2,1,0:T(8,128)(2,1)S(1)}, u32[]{:S(2)}, u32[]{:S(2)}) collective-permute-start(bf16[2,256,768]{2,1,0:T(8,128)(2,1)S(1)} %get-tuple-element.75), channel_id=1, source_target_pairs={{0,16},{4,20},{8,24},{12,28},{16,0},{20,4},{24,8},{28,12},{1,17},{... | collective-permute-start | bytes 2359304 | tf_op jit(solution)/shard_map/ppermute | solution.py:268
  262.0 37.0 %collective-permute-start.19 = (bf16[1,256,768]{2,1,0:T(8,128)(2,1)S(1)}, bf16[1,256,768]{2,1,0:T(8,128)(2,1)S(1)}, u32[]{:S(2)}, u32[]{:S(2)}) collective-permute-start(bf16[1,256,768]{2,1,0:T(8,128)(2,1)S(1)} %fusion.7), channel_id=1, source_target_pairs={{0,16},{4,20},{8,24},{12,28},{16,0},{20,4},{24,8},{28,12},{1,17},{... | collective-permute-start | bytes 1179656 | tf_op jit(solution)/shard_map/ppermute | solution.py:268
  273.9 25.1 %collective-permute-start.21 = (bf16[1,256,768]{2,1,0:T(8,128)(2,1)S(1)}, bf16[1,256,768]{2,1,0:T(8,128)(2,1)S(1)}, u32[]{:S(2)}, u32[]{:S(2)}) collective-permute-start(bf16[1,256,768]{2,1,0:T(8,128)(2,1)S(1)} %slice.136), channel_id=1, source_target_pairs={{0,8},{4,12},{8,0},{12,4},{16,24},{20,28},{24,16},{28,20},{1,9},{5... | collective-permute-start | bytes 1179656 | tf_op jit(solution)/shard_map/ppermute | solution.py:268
  280.4 23.6 %collective-permute-start.14 = (bf16[1,256,768]{2,1,0:T(8,128)(2,1)S(1)}, bf16[1,256,768]{2,1,0:T(8,128)(2,1)S(1)}, u32[]{:S(2)}, u32[]{:S(2)}) collective-permute-start(bf16[1,256,768]{2,1,0:T(8,128)(2,1)S(1)} %fusion.6), channel_id=1, source_target_pairs={{0,16},{4,20},{8,24},{12,28},{16,0},{20,4},{24,8},{28,12},{1,17},{... | collective-permute-start | bytes 1179656 | tf_op jit(solution)/shard_map/ppermute | solution.py:268
  290.8 13.3 %collective-permute-start.16 = (bf16[1,256,768]{2,1,0:T(8,128)(2,1)S(1)}, bf16[1,256,768]{2,1,0:T(8,128)(2,1)S(1)}, u32[]{:S(2)}, u32[]{:S(2)}) collective-permute-start(bf16[1,256,768]{2,1,0:T(8,128)(2,1)S(1)} %slice.137), channel_id=1, source_target_pairs={{0,8},{4,12},{8,0},{12,4},{16,24},{20,28},{24,16},{28,20},{1,9},{5... | collective-permute-start | bytes 1179656 | tf_op jit(solution)/shard_map/ppermute | solution.py:268
  (24 other events, 444.0 us)

commit v2 on v0

v2 whole, which is shorter than its diff:
```python
import functools
import math

import jax
import jax.numpy as jnp
from jax import lax
from jax.experimental import pallas as pl
from jax.experimental.pallas import tpu as pltpu
from jax.sharding import PartitionSpec as P

CAP = 64
EXTRA = 128
F32 = jnp.float32
BF16 = jnp.bfloat16
LONG = 10**12
VMEM_SPARE = 6 * 1024 * 1024


def whole(shape):
    return pl.BlockSpec(shape, lambda i, pos: (0,) * len(shape))


def call(kernel, grid, in_specs, out_specs, out_shape, pos, args, after, scratch=(), cost=1):
    held = sum(math.prod(ref.shape) * ref.dtype.itemsize for ref in scratch)
    for spec, array in zip([*in_specs, *out_specs], [*args, *out_shape]):
        if spec.block_shape is not None:
            held += 2 * math.prod(spec.block_shape) * array.dtype.itemsize
    first, count = 1 + len(args), len(after)

    def ordered(*refs):
        kernel(*refs[:first], *refs[first + count :])

    return pl.pallas_call(
        ordered,
        grid_spec=pltpu.PrefetchScalarGridSpec(
            num_scalar_prefetch=1,
            grid=grid,
            in_specs=list(in_specs) + [pl.BlockSpec(memory_space=pl.ANY)] * count,
            out_specs=out_specs,
            scratch_shapes=list(scratch),
        ),
        out_shape=out_shape,
        compiler_params=pltpu.CompilerParams(vmem_limit_bytes=held + VMEM_SPARE),
        cost_estimate=pl.CostEstimate(flops=cost, bytes_accessed=1, transcendentals=0),
    )(pos, *args, *after)


def shape_of(shape, dtype=BF16):
    return jax.ShapeDtypeStruct(shape, dtype)


def dot(left, right):
    return jnp.dot(left, right, preferred_element_type=F32)


def shard_at(i, me, replicas):
    half = replicas // 2
    return jnp.where(i < half, 2 * i + 1, 2 * i - replicas) ^ me


def slot_expert(rows, cols, my_expert):
    return (lax.broadcasted_iota(jnp.int32, (rows, cols), 1) // CAP) ^ my_expert


def slot_matrix(routes_ref, my_expert, slots):
    tok = routes_ref.shape[0]
    expert = slot_expert(tok, slots, my_expert)
    hit = jnp.zeros((tok, slots), jnp.bool_)
    for k in range(routes_ref.shape[1]):
        hit = hit | (routes_ref[:, k : k + 1] == expert)
    named = jnp.where(hit, 1.0, 0.0)
    before = lax.broadcasted_iota(jnp.int32, (tok, tok), 1) < lax.broadcasted_iota(
        jnp.int32, (tok, tok), 0
    )
    rank = dot(jnp.where(before, 1.0, 0.0).astype(BF16), named.astype(BF16))
    place = (lax.broadcasted_iota(jnp.int32, (tok, slots), 1) % CAP).astype(F32)
    return jnp.where(rank == place, named, 0.0), expert


def send_tokens_kernel(experts, replicas, pos_ref, routes_ref, tok_ref, *rest):
    outs, place_ref = rest[:experts], rest[experts]
    place, _ = slot_matrix(routes_ref, pos_ref[1], experts * CAP)
    place_ref[...] = place.astype(BF16)
    place_t = place.T.astype(BF16)
    width = tok_ref.shape[1] // replicas
    for i in range(replicas):
        at = pl.ds(pl.multiple_of(shard_at(i, pos_ref[0], replicas) * width, width), width)
        rows = dot(place_t, tok_ref[:, at]).astype(BF16)
        for j in range(experts):
            outs[j][:, i * width : (i + 1) * width] = rows[j * CAP : (j + 1) * CAP]


def send_cot_kernel(experts, replicas, pos_ref, routes_ref, probs_ref, cot_ref, *outs):
    place, expert = slot_matrix(routes_ref, pos_ref[1], experts * CAP)
    probs = probs_ref[...].astype(F32)
    weight = jnp.zeros_like(place)
    for k in range(routes_ref.shape[1]):
        weight += jnp.where(routes_ref[:, k : k + 1] == expert, probs[:, k : k + 1], 0.0)
    weighted = (place * weight).T.astype(BF16)
    width = cot_ref.shape[1] // replicas
    for i in range(replicas):
        at = pl.ds(pl.multiple_of(shard_at(i, pos_ref[0], replicas) * width, width), width)
        rows = dot(weighted, cot_ref[:, at]).astype(BF16)
        for j in range(experts):
            outs[j][:, i * width : (i + 1) * width] = rows[j * CAP : (j + 1) * CAP]


def forward_kernel(experts, replicas, pos_ref, *rest):
    xs, (wg_ref, wu_ref), outs, x_ref = (
        rest[:experts],
        rest[experts : experts + 2],
        rest[experts + 2 : -1],
        rest[-1],
    )
    act_ref, act_t_ref, for_gate_ref, for_up_ref = outs

    @pl.when(pl.program_id(0) == 0)
    def _():
        for j in range(experts):
            x_ref[j * CAP : (j + 1) * CAP, :] = xs[j][...]

    width = wg_ref.shape[1] // replicas
    gate = jnp.zeros(act_ref.shape, F32)
    up = jnp.zeros(act_ref.shape, F32)
    for i in range(replicas):
        at = pl.ds(pl.multiple_of(shard_at(i, pos_ref[0], replicas) * width, width), width)
        part = x_ref[:, i * width : (i + 1) * width]
        gate += dot(part, wg_ref[0, at, :])
        up += dot(part, wu_ref[0, at, :])
    gate, up = gate.T, up.T
    sig = jax.nn.sigmoid(gate)
    silu = gate * sig
    act = (silu * up).astype(BF16)
    act_ref[...] = act.T
    act_t_ref[...] = act
    for_gate_ref[...] = up * sig * (1.0 + gate * (1.0 - sig))
    for_up_ref[...] = silu


def joined(refs):
    return jnp.concatenate([ref[...] for ref in refs], axis=0)


def transpose_kernel(pos_ref, *rest):
    rest[-1][...] = joined(rest[:-1]).T


def scatter_pieces(part, q, outs):
    low_send, low_keep, high_send, high_keep = outs
    pieces = pl.num_programs(0)
    half = part.shape[0] // 2

    @pl.when(q % 2 == 1)
    def _():
        low_send[0] = part[:half].astype(BF16)

    @pl.when(q % 2 == 0)
    def _():
        low_keep[0] = part[:half]

    @pl.when(q >= pieces // 2)
    def _():
        high_send[0] = part[half:].astype(BF16)

    @pl.when(q < pieces // 2)
    def _():
        high_keep[0] = part[half:]


def scatter_specs(pieces, rows, cols):
    block = (1, rows // 2, cols)
    half = pieces // 2
    specs = [
        pl.BlockSpec(block, lambda q, pos: (q // 2, 0, 0)),
        pl.BlockSpec(block, lambda q, pos: (q // 2, 0, 0)),
        pl.BlockSpec(block, lambda q, pos: (jnp.maximum(q - half, 0), 0, 0)),
        pl.BlockSpec(block, lambda q, pos: (jnp.minimum(q, half - 1), 0, 0)),
    ]
    shapes = [shape_of((half, rows // 2, cols), t) for t in (BF16, F32, BF16, F32)]
    return specs, shapes


def back_hidden_kernel(
    pos_ref,
    wd_ref,
    dyt_ref,
    act_ref,
    for_gate_ref,
    for_up_ref,
    delta_ref,
    delta_t_ref,
    prob_ref,
    sum_ref,
):
    i = pl.program_id(0)
    term = dot(wd_ref[0], dyt_ref[...])

    @pl.when(i == 0)
    def _():
        sum_ref[...] = term

    @pl.when(i > 0)
    def _():
        sum_ref[...] += term

    @pl.when(i == pl.num_programs(0) - 1)
    def _():
        back = sum_ref[...]
        dh = (back * for_gate_ref[...]).astype(BF16)
        du = (back * for_up_ref[...]).astype(BF16)
        hidden = back.shape[0]
        delta_t_ref[:hidden] = dh
        delta_t_ref[hidden:] = du
        delta_ref[:, :hidden] = dh.T
        delta_ref[:, hidden:] = du.T
        prob_ref[...] = jnp.sum(act_ref[...].astype(F32) * back, axis=0, keepdims=True)


def grad_far_kernel(scale, pos_ref, xt_ref, delta_ref, out_ref):
    out_ref[...] = (dot(xt_ref[...], delta_ref[...]) * scale).astype(BF16)


def grad_near_kernel(scale, pos_ref, xt_ref, delta_ref, *rest):
    others, outs = rest[:-4], rest[-4:]
    other = jnp.concatenate([ref[...] for ref in others], axis=1)
    part = dot(xt_ref[...], delta_ref[...]) * scale + other.astype(F32)
    scatter_pieces(part, pl.program_id(0), outs)


def row_grad_kernel(pos_ref, delta_t_ref, prob_ref, wg_ref, wu_ref, *outs):
    i = pl.program_id(0)
    width, hidden = wg_ref.shape[1:]
    rows_t = dot(wg_ref[0], delta_t_ref[:hidden]) + dot(wu_ref[0], delta_t_ref[hidden:])
    rows = rows_t.astype(BF16).T
    at = pl.ds(pl.multiple_of(i * width, width), width)
    for j, out_ref in enumerate(outs):
        out_ref[:, at] = rows[j * CAP : (j + 1) * CAP]

    @pl.when(i == 0)
    def _():
        full = prob_ref[...]
        high = full.astype(BF16).astype(F32)
        lane = lax.broadcasted_iota(jnp.int32, (EXTRA, full.shape[1]), 0)
        both = jnp.where(lane == 0, high, jnp.where(lane == 1, full - high, 0.0)).T.astype(BF16)
        for j, out_ref in enumerate(outs):
            out_ref[:, out_ref.shape[1] - EXTRA :] = both[j * CAP : (j + 1) * CAP]


def add_kernel(pos_ref, *rest):
    ins, outs = rest[:-4], rest[-4:]

    def total(first):
        pairs = [(ins[k], ins[k + 1]) for k in range(first, len(ins), 4)]
        return jnp.concatenate([keep[0] + came[0].astype(F32) for keep, came in pairs], axis=1)

    part = jnp.concatenate([total(0), total(2)], axis=0)
    scatter_pieces(part, pl.program_id(0), outs)


def mark_kernel(pos_ref, out_ref):
    out_ref[...] = jnp.zeros(out_ref.shape, F32)


def combine_kernel(scale, pos_ref, place_ref, routes_ref, probs_ref, *rest):
    experts = (len(rest) - 2) // 2
    x_ref, prob_ref = rest[2 * experts :]
    rows = joined(rest[:experts])
    x_ref[...] = dot(place_ref[...], rows).astype(BF16)

    @pl.when(pl.program_id(0) == 0)
    def _():
        place = place_ref[...].astype(F32)
        extra = joined(rest[experts : 2 * experts])
        expert = slot_expert(place.shape[0], place.shape[1], pos_ref[1])
        probs = probs_ref[...].astype(F32)
        lane = lax.broadcasted_iota(jnp.int32, probs.shape, 1)
        result = jnp.zeros(probs.shape, F32)
        for k in range(routes_ref.shape[1]):
            mine = jnp.where(routes_ref[:, k : k + 1] == expert, place, 0.0).astype(BF16)
            found = jnp.sum(dot(mine, extra), axis=1, keepdims=True)
            result += jnp.where(lane == k, found, 0.0)
        prob_ref[...] = (result * scale / probs).astype(BF16)


def finish_kernel(
    pos_ref, low_keep_ref, low_ref, high_keep_ref, high_ref, down_ref, gate_ref, up_ref
):
    cols = gate_ref.shape[1]

    def total(keep_ref, ref, at):
        part = slice(at * cols, (at + 1) * cols)
        return keep_ref[0, :, part] + ref[0, :, part].astype(F32)

    halves = ((low_keep_ref, low_ref), (high_keep_ref, high_ref))
    down_ref[...] = jnp.concatenate([total(*half, 0).T for half in halves], axis=1)
    for at, out_ref in ((1, gate_ref), (2, up_ref)):
        out_ref[...] = jnp.concatenate([total(*half, at) for half in halves], axis=0)


def flip(x, axis, bit):
    count = lax.axis_size(axis)
    return lax.ppermute(x, axis, [(i, i ^ bit) for i in range(count)])


def body(tokens, out_grad, routes, gate_probs, w_gate, w_up, w_down):
    tok, width = tokens.shape
    experts = lax.axis_size("expert")
    replicas = lax.axis_size("dp")
    hidden = w_gate.shape[2]
    slots = experts * CAP
    shard = width // replicas
    pieces = replicas // 2
    levels = pieces.bit_length() - 1
    grad_scale = 1.0 / math.sqrt(tok * replicas * experts)
    prob_scale = 1.0 / math.sqrt(width)
    pos = jnp.stack([lax.axis_index("dp"), lax.axis_index("expert")]).astype(jnp.int32)
    chain = []

    def run(kernel, grid, in_specs, out_specs, out_shape, args, after=(), **kw):
        out = call(
            kernel, grid, in_specs, out_specs, out_shape, pos, args, [*chain[-1:], *after], **kw
        )
        chain.append(out[0])
        return out

    def exchange(blocks):
        return [blocks[0]] + [flip(blocks[j], "expert", j) for j in range(experts - 1, 0, -1)][::-1]

    def block_specs(cols, at):
        return [pl.BlockSpec((CAP, cols), at) for _ in range(experts)]

    def cross(state, level):
        low_send, low_keep, high_send, high_keep = state
        return (
            low_keep,
            flip(low_send, "dp", 2 << level),
            high_keep,
            flip(high_send, "dp", 2 << (levels - 1 - level)),
        )

    def add(*states):
        count, rows = states[0][0].shape[:2]
        specs, shapes = scatter_specs(count, 2 * rows, sum(s[0].shape[2] for s in states))
        ins = [a for state in states for a in state]
        blocks = [pl.BlockSpec((1, *a.shape[1:]), lambda q, pos: (q, 0, 0)) for a in ins]
        return run(add_kernel, (count,), blocks, specs, shapes, ins)

    def mark(after, cost):
        run(mark_kernel, (1,), [], [whole((8, 128))], [shape_of((8, 128), F32)], [], after, cost=cost)

    blocks = [whole((CAP, width)) for _ in range(experts)]
    *x_out, place = run(
        functools.partial(send_tokens_kernel, experts, replicas),
        (1,),
        [whole(routes.shape), whole(tokens.shape)],
        [*blocks, whole((tok, slots))],
        [shape_of((CAP, width)) for _ in range(experts)] + [shape_of((tok, slots))],
        [routes, tokens],
    )
    x_in = exchange(x_out)

    dy_out = run(
        functools.partial(send_cot_kernel, experts, replicas),
        (1,),
        [whole(routes.shape), whole(gate_probs.shape), whole(out_grad.shape)],
        blocks,
        [shape_of((CAP, width)) for _ in range(experts)],
        [routes, gate_probs, out_grad],
        [x_in[1]],
    )
    dy = exchange(dy_out)

    def grad_far(rows_t, right, which):
        (far,) = run(
            functools.partial(grad_far_kernel, grad_scale),
            (pieces,),
            [
                pl.BlockSpec((shard, slots), lambda i, pos: (i, 0)),
                pl.BlockSpec((slots, hidden), lambda i, pos: (0, which)),
            ],
            [pl.BlockSpec((shard, hidden), lambda i, pos: (i, 0))],
            [shape_of((pieces * shard, hidden))],
            [rows_t, right],
        )
        return flip(far, "dp", 1)

    def grad_near(rows_t, right, others):
        specs, shapes = scatter_specs(pieces, shard, right.shape[1])
        return run(
            functools.partial(grad_near_kernel, grad_scale),
            (pieces,),
            [
                pl.BlockSpec((shard, slots), lambda i, pos: (i + pieces, 0)),
                whole(right.shape),
            ]
            + [pl.BlockSpec((shard, hidden), lambda i, pos: (i, 0))] * len(others),
            specs,
            shapes,
            [rows_t, right, *others],
        )

    def transpose(rows):
        (out,) = run(
            transpose_kernel,
            (replicas,),
            block_specs(shard, lambda i, pos: (0, i)),
            [pl.BlockSpec((shard, slots), lambda i, pos: (i, 0))],
            [shape_of((width, slots))],
            rows,
        )
        return out

    hid = hidden // 3
    act, act_t, for_gate, for_up = run(
        functools.partial(forward_kernel, experts, replicas),
        (3,),
        [whole((CAP, width)) for _ in range(experts)]
        + [pl.BlockSpec((1, width, hid), lambda i, pos: (0, 0, i)) for _ in range(2)],
        [pl.BlockSpec((slots, hid), lambda i, pos: (0, i))]
        + [pl.BlockSpec((hid, slots), lambda i, pos: (i, 0))] * 3,
        [shape_of((slots, hidden))] + [shape_of((hidden, slots), t) for t in (BF16, F32, F32)],
        [*x_in, w_gate, w_up],
        scratch=[pltpu.VMEM((slots, width), BF16)],
    )
    x_t = transpose(x_in)
    dy_t = transpose(dy)

    other = grad_far(dy_t, act, 0)
    delta, delta_t, prob = run(
        back_hidden_kernel,
        (replicas,),
        [
            pl.BlockSpec(
                (1, hidden, shard), lambda i, pos: (0, 0, shard_at(i, pos[0], replicas))
            ),
            pl.BlockSpec((shard, slots), lambda i, pos: (i, 0)),
        ]
        + [whole((hidden, slots))] * 3,
        [whole((slots, 2 * hidden)), whole((2 * hidden, slots)), whole((1, slots))],
        [
            shape_of((slots, 2 * hidden)),
            shape_of((2 * hidden, slots)),
            shape_of((1, slots), F32),
        ],
        [w_down, dy_t, act_t, for_gate, for_up],
        scratch=[pltpu.VMEM((hidden, slots), F32)],
    )
    down = cross(grad_near(dy_t, act, [other]), 0)
    others = [grad_far(x_t, delta, 0), grad_far(x_t, delta, 1)]

    back_out = run(
        row_grad_kernel,
        (8,),
        [whole((2 * hidden, slots)), whole((1, slots))]
        + [pl.BlockSpec((1, width // 8, hidden), lambda i, pos: (0, i, 0)) for _ in range(2)],
        [whole((CAP, width + EXTRA)) for _ in range(experts)],
        [shape_of((CAP, width + EXTRA)) for _ in range(experts)],
        [delta_t, prob, w_gate, w_up],
    )
    back_in = exchange(back_out)

    both = cross(grad_near(x_t, delta, others), 0)
    mark([down[1], down[3]], 1)
    mark([], LONG)
    state = add(down, both)
    for level in range(1, levels):
        state = cross(state, level)
        if level + 1 < levels:
            state = add(state)

    step = width // 4
    x_grad, prob_grad = run(
        functools.partial(combine_kernel, prob_scale),
        (4,),
        [whole((tok, slots)), whole(routes.shape), whole(gate_probs.shape)]
        + block_specs(step, lambda i, pos: (0, i))
        + block_specs(EXTRA, lambda i, pos: (0, width // EXTRA)),
        [pl.BlockSpec((tok, step), lambda i, pos: (0, i)), whole(gate_probs.shape)],
        [shape_of((tok, width)), shape_of(gate_probs.shape)],
        [place, routes, gate_probs, *back_in, *back_in],
        cost=LONG,
    )
    down_grad, gate_grad, up_grad = run(
        finish_kernel,
        (1,),
        [whole(state[0].shape)] * 4,
        [whole((hidden, shard)), whole((shard, hidden)), whole((shard, hidden))],
        [shape_of((hidden, shard), F32)] + [shape_of((shard, hidden), F32)] * 2,
        state,
    )
    return (x_grad, prob_grad, gate_grad[None], up_grad[None], down_grad[None])


def solution(mesh):
    return jax.shard_map(
        body,
        mesh=mesh,
        in_specs=(
            P(("dp", "expert"), None),
            P(("dp", "expert"), None),
            P(("dp", "expert"), None),
            P(("dp", "expert"), None),
            P("expert", None, None),
            P("expert", None, None),
            P("expert", None, None),
        ),
        out_specs=(
            P(("dp", "expert"), None),
            P(("dp", "expert"), None),
            P("expert", "dp", None),
            P("expert", "dp", None),
            P("expert", None, "dp"),
        ),
        check_vma=False,
    )
```

time: 328 us -> 217 us (0.66)
  Pallas kernels: 0 us -> 55.3 us
  blocking collectives: 52.8 us -> 0 us
  matrix products: 48.2 us -> 0 us
  other arithmetic: 35.8 us -> 0.08 us
  waiting for transfers between devices: 127 us -> 112 us
  between operations: 14.2 us -> 0.91 us
  local copies, waits for them, and re-layouts: 29.7 us -> 16.5 us
  starting transfers between devices: 19.3 us -> 29.7 us
    ppermute x0 -> x18, waiting for transfers between devices: none -> 112 us  [flip(): return lax.ppermute(x, axis, [(i, i ^ bit) for i in range(count)])]
    all_to_all x4 -> x0, waiting for transfers between devices: 85.9 us -> none  [the longest x1 44.4 us: body(): lax.all_to_all(row_grad.reshape(experts, CAP, width), 'expert', split_axi...]
    pallas_call x0 -> x17, Pallas kernels: none -> 55.3 us  [call(): pl.pallas_call(ordered, grid_spec=pltpu.PrefetchScalarGridSpec(num_scalar...]
    all_to_all x1 -> x0, blocking collectives: 52.8 us -> none  [body(): lax.all_to_all(tok_send, 'expert', split_axis=0, concat_axis=0, tiled=True)]
    dot_general x8 -> x0, matrix products: 48.2 us -> none  [the longest x2 18.1 us: contract_rows(): lax.dot_general(left, right, (((0,), (0,)), ((), ())), preferred_element_...]
    reduce_scatter x1 -> x0, waiting for transfers between devices: 41 us -> none  [body(): lax.psum_scatter((jnp.concatenate([paired, downward], axis=1) * grad_scal...]
    ppermute x0 -> x18, starting transfers between devices: none -> 29.7 us  [flip(): return lax.ppermute(x, axis, [(i, i ^ bit) for i in range(count)])]
    convert_element_type x5 -> x0, other arithmetic: 21.8 us -> none  [the longest x1 19.5 us: body(): (jnp.concatenate([paired, downward], axis=1) * grad_scale).astype(jnp.bfl...]
  transfers between devices with their start and end apart: 5 -> 18, of which waited for: 3 -> 8; matrix products, arithmetic and copies ran while one was open for 15% -> 1% of each run, Pallas kernels for 0% -> 18%
where the time goes in v2:
time: 217 us; the launch traced here: 215 us
  waiting for transfers between devices  112 us (52%)
  Pallas kernels  55.3 us (25%)
  starting transfers between devices  29.7 us (14%)
  local copies, waits for them, and re-layouts  16.5 us (8%)
    ppermute x18, waiting for transfers between devices, flip(): return lax.ppermute(x, axis, [(i, i ^ bit) for i in range(count)])  112 us
    pallas_call x17, Pallas kernels, call(): pl.pallas_call(ordered, grid_spec=pltpu.PrefetchScalarGridSpec(num_scalar...  55.3 us
    ppermute x18, starting transfers between devices, flip(): return lax.ppermute(x, axis, [(i, i ^ bit) for i in range(count)])  29.7 us
    unnamed x49, local copies, waits for them, and re-layouts  16.5 us
  transfers between devices with their start and end apart: 18, of which 8 were waited for; matrix products, arithmetic and copies ran while one was open for 1% of the time, Pallas kernels for 18%

profile of v2, /device:TPU:0, one launch (start us, length us, event | category | flops | bytes accessed | tf_op | source)
XLA Modules:
  0.0 214.8 jit_solution(15766084119787643138)
XLA Ops:
  1.5 1.2 copy-done.11
  2.7 2.3 %shard_map.110 = (bf16[64,4096]{1,0:T(8,128)(2,1)S(1)}, bf16[64,4096]{1,0:T(8,128)(2,1)}, bf16[64,4096]{1,0:T(8,128)(2,1)S(1)}, bf16[64,4096]{1,0:T(8,128)(2,1)S(1)}, bf16[128,256]{1,0:T(8,128)(2,1)S(1)}) custom-call(s32[2]{0:T(128)S(1)} %pad_add_fusion.refs_0_, s32[128,2]{1,0:T(8,128)S(1)} %copy.12.refs_1_.refs_2_, bf16[128,4096]{1,0:T(8,128)(2,1)S(1)} %copy-done.11), custom_call_target="tpu_custom_call" | custom-call | flops 1 | bytes 1 | tf_op jit(solution)/shard_map/pallas_call | solution.py:33
  5.0 3.0 %collective-permute-start = (bf16[64,4096]{1,0:T(8,128)(2,1)}, bf16[64,4096]{1,0:T(8,128)(2,1)S(1)}, u32[]{:S(2)}, u32[]{:S(2)}) collective-permute-start(bf16[64,4096]{1,0:T(8,128)(2,1)} %get-tuple-element.44), channel_id=1, source_target_pairs={{0,1},{1,0},{2,3},{3,2},{4,5},{5,4},{6,7},{7,6},{8,9},{9,8},{10,11... | collective-permute-start | bytes 1572872 | tf_op jit(solution)/shard_map/ppermute | solution.py:302
  8.0 2.6 %collective-permute-start.4 = (bf16[64,4096]{1,0:T(8,128)(2,1)S(1)}, bf16[64,4096]{1,0:T(8,128)(2,1)S(1)}, u32[]{:S(2)}, u32[]{:S(2)}) collective-permute-start(bf16[64,4096]{1,0:T(8,128)(2,1)S(1)} %get-tuple-element.49), channel_id=1, source_target_pairs={{0,2},{1,3},{2,0},{3,1},{4,6},{5,7},{6,4},{7,5},{8,10},{9,11},{10,... | collective-permute-start | bytes 1572872 | tf_op jit(solution)/shard_map/ppermute | solution.py:302
  11.4 19.3 %collective-permute-done.refs_5_.refs_2_ = bf16[64,4096]{1,0:T(8,128)(2,1)S(1)} collective-permute-done((bf16[64,4096]{1,0:T(8,128)(2,1)}, bf16[64,4096]{1,0:T(8,128)(2,1)S(1)}, u32[]{:S(2)}, u32[]{:S(2)}) %collective-permute-start) | collective-permute-done | bytes 524320 | tf_op jit(solution)/shard_map/ppermute | solution.py:302
  32.0 1.5 shard_map.111
  33.6 3.8 %collective-permute-start.2 = (bf16[64,4096]{1,0:T(8,128)(2,1)S(1)}, bf16[64,4096]{1,0:T(8,128)(2,1)S(1)}, u32[]{:S(2)}, u32[]{:S(2)}) collective-permute-start(bf16[64,4096]{1,0:T(8,128)(2,1)S(1)} %get-tuple-element.47), channel_id=1, source_target_pairs={{0,2},{1,3},{2,0},{3,1},{4,6},{5,7},{6,4},{7,5},{8,10},{9,11},{10,... | collective-permute-start | bytes 1572872 | tf_op jit(solution)/shard_map/ppermute | solution.py:302
  38.0 8.4 %collective-permute-done.4.refs_3_ = bf16[64,4096]{1,0:T(8,128)(2,1)S(1)} collective-permute-done((bf16[64,4096]{1,0:T(8,128)(2,1)S(1)}, bf16[64,4096]{1,0:T(8,128)(2,1)S(1)}, u32[]{:S(2)}, u32[]{:S(2)}) %collective-permute-start.4) | collective-permute-done | bytes 524320 | tf_op jit(solution)/shard_map/ppermute | solution.py:302
  46.3 2.8 %copy-done = bf16[1,4096,768]{2,1,0:T(8,128)(2,1)S(1)} copy-done((bf16[1,4096,768]{2,1,0:T(8,128)(2,1)S(1)}, bf16[1,4096,768]{2,1,0:T(8,128)(2,1)}, u32[]{:S(2)}) %copy-start) | copy-done | bytes 6291480
  49.1 2.8 %copy-done.1 = bf16[1,4096,768]{2,1,0:T(8,128)(2,1)S(1)} copy-done((bf16[1,4096,768]{2,1,0:T(8,128)(2,1)S(1)}, bf16[1,4096,768]{2,1,0:T(8,128)(2,1)}, u32[]{:S(2)}) %copy-start.1) | copy-done | bytes 6291480
  51.9 6.0 %shard_map.112 = (bf16[256,768]{1,0:T(8,128)(2,1)S(1)}, bf16[768,256]{1,0:T(8,128)(2,1)S(1)}, f32[768,256]{1,0:T(8,128)S(1)}, f32[768,256]{1,0:T(8,128)S(1)}) custom-call(s32[2]{0:T(128)S(1)} %pad_add_fusion.refs_0_, bf16[64,4096]{1,0:T(8,128)(2,1)S(1)} %get-tuple-element.43.refs_4_.refs_1_, bf16[64,4096]{1,0:T(8,128)(2,1)S(1)} %collective-permute-done.refs_5_.refs_2_, ...), custom_call_target="tpu_custom_call" | custom-call | flops 1 | bytes 1 | tf_op jit(solution)/shard_map/pallas_call | solution.py:33
  57.9 1.8 shard_map.113.refs_5_.refs_1_
  59.7 31.5 %collective-permute-done.2.refs_3_ = bf16[64,4096]{1,0:T(8,128)(2,1)S(1)} collective-permute-done((bf16[64,4096]{1,0:T(8,128)(2,1)S(1)}, bf16[64,4096]{1,0:T(8,128)(2,1)S(1)}, u32[]{:S(2)}, u32[]{:S(2)}) %collective-permute-start.2) | collective-permute-done | bytes 524320 | tf_op jit(solution)/shard_map/ppermute | solution.py:302
  91.3 1.8 shard_map.114.refs_1_.refs_3_.refs_2_
  93.1 2.1 shard_map.115.refs_6_
  95.2 5.0 %shard_map.116 = (bf16[256,1536]{1,0:T(8,128)(2,1)S(1)}, bf16[1536,256]{1,0:T(8,128)(2,1)S(1)}, f32[1,256]{1,0:T(1,128)S(1)}) custom-call(s32[2]{0:T(128)S(1)} %pad_add_fusion.refs_0_, bf16[1,768,4096]{2,1,0:T(8,128)(2,1)S(1)} %bitcast.10, bf16[4096,256]{1,0:T(8,128)(2,1)S(1)} %shard_map.114.refs_1_.refs_3_.refs_2_, ...), custom_call_target="tpu_custom_call" | custom-call | flops 1 | bytes 1 | tf_op jit(solution)/shard_map/pallas_call | solution.py:33
  100.9 2.5 %shard_map.117 = (bf16[2,256,768]{2,1,0:T(8,128)(2,1)S(1)}, f32[2,256,768]{2,1,0:T(8,128)S(1)}, bf16[2,256,768]{2,1,0:T(8,128)(2,1)S(1)}, f32[2,256,768]{2,1,0:T(8,128)S(1)}) custom-call(s32[2]{0:T(128)S(1)} %pad_add_fusion.refs_0_, bf16[4096,256]{1,0:T(8,128)(2,1)S(1)} %shard_map.114.refs_1_.refs_3_.refs_2_, ...), custom_call_target="tpu_custom_call" | custom-call | flops 1 | bytes 1 | tf_op jit(solution)/shard_map/pallas_call | solution.py:33
  104.5 2.1 shard_map.118.refs_3_
  106.6 2.1 shard_map.119.refs_5_
  109.4 1.5 collective-permute-start.11
  110.9 1.5 collective-permute-start.10
  112.4 7.0 %shard_map.120 = (bf16[64,4224]{1,0:T(8,128)(2,1)S(1)}, bf16[64,4224]{1,0:T(8,128)(2,1)}, bf16[64,4224]{1,0:T(8,128)(2,1)}, bf16[64,4224]{1,0:T(8,128)(2,1)}) custom-call(s32[2]{0:T(128)S(1)} %pad_add_fusion.refs_0_, bf16[1536,256]{1,0:T(8,128)(2,1)S(1)} %get-tuple-element.55.refs_1_, f32[1,256]{1,0:T(1,128)S(1)} %get-tuple-element.56.refs_2_, ...), custom_call_target="tpu_custom_call" | custom-call | flops 1 | bytes 1 | tf_op jit(solution)/shard_map/pallas_call | solution.py:33
  119.4 10.4 %collective-permute-start.7 = (bf16[64,4224]{1,0:T(8,128)(2,1)}, bf16[64,4224]{1,0:T(8,128)(2,1)}, u32[]{:S(2)}, u32[]{:S(2)}) collective-permute-start(bf16[64,4224]{1,0:T(8,128)(2,1)} %get-tuple-element.60), channel_id=1, source_target_pairs={{0,1},{1,0},{2,3},{3,2},{4,5},{5,4},{6,7},{7,6},{8,9},{9,8},{10,11... | collective-permute-start | bytes 1622024 | tf_op jit(solution)/shard_map/ppermute | solution.py:302
  130.8 1.5 collective-permute-start.9
  132.3 4.9 %shard_map.121 = (bf16[2,256,1536]{2,1,0:T(8,128)(2,1)}, f32[2,256,1536]{2,1,0:T(8,128)S(1)}, bf16[2,256,1536]{2,1,0:T(8,128)(2,1)}, f32[2,256,1536]{2,1,0:T(8,128)S(1)}) custom-call(s32[2]{0:T(128)S(1)} %pad_add_fusion.refs_0_, bf16[4096,256]{1,0:T(8,128)(2,1)S(1)} %shard_map.113.refs_5_.refs_1_, bf16[256,1536]{1,0:T(8,128)(2,1)S(1)} %get-tuple-element.57.refs_4_.refs_2_, ...), custom_call_target="tpu_custom_call" | custom-call | flops 1 | bytes 1 | tf_op jit(solution)/shard_map/pallas_call | solution.py:33
  139.5 33.5 %collective-permute-done.15.refs_8_ = bf16[2,256,1536]{2,1,0:T(8,128)(2,1)} collective-permute-done((bf16[2,256,1536]{2,1,0:T(8,128)(2,1)}, bf16[2,256,1536]{2,1,0:T(8,128)(2,1)}, u32[]{:S(2)}, u32[]{:S(2)}) %collective-permute-start.15) | collective-permute-done | bytes 1572896 | tf_op jit(solution)/shard_map/ppermute | solution.py:302
  175.4 5.3 %shard_map.124 = (bf16[1,256,2304]{2,1,0:T(8,128)(2,1)}, f32[1,256,2304]{2,1,0:T(8,128)S(1)}, bf16[1,256,2304]{2,1,0:T(8,128)(2,1)}, f32[1,256,2304]{2,1,0:T(8,128)S(1)}) custom-call(s32[2]{0:T(128)S(1)} %pad_add_fusion.refs_0_, f32[2,256,768]{2,1,0:T(8,128)S(1)} %get-tuple-element.63.refs_1_, bf16[2,256,768]{2,1,0:T(8,128)(2,1)S(1)} %copy-done.5, ...), custom_call_target="tpu_custom_call" | custom-call | flops 1 | bytes 1 | tf_op jit(solution)/shard_map/pallas_call | solution.py:33
  181.3 1.5 collective-permute-start.16
  182.8 4.9 %shard_map.125 = (bf16[128,4096]{1,0:T(8,128)(2,1)}, bf16[128,2]{1,0:T(8,128)(2,1)S(1)}) custom-call(s32[2]{0:T(128)S(1)} %pad_add_fusion.refs_0_, bf16[128,256]{1,0:T(8,128)(2,1)S(1)} %get-tuple-element.42.refs_1_, s32[128,2]{1,0:T(8,128)S(1)} %copy-done.14, bf16[128,2]{1,0:T(8,128)(2,1)S(1)} %copy-done.16, ...), custom_call_target="tpu_custom_call" | custom-call | flops 999999995904 | bytes 1 | tf_op jit(solution)/shard_map/pallas_call | solution.py:33
  188.3 18.5 %collective-permute-done.17.refs_4_ = bf16[1,256,2304]{2,1,0:T(8,128)(2,1)} collective-permute-done((bf16[1,256,2304]{2,1,0:T(8,128)(2,1)}, bf16[1,256,2304]{2,1,0:T(8,128)(2,1)}, u32[]{:S(2)}, u32[]{:S(2)}) %collective-permute-start.17) | collective-permute-done | bytes 1179680 | tf_op jit(solution)/shard_map/ppermute | solution.py:302
  207.0 1.7 copy-done.7
  209.9 4.8 %shard_map.126 = (f32[768,512]{1,0:T(8,128)}, f32[512,768]{1,0:T(8,128)}, f32[512,768]{1,0:T(8,128)}) custom-call(s32[2]{0:T(128)S(1)} %pad_add_fusion.refs_0_, f32[1,256,2304]{2,1,0:T(8,128)S(1)} %get-tuple-element.73.refs_1_, bf16[1,256,2304]{2,1,0:T(8,128)(2,1)} %collective-permute-done.16.refs_2_, f32[1,256,2304]{2,1,0:T(8,128)S(1)} %copy-done.7, ...), custom_call_target="tpu_custom_call" | custom-call | flops 1 | bytes 1 | tf_op jit(solution)/shard_map/pallas_call | solution.py:33
  (74 shorter events, 14.2 us)
Async XLA Ops:
  1.4 56.5 %copy-start.13 = (s32[128,2]{1,0:T(8,128)}, s32[128,2]{1,0:T(8,128)S(1)}, u32[]{:S(2)}) copy-start(s32[128,2]{1,0:T(8,128)S(1)} %copy.12.refs_1_.refs_2_) | copy-start | bytes 3076
  5.0 25.7 %collective-permute-start = (bf16[64,4096]{1,0:T(8,128)(2,1)}, bf16[64,4096]{1,0:T(8,128)(2,1)S(1)}, u32[]{:S(2)}, u32[]{:S(2)}) collective-permute-start(bf16[64,4096]{1,0:T(8,128)(2,1)} %get-tuple-element.44), channel_id=1, source_target_pairs={{0,1},{1,0},{2,3},{3,2},{4,5},{5,4},{6,7},{7,6},{8,9},{9,8},{10,11... | collective-permute-start | bytes 1572872 | tf_op jit(solution)/shard_map/ppermute | solution.py:302
  8.0 38.3 %collective-permute-start.4 = (bf16[64,4096]{1,0:T(8,128)(2,1)S(1)}, bf16[64,4096]{1,0:T(8,128)(2,1)S(1)}, u32[]{:S(2)}, u32[]{:S(2)}) collective-permute-start(bf16[64,4096]{1,0:T(8,128)(2,1)S(1)} %get-tuple-element.49), channel_id=1, source_target_pairs={{0,2},{1,3},{2,0},{3,1},{4,6},{5,7},{6,4},{7,5},{8,10},{9,11},{10,... | collective-permute-start | bytes 1572872 | tf_op jit(solution)/shard_map/ppermute | solution.py:302
  10.6 35.7 %collective-permute-start.5 = (bf16[64,4096]{1,0:T(8,128)(2,1)S(1)}, bf16[64,4096]{1,0:T(8,128)(2,1)S(1)}, u32[]{:S(2)}, u32[]{:S(2)}) collective-permute-start(bf16[64,4096]{1,0:T(8,128)(2,1)S(1)} %get-tuple-element.50), channel_id=1, source_target_pairs={{0,3},{1,2},{2,1},{3,0},{4,7},{5,6},{6,5},{7,4},{8,11},{9,10},{10,... | collective-permute-start | bytes 1572872 | tf_op jit(solution)/shard_map/ppermute | solution.py:302
  11.4 46.5 %copy-start.15 = (bf16[128,2]{1,0:T(8,128)(2,1)}, bf16[128,2]{1,0:T(8,128)(2,1)S(1)}, u32[]{:S(2)}) copy-start(bf16[128,2]{1,0:T(8,128)(2,1)S(1)} %copy.16.refs_2_.refs_3_) | copy-start | bytes 1540
  33.5 26.2 %collective-permute-start.1 = (bf16[64,4096]{1,0:T(8,128)(2,1)S(1)}, bf16[64,4096]{1,0:T(8,128)(2,1)S(1)}, u32[]{:S(2)}, u32[]{:S(2)}) collective-permute-start(bf16[64,4096]{1,0:T(8,128)(2,1)S(1)} %get-tuple-element.46), channel_id=1, source_target_pairs={{0,1},{1,0},{2,3},{3,2},{4,5},{5,4},{6,7},{7,6},{8,9},{9,8},{10,11... | collective-permute-start | bytes 1572872 | tf_op jit(solution)/shard_map/ppermute | solution.py:302
  33.6 57.7 %collective-permute-start.2 = (bf16[64,4096]{1,0:T(8,128)(2,1)S(1)}, bf16[64,4096]{1,0:T(8,128)(2,1)S(1)}, u32[]{:S(2)}, u32[]{:S(2)}) collective-permute-start(bf16[64,4096]{1,0:T(8,128)(2,1)S(1)} %get-tuple-element.47), channel_id=1, source_target_pairs={{0,2},{1,3},{2,0},{3,1},{4,6},{5,7},{6,4},{7,5},{8,10},{9,11},{10,... | collective-permute-start | bytes 1572872 | tf_op jit(solution)/shard_map/ppermute | solution.py:302
  37.4 53.9 %collective-permute-start.3 = (bf16[64,4096]{1,0:T(8,128)(2,1)S(1)}, bf16[64,4096]{1,0:T(8,128)(2,1)S(1)}, u32[]{:S(2)}, u32[]{:S(2)}) collective-permute-start(bf16[64,4096]{1,0:T(8,128)(2,1)S(1)} %get-tuple-element.48), channel_id=1, source_target_pairs={{0,3},{1,2},{2,1},{3,0},{4,7},{5,6},{6,5},{7,4},{8,11},{9,10},{10,... | collective-permute-start | bytes 1572872 | tf_op jit(solution)/shard_map/ppermute | solution.py:302
  46.3 2.8 %copy-start = (bf16[1,4096,768]{2,1,0:T(8,128)(2,1)S(1)}, bf16[1,4096,768]{2,1,0:T(8,128)(2,1)}, u32[]{:S(2)}) copy-start(bf16[1,4096,768]{2,1,0:T(8,128)(2,1)} %refs_3_.4) | copy-start | bytes 18874372
  49.1 2.8 %copy-start.1 = (bf16[1,4096,768]{2,1,0:T(8,128)(2,1)S(1)}, bf16[1,4096,768]{2,1,0:T(8,128)(2,1)}, u32[]{:S(2)}) copy-start(bf16[1,4096,768]{2,1,0:T(8,128)(2,1)} %refs_4_.1) | copy-start | bytes 18874372
  91.3 4.0 %slice-start.4 = ((s8[6291456]{0:T(1024)(128)(4,1)}), s8[4194304]{0:T(1024)(128)(4,1)S(1)}, s32[]{:S(2)}) async-start(s8[6291456]{0:T(1024)(128)(4,1)} %bitcast.9), calls=%async_computation.4 | async-start | bytes 8388608
  93.0 2.2 %slice-start.5 = ((s8[6291456]{0:T(1024)(128)(4,1)}), s8[2097152]{0:T(1024)(128)(4,1)S(1)}, s32[]{:S(2)}) async-start(s8[6291456]{0:T(1024)(128)(4,1)} %bitcast.9), calls=%async_computation.5 | async-start | bytes 4194304
  95.1 5.7 %collective-permute-start.6 = (bf16[2048,768]{1,0:T(8,128)(2,1)S(1)}, bf16[2048,768]{1,0:T(8,128)(2,1)S(1)}, u32[]{:S(2)}, u32[]{:S(2)}) collective-permute-start(bf16[2048,768]{1,0:T(8,128)(2,1)S(1)} %shard_map.115.refs_6_), channel_id=1, source_target_pairs={{0,4},{4,0},{8,12},{12,8},{16,20},{20,16},{24,28},{28,24},{1,5},{5... | collective-permute-start | bytes 9437192 | tf_op jit(solution)/shard_map/ppermute | solution.py:302
  100.9 11.5 %slice-start.2 = ((s8[6291456]{0:T(1024)(128)(4,1)}), s8[2097152]{0:T(1024)(128)(4,1)S(1)}, s32[]{:S(2)}) async-start(s8[6291456]{0:T(1024)(128)(4,1)} %bitcast.7), calls=%async_computation.2 | async-start | bytes 4194304
  104.5 7.9 %slice-start = ((s8[6291456]{0:T(1024)(128)(4,1)}), s8[4194304]{0:T(1024)(128)(4,1)S(1)}, s32[]{:S(2)}) async-start(s8[6291456]{0:T(1024)(128)(4,1)} %bitcast.5), calls=%async_computation | async-start | bytes 8388608
  104.5 7.9 %slice-start.3 = ((s8[6291456]{0:T(1024)(128)(4,1)}), s8[4194304]{0:T(1024)(128)(4,1)S(1)}, s32[]{:S(2)}) async-start(s8[6291456]{0:T(1024)(128)(4,1)} %bitcast.7), calls=%async_computation.3 | async-start | bytes 8388608
  106.6 5.7 %slice-start.1 = ((s8[6291456]{0:T(1024)(128)(4,1)}), s8[2097152]{0:T(1024)(128)(4,1)S(1)}, s32[]{:S(2)}) async-start(s8[6291456]{0:T(1024)(128)(4,1)} %bitcast.5), calls=%async_computation.1 | async-start | bytes 4194304
  108.8 21.0 %collective-permute-start.13 = (bf16[2048,768]{1,0:T(8,128)(2,1)S(1)}, bf16[2048,768]{1,0:T(8,128)(2,1)S(1)}, u32[]{:S(2)}, u32[]{:S(2)}) collective-permute-start(bf16[2048,768]{1,0:T(8,128)(2,1)S(1)} %shard_map.119.refs_5_), channel_id=1, source_target_pairs={{0,4},{4,0},{8,12},{12,8},{16,20},{20,16},{24,28},{28,24},{1,5},{5... | collective-permute-start | bytes 9437192 | tf_op jit(solution)/shard_map/ppermute | solution.py:302
  109.0 21.8 %collective-permute-start.12 = (bf16[2048,768]{1,0:T(8,128)(2,1)S(1)}, bf16[2048,768]{1,0:T(8,128)(2,1)S(1)}, u32[]{:S(2)}, u32[]{:S(2)}) collective-permute-start(bf16[2048,768]{1,0:T(8,128)(2,1)S(1)} %shard_map.118.refs_3_), channel_id=1, source_target_pairs={{0,4},{4,0},{8,12},{12,8},{16,20},{20,16},{24,28},{28,24},{1,5},{5... | collective-permute-start | bytes 9437192 | tf_op jit(solution)/shard_map/ppermute | solution.py:302
  109.4 27.9 %collective-permute-start.11 = (bf16[2,256,768]{2,1,0:T(8,128)(2,1)S(1)}, bf16[2,256,768]{2,1,0:T(8,128)(2,1)S(1)}, u32[]{:S(2)}, u32[]{:S(2)}) collective-permute-start(bf16[2,256,768]{2,1,0:T(8,128)(2,1)S(1)} %get-tuple-element.65), channel_id=1, source_target_pairs={{0,16},{4,20},{8,24},{12,28},{16,0},{20,4},{24,8},{28,12},{1,17},{... | collective-permute-start | bytes 2359304 | tf_op jit(solution)/shard_map/ppermute | solution.py:302
  110.9 26.9 %collective-permute-start.10 = (bf16[2,256,768]{2,1,0:T(8,128)(2,1)S(1)}, bf16[2,256,768]{2,1,0:T(8,128)(2,1)S(1)}, u32[]{:S(2)}, u32[]{:S(2)}) collective-permute-start(bf16[2,256,768]{2,1,0:T(8,128)(2,1)S(1)} %get-tuple-element.58.refs_3_), channel_id=1, source_target_pairs={{0,8},{4,12},{8,0},{12,4},{16,24},{20,28},{24,16},{28,20},{1,9},{5... | collective-permute-start | bytes 2359304 | tf_op jit(solution)/shard_map/ppermute | solution.py:302
  119.4 63.4 %collective-permute-start.7 = (bf16[64,4224]{1,0:T(8,128)(2,1)}, bf16[64,4224]{1,0:T(8,128)(2,1)}, u32[]{:S(2)}, u32[]{:S(2)}) collective-permute-start(bf16[64,4224]{1,0:T(8,128)(2,1)} %get-tuple-element.60), channel_id=1, source_target_pairs={{0,1},{1,0},{2,3},{3,2},{4,5},{5,4},{6,7},{7,6},{8,9},{9,8},{10,11... | collective-permute-start | bytes 1622024 | tf_op jit(solution)/shard_map/ppermute | solution.py:302
  129.8 53.0 %collective-permute-start.8 = (bf16[64,4224]{1,0:T(8,128)(2,1)}, bf16[64,4224]{1,0:T(8,128)(2,1)}, u32[]{:S(2)}, u32[]{:S(2)}) collective-permute-start(bf16[64,4224]{1,0:T(8,128)(2,1)} %get-tuple-element.61), channel_id=1, source_target_pairs={{0,2},{1,3},{2,0},{3,1},{4,6},{5,7},{6,4},{7,5},{8,10},{9,11},{10,... | collective-permute-start | bytes 1622024 | tf_op jit(solution)/shard_map/ppermute | solution.py:302
  130.8 52.0 %collective-permute-start.9 = (bf16[64,4224]{1,0:T(8,128)(2,1)}, bf16[64,4224]{1,0:T(8,128)(2,1)}, u32[]{:S(2)}, u32[]{:S(2)}) collective-permute-start(bf16[64,4224]{1,0:T(8,128)(2,1)} %get-tuple-element.62), channel_id=1, source_target_pairs={{0,3},{1,2},{2,1},{3,0},{4,7},{5,6},{6,5},{7,4},{8,11},{9,10},{10,... | collective-permute-start | bytes 1622024 | tf_op jit(solution)/shard_map/ppermute | solution.py:302
  137.3 35.6 %collective-permute-start.15 = (bf16[2,256,1536]{2,1,0:T(8,128)(2,1)}, bf16[2,256,1536]{2,1,0:T(8,128)(2,1)}, u32[]{:S(2)}, u32[]{:S(2)}) collective-permute-start(bf16[2,256,1536]{2,1,0:T(8,128)(2,1)} %get-tuple-element.69), channel_id=1, source_target_pairs={{0,16},{4,20},{8,24},{12,28},{16,0},{20,4},{24,8},{28,12},{1,17},{... | collective-permute-start | bytes 4718600 | tf_op jit(solution)/shard_map/ppermute | solution.py:302
  137.8 35.4 %collective-permute-start.14 = (bf16[2,256,1536]{2,1,0:T(8,128)(2,1)}, bf16[2,256,1536]{2,1,0:T(8,128)(2,1)}, u32[]{:S(2)}, u32[]{:S(2)}) collective-permute-start(bf16[2,256,1536]{2,1,0:T(8,128)(2,1)} %get-tuple-element.67.refs_1_), channel_id=1, source_target_pairs={{0,8},{4,12},{8,0},{12,4},{16,24},{20,28},{24,16},{28,20},{1,9},{5... | collective-permute-start | bytes 4718600 | tf_op jit(solution)/shard_map/ppermute | solution.py:302
  138.9 34.3 %copy-start.9 = (f32[2,256,768]{2,1,0:T(8,128)S(1)}, f32[2,256,768]{2,1,0:T(8,128)}, u32[]{:S(2)}) copy-start(f32[2,256,768]{2,1,0:T(8,128)} %copy-done.8) | copy-start | bytes 4718596
  175.4 7.4 %copy-start.14 = (s32[128,2]{1,0:T(8,128)S(1)}, s32[128,2]{1,0:T(8,128)}, u32[]{:S(2)}) copy-start(s32[128,2]{1,0:T(8,128)} %copy-done.13) | copy-start | bytes 3076
  175.4 7.4 %copy-start.16 = (bf16[128,2]{1,0:T(8,128)(2,1)S(1)}, bf16[128,2]{1,0:T(8,128)(2,1)}, u32[]{:S(2)}) copy-start(bf16[128,2]{1,0:T(8,128)(2,1)} %copy-done.15) | copy-start | bytes 1540
  180.7 7.0 %copy-start.6 = (f32[1,256,2304]{2,1,0:T(8,128)}, f32[1,256,2304]{2,1,0:T(8,128)S(1)}, u32[]{:S(2)}) copy-start(f32[1,256,2304]{2,1,0:T(8,128)S(1)} %get-tuple-element.74.refs_3_) | copy-start | bytes 7077892
  180.7 26.1 %collective-permute-start.17 = (bf16[1,256,2304]{2,1,0:T(8,128)(2,1)}, bf16[1,256,2304]{2,1,0:T(8,128)(2,1)}, u32[]{:S(2)}, u32[]{:S(2)}) collective-permute-start(bf16[1,256,2304]{2,1,0:T(8,128)(2,1)} %get-tuple-element.75), channel_id=1, source_target_pairs={{0,8},{4,12},{8,0},{12,4},{16,24},{20,28},{24,16},{28,20},{1,9},{5... | collective-permute-start | bytes 3538952 | tf_op jit(solution)/shard_map/ppermute | solution.py:302
  181.3 25.8 %collective-permute-start.16 = (bf16[1,256,2304]{2,1,0:T(8,128)(2,1)}, bf16[1,256,2304]{2,1,0:T(8,128)(2,1)}, u32[]{:S(2)}, u32[]{:S(2)}) collective-permute-start(bf16[1,256,2304]{2,1,0:T(8,128)(2,1)} %get-tuple-element.70.refs_12_), channel_id=1, source_target_pairs={{0,16},{4,20},{8,24},{12,28},{16,0},{20,4},{24,8},{28,12},{1,17},{... | collective-permute-start | bytes 3538952 | tf_op jit(solution)/shard_map/ppermute | solution.py:302
  (9 other events, 12.6 us)

commit v3 on v2

v3 whole, which is shorter than its diff:
```python
import functools
import math

import jax
import jax.numpy as jnp
from jax import lax
from jax.experimental import pallas as pl
from jax.experimental.pallas import tpu as pltpu
from jax.sharding import PartitionSpec as P

CAP = 64
EXTRA = 128
F32 = jnp.float32
BF16 = jnp.bfloat16
LONG = 6 * 10**10
VMEM_SPARE = 2 * 1024 * 1024


def whole(shape):
    return pl.BlockSpec(shape, lambda i, pos: (0,) * len(shape))


def call(kernel, grid, in_specs, out_specs, out_shape, pos, args, after, scratch=(), cost=1):
    held = sum(math.prod(ref.shape) * ref.dtype.itemsize for ref in scratch)
    for spec, array in zip([*in_specs, *out_specs], [*args, *out_shape]):
        if spec.block_shape is not None:
            held += 2 * math.prod(spec.block_shape) * array.dtype.itemsize
    first, count, last = 1 + len(args), len(after), len(out_shape)

    def ordered(*refs):
        outs = refs[first + count :]
        kernel(*refs[:first], *outs[:last], *outs[last + 1 :])
        outs[last][...] = jnp.zeros(outs[last].shape, F32)

    return pl.pallas_call(
        ordered,
        grid_spec=pltpu.PrefetchScalarGridSpec(
            num_scalar_prefetch=1,
            grid=grid,
            in_specs=list(in_specs) + [pl.BlockSpec(memory_space=pl.ANY)] * count,
            out_specs=[*out_specs, whole((8, 128))],
            scratch_shapes=list(scratch),
        ),
        out_shape=[*out_shape, shape_of((8, 128), F32)],
        compiler_params=pltpu.CompilerParams(vmem_limit_bytes=held + VMEM_SPARE),
        cost_estimate=pl.CostEstimate(flops=cost, bytes_accessed=1, transcendentals=0),
    )(pos, *args, *after)


def shape_of(shape, dtype=BF16):
    return jax.ShapeDtypeStruct(shape, dtype)


def dot(left, right):
    return jnp.dot(left, right, preferred_element_type=F32)


def shard_at(i, me, replicas):
    half = replicas // 2
    return jnp.where(i < half, 2 * i + 1, 2 * i - replicas) ^ me


def slot_matrix(routes_ref, my_expert, slots):
    top, tok = routes_ref.shape
    index = lax.broadcasted_iota(jnp.int32, (slots, tok), 0)
    expert = (index // CAP) ^ my_expert
    hit = jnp.zeros((slots, tok), jnp.bool_)
    for k in range(top):
        hit = hit | (routes_ref[k : k + 1, :] == expert)
    named = jnp.where(hit, 1.0, 0.0)
    before = lax.broadcasted_iota(jnp.int32, (tok, tok), 0) < lax.broadcasted_iota(
        jnp.int32, (tok, tok), 1
    )
    rank = dot(named.astype(BF16), jnp.where(before, 1.0, 0.0).astype(BF16))
    return jnp.where(rank == (index % CAP).astype(F32), named, 0.0), expert


def send_tokens_kernel(experts, replicas, pos_ref, routes_ref, tok_ref, *outs):
    place, _ = slot_matrix(routes_ref, pos_ref[1], experts * CAP)
    place = place.astype(BF16)
    width = tok_ref.shape[1] // replicas
    for i in range(replicas):
        at = pl.ds(pl.multiple_of(shard_at(i, pos_ref[0], replicas) * width, width), width)
        rows = dot(place, tok_ref[:, at]).astype(BF16)
        for j in range(experts):
            outs[j][:, i * width : (i + 1) * width] = rows[j * CAP : (j + 1) * CAP]


def send_cot_kernel(
    experts, replicas, pos_ref, routes_ref, probs_ref, cot_ref, *rest
):
    outs, place_t_ref = rest[:-1], rest[-1]
    place, expert = slot_matrix(routes_ref, pos_ref[1], experts * CAP)
    probs = probs_ref[...].astype(F32)
    weight = jnp.zeros_like(place)
    for k in range(routes_ref.shape[0]):
        weight += jnp.where(routes_ref[k : k + 1, :] == expert, probs[k : k + 1, :], 0.0)
    weighted = (place * weight).astype(BF16)
    width = cot_ref.shape[1] // replicas
    for i in range(replicas):
        at = pl.ds(pl.multiple_of(shard_at(i, pos_ref[0], replicas) * width, width), width)
        rows = dot(weighted, cot_ref[:, at]).astype(BF16)
        for j in range(experts):
            outs[j][:, i * width : (i + 1) * width] = rows[j * CAP : (j + 1) * CAP]
    place_t_ref[...] = place.T.astype(BF16)


def forward_kernel(experts, replicas, pos_ref, *rest):
    xs, (wg_ref, wu_ref), outs, x_ref = (
        rest[:experts],
        rest[experts : experts + 2],
        rest[experts + 2 : -1],
        rest[-1],
    )
    act_ref, act_t_ref, for_gate_ref, for_up_ref = outs

    @pl.when(pl.program_id(0) == 0)
    def _():
        for j in range(experts):
            x_ref[j * CAP : (j + 1) * CAP, :] = xs[j][...]

    width = wg_ref.shape[1] // replicas
    gate = jnp.zeros(act_ref.shape, F32)
    up = jnp.zeros(act_ref.shape, F32)
    for i in range(replicas):
        at = pl.ds(pl.multiple_of(shard_at(i, pos_ref[0], replicas) * width, width), width)
        part = x_ref[:, i * width : (i + 1) * width]
        gate += dot(part, wg_ref[0, at, :])
        up += dot(part, wu_ref[0, at, :])
    gate, up = gate.T, up.T
    sig = jax.nn.sigmoid(gate)
    silu = gate * sig
    act = (silu * up).astype(BF16)
    act_ref[...] = act.T
    act_t_ref[...] = act
    for_gate_ref[...] = up * sig * (1.0 + gate * (1.0 - sig))
    for_up_ref[...] = silu


def joined(refs):
    return jnp.concatenate([ref[...] for ref in refs], axis=0)


def transpose_kernel(pos_ref, *rest):
    rest[-1][...] = joined(rest[:-1]).T


def transpose_far_kernel(scale, pos_ref, act_ref, *rest):
    ins, (far_t_ref, near_t_ref, far_ref) = rest[:-3], rest[-3:]
    middle = len(ins) // 2
    rows_t = joined(ins[:middle]).T
    far_t_ref[...] = rows_t
    far_ref[...] = (dot(rows_t, act_ref[...]) * scale).astype(BF16)
    near_t_ref[...] = joined(ins[middle:]).T


def back_hidden_kernel(pos_ref, *rest):
    weights, rest = rest[:4], rest[4:]
    far_t_ref, near_t_ref, act_ref, for_gate_ref, for_up_ref, *outs, sum_ref = rest
    delta_ref, delta_t_ref, prob_ref = outs
    i = pl.program_id(0)
    width = weights[0].shape[2]
    term = sum(
        dot(weights[at][0], ref[at % 2 * width : (at % 2 + 1) * width])
        for at, ref in enumerate((far_t_ref, far_t_ref, near_t_ref, near_t_ref))
    )

    @pl.when(i == 0)
    def _():
        sum_ref[...] = term

    @pl.when(i > 0)
    def _():
        sum_ref[...] += term

    @pl.when(i == pl.num_programs(0) - 1)
    def _():
        back = sum_ref[...]
        dh = (back * for_gate_ref[...]).astype(BF16)
        du = (back * for_up_ref[...]).astype(BF16)
        hidden = back.shape[0]
        delta_t_ref[:hidden] = dh
        delta_t_ref[hidden:] = du
        delta_ref[:, :hidden] = dh.T
        delta_ref[:, hidden:] = du.T
        prob_ref[...] = jnp.sum(act_ref[...].astype(F32) * back, axis=0, keepdims=True)


def grad_far_kernel(scale, pos_ref, xt_ref, delta_ref, *outs):
    part = (dot(xt_ref[...], delta_ref[...]) * scale).astype(BF16)
    cols = outs[0].shape[1]
    for at, out_ref in enumerate(outs):
        out_ref[...] = part[:, at * cols : (at + 1) * cols]


def grad_near_kernel(scale, pos_ref, xt_ref, delta_ref, *rest):
    others, (low_send, low_keep, high_send, high_keep) = rest[:-4], rest[-4:]
    hidden = others[0].shape[1]
    rows = xt_ref.shape[0] // 2
    half = rows // 2
    first = pl.program_id(0) < pl.num_programs(0) // 2

    def upper(out_ref, piece, at, part):
        out_ref[piece, at * half : (at + 1) * half] = part

    for at, ref in enumerate(others):
        part = dot(xt_ref[...], delta_ref[:, at * hidden : (at + 1) * hidden]) * scale
        part = (part + ref[...].astype(F32)).astype(BF16)
        low_keep[0, at * half : (at + 1) * half] = part[:half]
        low_send[0, at * half : (at + 1) * half] = part[rows : rows + half]
        for piece in (0, 1):
            high = part[piece * rows + half : (piece + 1) * rows]
            pl.when(first)(functools.partial(upper, high_keep, piece, at, high))
            pl.when(jnp.logical_not(first))(functools.partial(upper, high_send, piece, at, high))


def row_grad_kernel(pos_ref, delta_t_ref, prob_ref, wg_ref, wu_ref, *outs):
    i = pl.program_id(0)
    width, hidden = wg_ref.shape[1:]
    rows_t = dot(wg_ref[0], delta_t_ref[:hidden]) + dot(wu_ref[0], delta_t_ref[hidden:])
    rows = rows_t.astype(BF16).T
    at = pl.ds(pl.multiple_of(i * width, width), width)
    for j, out_ref in enumerate(outs):
        out_ref[:, at] = rows[j * CAP : (j + 1) * CAP]

    @pl.when(i == 0)
    def _():
        full = prob_ref[...]
        high = full.astype(BF16).astype(F32)
        lane = lax.broadcasted_iota(jnp.int32, (EXTRA, full.shape[1]), 0)
        both = jnp.where(lane == 0, high, jnp.where(lane == 1, full - high, 0.0)).T.astype(BF16)
        for j, out_ref in enumerate(outs):
            out_ref[:, out_ref.shape[1] - EXTRA :] = both[j * CAP : (j + 1) * CAP]


def total_of(refs):
    down, *rest = [ref[0].astype(F32) for ref in refs]
    first = [down, rest[0] + rest[1], rest[2] + rest[3]]
    return sum(rest[4:], jnp.concatenate(first, axis=0))


def add_kernel(pos_ref, *rest):
    ins, outs = rest[:-2], rest[-2:]
    middle = len(ins) // 2
    for refs, out_ref in zip((ins[:middle], ins[middle:]), outs):
        out_ref[0] = total_of(refs).astype(BF16)


def add_pairs_kernel(pos_ref, a_ref, b_ref, c_ref, d_ref, low_ref, high_ref):
    low_ref[...] = (a_ref[...].astype(F32) + b_ref[...].astype(F32)).astype(BF16)
    high_ref[...] = (c_ref[...].astype(F32) + d_ref[...].astype(F32)).astype(BF16)


def combine_kernel(scale, pos_ref, place_ref, routes_ref, probs_ref, *rest):
    experts = (len(rest) - 2) // 2
    x_ref, prob_ref = rest[2 * experts :]
    rows = joined(rest[:experts])
    x_ref[...] = dot(place_ref[...], rows).astype(BF16)

    @pl.when(pl.program_id(0) == 0)
    def _():
        extra = joined(rest[experts : 2 * experts])
        tok, slots = place_ref.shape
        top = routes_ref.shape[0]
        place, expert = slot_matrix(routes_ref, pos_ref[1], slots)
        value = jnp.sum(extra.astype(F32), axis=1, keepdims=True)
        probs = probs_ref[...].astype(F32)
        line = lax.broadcasted_iota(jnp.int32, probs.shape, 0)
        result = jnp.zeros(probs.shape, F32)
        for k in range(top):
            mine = jnp.where(routes_ref[k : k + 1, :] == expert, place, 0.0)
            found = jnp.sum(mine * value, axis=0, keepdims=True)
            result += jnp.where(line == k, found, 0.0)
        prob_ref[...] = (result * scale / probs).astype(BF16)


def finish_kernel(
    pos_ref, low_ref, low_last_ref, high_ref, high_last_ref, down_ref, gate_ref, up_ref
):
    rows = gate_ref.shape[0]
    lower = pl.program_id(0) < pl.num_programs(0) // 2

    def write(ref, last_ref):
        total = ref[0].astype(F32) + last_ref[0].astype(F32)
        down_ref[...] = total[:rows].T
        gate_ref[...] = total[rows : 2 * rows]
        up_ref[...] = total[2 * rows :]

    @pl.when(lower)
    def _():
        write(low_ref, low_last_ref)

    @pl.when(jnp.logical_not(lower))
    def _():
        write(high_ref, high_last_ref)


def flip(x, axis, bit):
    count = lax.axis_size(axis)
    return lax.ppermute(x, axis, [(i, i ^ bit) for i in range(count)])


def body(tokens, out_grad, routes, gate_probs, w_gate, w_up, w_down):
    tok, width = tokens.shape
    experts = lax.axis_size("expert")
    replicas = lax.axis_size("dp")
    hidden = w_gate.shape[2]
    slots = experts * CAP
    shard = width // replicas
    pieces = replicas // 2
    levels = pieces.bit_length() - 1
    grad_scale = 1.0 / math.sqrt(tok * replicas * experts)
    prob_scale = 1.0 / math.sqrt(width)
    pos = jnp.stack([lax.axis_index("dp"), lax.axis_index("expert")]).astype(jnp.int32)
    chain = []

    def run(kernel, grid, in_specs, out_specs, out_shape, args, after=(), **kw):
        out = call(
            kernel, grid, in_specs, out_specs, out_shape, pos, args, [*chain[-1:], *after], **kw
        )
        chain.append(out[-1])
        return out[:-1]

    def exchange(blocks):
        return [blocks[0]] + [flip(blocks[j], "expert", j) for j in range(experts - 1, 0, -1)][::-1]

    def block_specs(cols, at):
        return [pl.BlockSpec((CAP, cols), at) for _ in range(experts)]

    def cross(low, high, level):
        return flip(low, "dp", 2 << level), flip(high, "dp", 2 << (levels - 1 - level))

    half = shard // 2
    steps, rows = 1, half

    def add(halves, level, count, places):
        specs, arrays = [], []
        for high, (down, keep, came, *later) in enumerate(halves):

            def spec(size, first, behind, high=high):
                shift = 0 if high else behind
                return pl.BlockSpec(
                    (1, size, hidden),
                    lambda i, pos: (places[high](i // steps) << shift, first + i % steps, 0),
                )

            specs += [spec(rows, at, level - 1) for at in (0, 0, 0, steps, steps)]
            arrays += [down, keep, came, keep, came]
            for at, array in enumerate(later):
                specs.append(spec(3 * rows, 0, level - 2 - at))
                arrays.append(array)
        return run(
            add_kernel,
            (count * steps,),
            specs,
            [pl.BlockSpec((1, 3 * rows, hidden), lambda i, pos: (i // steps, i % steps, 0))] * 2,
            [shape_of((count, 3 * half, hidden))] * 2,
            arrays,
        )

    def mark(after, cost):
        run(lambda pos_ref: None, (1,), [], [], [], [], after, cost=cost)

    blocks = [whole((CAP, width)) for _ in range(experts)]
    routes, gate_probs = routes.T, gate_probs.T
    x_out = run(
        functools.partial(send_tokens_kernel, experts, replicas),
        (1,),
        [whole(routes.shape), whole(tokens.shape)],
        blocks,
        [shape_of((CAP, width)) for _ in range(experts)],
        [routes, tokens],
    )
    x_in = exchange(x_out)

    *dy_out, place = run(
        functools.partial(send_cot_kernel, experts, replicas),
        (1,),
        [whole(routes.shape), whole(gate_probs.shape), whole(out_grad.shape)],
        [*blocks, whole((tok, slots))],
        [shape_of((CAP, width)) for _ in range(experts)] + [shape_of((tok, slots))],
        [routes, gate_probs, out_grad],
        [x_in[1]],
    )
    dy = exchange(dy_out)

    def grad_near(rows_t, first, right, others):
        size = half * len(others)
        grid = pieces // 2
        return run(
            functools.partial(grad_near_kernel, grad_scale),
            (grid,),
            [
                pl.BlockSpec((2 * shard, slots), lambda i, pos: (i + first, 0)),
                whole(right.shape),
            ]
            + [pl.BlockSpec((2 * shard, hidden), lambda i, pos: (i, 0))] * len(others),
            [pl.BlockSpec((1, size, hidden), lambda i, pos: (i, 0, 0))] * 2
            + [
                pl.BlockSpec(
                    (2, size, hidden), lambda i, pos: (jnp.maximum(i - grid // 2, 0), 0, 0)
                ),
                pl.BlockSpec(
                    (2, size, hidden), lambda i, pos: (jnp.minimum(i, grid // 2 - 1), 0, 0)
                ),
            ],
            [shape_of((grid, size, hidden))] * 4,
            [rows_t, right, *others],
        )

    hid = hidden // 3
    act, act_t, for_gate, for_up = run(
        functools.partial(forward_kernel, experts, replicas),
        (3,),
        [whole((CAP, width)) for _ in range(experts)]
        + [pl.BlockSpec((1, width, hid), lambda i, pos: (0, 0, i)) for _ in range(2)],
        [pl.BlockSpec((slots, hid), lambda i, pos: (0, i))]
        + [pl.BlockSpec((hid, slots), lambda i, pos: (i, 0))] * 3,
        [shape_of((slots, hidden))] + [shape_of((hidden, slots), t) for t in (BF16, F32, F32)],
        [*x_in, w_gate, w_up],
        scratch=[pltpu.VMEM((slots, width), BF16)],
    )
    (x_t,) = run(
        transpose_kernel,
        (4,),
        block_specs(width // 4, lambda i, pos: (0, i)),
        [pl.BlockSpec((width // 4, slots), lambda i, pos: (i, 0))],
        [shape_of((width, slots))],
        x_in,
    )
    far_t, near_t, far = run(
        functools.partial(transpose_far_kernel, grad_scale),
        (2,),
        [whole((slots, hidden))]
        + block_specs(width // 4, lambda i, pos: (0, i))
        + block_specs(width // 4, lambda i, pos: (0, i + 2)),
        [pl.BlockSpec((width // 4, slots), lambda i, pos: (i, 0))] * 2
        + [pl.BlockSpec((width // 4, hidden), lambda i, pos: (i, 0))],
        [shape_of((width // 2, slots))] * 2 + [shape_of((width // 2, hidden))],
        [act, *dy, *dy],
    )
    other = flip(far, "dp", 1)
    delta, delta_t, prob = run(
        back_hidden_kernel,
        (replicas // 4,),
        [
            pl.BlockSpec(
                (1, hidden, shard),
                lambda i, pos, at=at: (0, 0, shard_at(2 * i + at, pos[0], replicas)),
            )
            for at in (0, 1, pieces, pieces + 1)
        ]
        + [pl.BlockSpec((2 * shard, slots), lambda i, pos: (i, 0))] * 2
        + [whole((hidden, slots))] * 3,
        [whole((slots, 2 * hidden)), whole((2 * hidden, slots)), whole((1, slots))],
        [
            shape_of((slots, 2 * hidden)),
            shape_of((2 * hidden, slots)),
            shape_of((1, slots), F32),
        ],
        [w_down] * 4 + [far_t, near_t, act_t, for_gate, for_up],
        scratch=[pltpu.VMEM((hidden, slots), F32)],
    )
    far = run(
        functools.partial(grad_far_kernel, grad_scale),
        (2,),
        [pl.BlockSpec((width // 4, slots), lambda i, pos: (i, 0)), whole((slots, 2 * hidden))],
        [pl.BlockSpec((width // 4, hidden), lambda i, pos: (i, 0))] * 2,
        [shape_of((width // 2, hidden))] * 2,
        [x_t, delta],
    )
    others = [flip(part, "dp", 1) for part in far]
    low_send, low_keep, high_send, high_keep = grad_near(near_t, 0, act, [other])
    down_low, down_high = cross(low_send, high_send, 0)
    down_keep = low_keep, high_keep

    back_out = run(
        row_grad_kernel,
        (4,),
        [whole((2 * hidden, slots)), whole((1, slots))]
        + [pl.BlockSpec((1, width // 4, hidden), lambda i, pos: (0, i, 0)) for _ in range(2)],
        [whole((CAP, width + EXTRA)) for _ in range(experts)],
        [shape_of((CAP, width + EXTRA)) for _ in range(experts)],
        [delta_t, prob, w_gate, w_up],
    )
    back_in = exchange(back_out)

    low_send, low_keep, high_send, high_keep = grad_near(x_t, pieces // 2, delta, others)
    low, high = cross(low_send, high_send, 0)
    down_low, down_high = run(
        add_pairs_kernel,
        (1,),
        [whole(low_keep.shape[:1] + (half, hidden))] * 4,
        [whole(low_keep.shape[:1] + (half, hidden))] * 2,
        [shape_of(low_keep.shape[:1] + (half, hidden))] * 2,
        [down_keep[0], down_low, down_keep[1], down_high],
    )
    mark([], LONG)
    halves = [[down_low, low_keep, low], [down_high, high_keep, high]]
    for level in range(1, levels):
        count = pieces >> (level + 1)
        places = lambda i: 2 * i + 1, lambda i, count=count: count + i
        low, high = cross(*add(halves, level, count, places), level)
        if level + 1 < levels:
            halves[0].append(low)
            halves[1].append(high)
    mine = add(halves, levels, 1, (lambda i: i, lambda i: i))

    step = width // 2
    x_grad, prob_grad = run(
        functools.partial(combine_kernel, prob_scale),
        (2,),
        [whole((tok, slots)), whole(routes.shape), whole(gate_probs.shape)]
        + block_specs(step, lambda i, pos: (0, i))
        + block_specs(EXTRA, lambda i, pos: (0, width // EXTRA)),
        [pl.BlockSpec((tok, step), lambda i, pos: (0, i)), whole(gate_probs.shape)],
        [shape_of((tok, width)), shape_of(gate_probs.shape)],
        [place, routes, gate_probs, *back_in, *back_in],
        cost=LONG,
    )
    low_spec = pl.BlockSpec(
        (1, 3 * rows, hidden), lambda i, pos: (0, jnp.minimum(i, steps - 1), 0)
    )
    high_spec = pl.BlockSpec(
        (1, 3 * rows, hidden), lambda i, pos: (0, jnp.maximum(i - steps, 0), 0)
    )
    down_grad, gate_grad, up_grad = run(
        finish_kernel,
        (2 * steps,),
        [low_spec, low_spec, high_spec, high_spec],
        [pl.BlockSpec((hidden, rows), lambda i, pos: (0, i))]
        + [pl.BlockSpec((rows, hidden), lambda i, pos: (i, 0))] * 2,
        [shape_of((hidden, shard), F32)] + [shape_of((shard, hidden), F32)] * 2,
        [mine[0], low, mine[1], high],
    )
    return (x_grad, prob_grad.T, gate_grad[None], up_grad[None], down_grad[None])


def solution(mesh):
    return jax.shard_map(
        body,
        mesh=mesh,
        in_specs=(
            P(("dp", "expert"), None),
            P(("dp", "expert"), None),
            P(("dp", "expert"), None),
            P(("dp", "expert"), None),
            P("expert", None, None),
            P("expert", None, None),
            P("expert", None, None),
        ),
        out_specs=(
            P(("dp", "expert"), None),
            P(("dp", "expert"), None),
            P("expert", "dp", None),
            P("expert", "dp", None),
            P("expert", None, "dp"),
        ),
        check_vma=False,
    )
```

time: 217 us -> 198 us (0.912)
  the two profiles are of different devices: /device:TPU:0 before, /device:TPU:8 now
where the time goes in v3:
time: 198 us
  waiting for transfers between devices  129 us (65%)
  Pallas kernels  38.1 us (19%)
  starting transfers between devices  20.8 us (11%)
  local copies, waits for them, and re-layouts  8.92 us (5%)
    ppermute x18, waiting for transfers between devices, flip(): return lax.ppermute(x, axis, [(i, i ^ bit) for i in range(count)])  129 us
    pallas_call x16, Pallas kernels, call(): pl.pallas_call(ordered, grid_spec=pltpu.PrefetchScalarGridSpec(num_scalar...  38.1 us
    ppermute x18, starting transfers between devices, flip(): return lax.ppermute(x, axis, [(i, i ^ bit) for i in range(count)])  20.8 us
    unnamed x30, local copies, waits for them, and re-layouts  8.92 us
  transfers between devices with their start and end apart: 18, of which 9 were waited for; matrix products, arithmetic and copies ran while one was open for 0% of the time, Pallas kernels for 16%

profile of v3, /device:TPU:8, one launch (start us, length us, event | category | flops | bytes accessed | tf_op | source)
XLA Modules:
  0.0 197.6 jit_solution(4996366085980977618)
XLA Ops:
  0.7 1.3 copy-done.3
  2.7 1.3 shard_map.110
  4.1 3.0 %collective-permute-start.1 = (bf16[64,4096]{1,0:T(8,128)(2,1)S(1)}, bf16[64,4096]{1,0:T(8,128)(2,1)S(1)}, u32[]{:S(2)}, u32[]{:S(2)}) collective-permute-start(bf16[64,4096]{1,0:T(8,128)(2,1)S(1)} %get-tuple-element.68), channel_id=1, source_target_pairs={{0,2},{1,3},{2,0},{3,1},{4,6},{5,7},{6,4},{7,5},{8,10},{9,11},{10,... | collective-permute-start | bytes 1572872 | tf_op jit(solution)/shard_map/ppermute | solution.py:300
  7.6 18.4 %collective-permute-done.refs_5_.refs_2_ = bf16[64,4096]{1,0:T(8,128)(2,1)S(1)} collective-permute-done((bf16[64,4096]{1,0:T(8,128)(2,1)S(1)}, bf16[64,4096]{1,0:T(8,128)(2,1)S(1)}, u32[]{:S(2)}, u32[]{:S(2)}) %collective-permute-start) | collective-permute-done | bytes 524320 | tf_op jit(solution)/shard_map/ppermute | solution.py:300
  27.4 1.4 shard_map.111
  28.8 2.5 %collective-permute-start.3 = (bf16[64,4096]{1,0:T(8,128)(2,1)S(1)}, bf16[64,4096]{1,0:T(8,128)(2,1)S(1)}, u32[]{:S(2)}, u32[]{:S(2)}) collective-permute-start(bf16[64,4096]{1,0:T(8,128)(2,1)S(1)} %get-tuple-element.73), channel_id=1, source_target_pairs={{0,1},{1,0},{2,3},{3,2},{4,5},{5,4},{6,7},{7,6},{8,9},{9,8},{10,11... | collective-permute-start | bytes 1572872 | tf_op jit(solution)/shard_map/ppermute | solution.py:300
  31.3 1.8 collective-permute-start.4
  33.6 8.4 %collective-permute-done.1.refs_3_ = bf16[64,4096]{1,0:T(8,128)(2,1)S(1)} collective-permute-done((bf16[64,4096]{1,0:T(8,128)(2,1)S(1)}, bf16[64,4096]{1,0:T(8,128)(2,1)S(1)}, u32[]{:S(2)}, u32[]{:S(2)}) %collective-permute-start.1) | collective-permute-done | bytes 524320 | tf_op jit(solution)/shard_map/ppermute | solution.py:300
  42.0 34.6 %collective-permute-done.2.refs_4_ = bf16[64,4096]{1,0:T(8,128)(2,1)S(1)} collective-permute-done((bf16[64,4096]{1,0:T(8,128)(2,1)S(1)}, bf16[64,4096]{1,0:T(8,128)(2,1)S(1)}, u32[]{:S(2)}, u32[]{:S(2)}) %collective-permute-start.2) | collective-permute-done | bytes 524320 | tf_op jit(solution)/shard_map/ppermute | solution.py:300
  76.6 2.8 %copy-done = bf16[1,4096,768]{2,1,0:T(8,128)(2,1)S(1)} copy-done((bf16[1,4096,768]{2,1,0:T(8,128)(2,1)S(1)}, bf16[1,4096,768]{2,1,0:T(8,128)(2,1)}, u32[]{:S(2)}) %copy-start) | copy-done | bytes 6291480
  79.4 2.8 %copy-done.1 = bf16[1,4096,768]{2,1,0:T(8,128)(2,1)S(1)} copy-done((bf16[1,4096,768]{2,1,0:T(8,128)(2,1)S(1)}, bf16[1,4096,768]{2,1,0:T(8,128)(2,1)}, u32[]{:S(2)}) %copy-start.1) | copy-done | bytes 6291480
  82.2 6.0 %shard_map.112 = (bf16[256,768]{1,0:T(8,128)(2,1)S(1)}, bf16[768,256]{1,0:T(8,128)(2,1)S(1)}, f32[768,256]{1,0:T(8,128)S(1)}, f32[768,256]{1,0:T(8,128)S(1)}, f32[8,128]{1,0:T(8,128)S(1)}) custom-call(s32[2]{0:T(128)S(1)} %pad_add_fusion.refs_0_, bf16[64,4096]{1,0:T(8,128)(2,1)S(1)} %get-tuple-element.67.refs_1_, ...), custom_call_target="tpu_custom_call" | custom-call | flops 1 | bytes 1 | tf_op jit(solution)/shard_map/pallas_call | solution.py:35
  88.2 1.5 shard_map.113
  89.8 7.9 %collective-permute-done.5.refs_5_.refs_9_ = bf16[64,4096]{1,0:T(8,128)(2,1)S(1)} collective-permute-done((bf16[64,4096]{1,0:T(8,128)(2,1)S(1)}, bf16[64,4096]{1,0:T(8,128)(2,1)S(1)}, u32[]{:S(2)}, u32[]{:S(2)}) %collective-permute-start.5) | collective-permute-done | bytes 524320 | tf_op jit(solution)/shard_map/ppermute | solution.py:300
  97.7 2.0 %shard_map.114 = (bf16[2048,256]{1,0:T(8,128)(2,1)S(1)}, bf16[2048,256]{1,0:T(8,128)(2,1)S(1)}, bf16[2048,768]{1,0:T(8,128)(2,1)S(1)}, f32[8,128]{1,0:T(8,128)S(1)}) custom-call(s32[2]{0:T(128)S(1)} %pad_add_fusion.refs_0_, bf16[256,768]{1,0:T(8,128)(2,1)S(1)} %get-tuple-element.71.refs_1_.refs_2_, bf16[64,4096]{1,0:T(8,128)(2,1)S(1)} %get-tuple-element.72.refs_2_.refs_6_, ...), custom_call_target="tpu_custom_call" | custom-call | flops 1 | bytes 1 | tf_op jit(solution)/shard_map/pallas_call | solution.py:35
  99.9 3.7 %shard_map.115 = (bf16[256,1536]{1,0:T(8,128)(2,1)S(1)}, bf16[1536,256]{1,0:T(8,128)(2,1)S(1)}, f32[1,256]{1,0:T(1,128)S(1)}, f32[8,128]{1,0:T(8,128)S(1)}) custom-call(s32[2]{0:T(128)S(1)} %pad_add_fusion.refs_0_, bf16[1,768,4096]{2,1,0:T(8,128)(2,1)S(1)} %bitcast.9, bf16[1,768,4096]{2,1,0:T(8,128)(2,1)S(1)} %bitcast.9, bf16[1,768,4096]{2,1,0:T(8,128)(2,1)S(1)} %bitcast.9, ...), custom_call_target="tpu_custom_call" | custom-call | flops 1 | bytes 1 | tf_op jit(solution)/shard_map/pallas_call | solution.py:35
  103.6 2.5 %shard_map.116 = (bf16[2048,768]{1,0:T(8,128)(2,1)S(1)}, bf16[2048,768]{1,0:T(8,128)(2,1)S(1)}, f32[8,128]{1,0:T(8,128)S(1)}) custom-call(s32[2]{0:T(128)S(1)} %pad_add_fusion.refs_0_, bf16[4096,256]{1,0:T(8,128)(2,1)S(1)} %get-tuple-element.87.refs_1_, bf16[256,1536]{1,0:T(8,128)(2,1)S(1)} %get-tuple-element.88.refs_2_, f32[8,128]{1,0:T(8,128)S(1)} %get-tuple-element.89.refs_3_), custom_call_target="tpu_custom_call" | custom-call | flops 1 | bytes 1 | tf_op jit(solution)/shard_map/pallas_call | solution.py:35
  106.7 1.9 shard_map.117
  108.6 1.6 collective-permute-start.10
  110.2 1.5 collective-permute-start.11
  111.7 4.8 %shard_map.118 = (bf16[64,4224]{1,0:T(8,128)(2,1)S(1)}, bf16[64,4224]{1,0:T(8,128)(2,1)S(1)}, bf16[64,4224]{1,0:T(8,128)(2,1)S(1)}, bf16[64,4224]{1,0:T(8,128)(2,1)S(1)}, f32[8,128]{1,0:T(8,128)S(1)}) custom-call(s32[2]{0:T(128)S(1)} %pad_add_fusion.refs_0_, bf16[1536,256]{1,0:T(8,128)(2,1)S(1)} %get-tuple-element.84.refs_1_, ...), custom_call_target="tpu_custom_call" | custom-call | flops 1 | bytes 1 | tf_op jit(solution)/shard_map/pallas_call | solution.py:35
  116.7 3.0 %collective-permute-start.8 = (bf16[64,4224]{1,0:T(8,128)(2,1)S(1)}, bf16[64,4224]{1,0:T(8,128)(2,1)S(1)}, u32[]{:S(2)}, u32[]{:S(2)}) collective-permute-start(bf16[64,4224]{1,0:T(8,128)(2,1)S(1)} %get-tuple-element.94), channel_id=1, source_target_pairs={{0,2},{1,3},{2,0},{3,1},{4,6},{5,7},{6,4},{7,5},{8,10},{9,11},{10,... | collective-permute-start | bytes 1622024 | tf_op jit(solution)/shard_map/ppermute | solution.py:300
  120.1 3.7 %shard_map.119 = (bf16[2,512,768]{2,1,0:T(8,128)(2,1)S(1)}, bf16[2,512,768]{2,1,0:T(8,128)(2,1)S(1)}, bf16[2,512,768]{2,1,0:T(8,128)(2,1)S(1)}, bf16[2,512,768]{2,1,0:T(8,128)(2,1)S(1)}, f32[8,128]{1,0:T(8,128)S(1)}) custom-call(s32[2]{0:T(128)S(1)} %pad_add_fusion.refs_0_, bf16[4096,256]{1,0:T(8,128)(2,1)S(1)} %get-tuple-element.87.refs_1_, ...), custom_call_target="tpu_custom_call" | custom-call | flops 1 | bytes 1 | tf_op jit(solution)/shard_map/pallas_call | solution.py:35
  123.8 4.7 %collective-permute-done.10.refs_2_ = bf16[2,256,768]{2,1,0:T(8,128)(2,1)S(1)} collective-permute-done((bf16[2,256,768]{2,1,0:T(8,128)(2,1)S(1)}, bf16[2,256,768]{2,1,0:T(8,128)(2,1)S(1)}, u32[]{:S(2)}, u32[]{:S(2)}) %collective-permute-start.10) | collective-permute-done | bytes 786464 | tf_op jit(solution)/shard_map/ppermute | solution.py:300
  128.6 1.5 collective-permute-start.14
  130.1 1.5 collective-permute-start.15
  133.1 31.5 %collective-permute-done.14.refs_3_.refs_5_ = bf16[2,512,768]{2,1,0:T(8,128)(2,1)S(1)} collective-permute-done((bf16[2,512,768]{2,1,0:T(8,128)(2,1)S(1)}, bf16[2,512,768]{2,1,0:T(8,128)(2,1)S(1)}, u32[]{:S(2)}, u32[]{:S(2)}) %collective-permute-start.14) | collective-permute-done | bytes 1572896 | tf_op jit(solution)/shard_map/ppermute | solution.py:300
  166.7 1.6 collective-permute-start.16
  169.8 2.6 %shard_map.124 = (bf16[128,4096]{1,0:T(8,128)(2,1)}, bf16[2,128]{1,0:T(2,128)(2,1)}, f32[8,128]{1,0:T(8,128)S(1)}) custom-call(s32[2]{0:T(128)S(1)} %pad_add_fusion.refs_0_, bf16[128,256]{1,0:T(8,128)(2,1)S(1)} %get-tuple-element.66.refs_1_, s32[2,128]{1,0:T(2,128)S(1)} %bitcast.16, bf16[2,128]{1,0:T(2,128)(2,1)S(1)} %bitcast.18, ...), custom_call_target="tpu_custom_call" | custom-call | flops 60000002048 | bytes 1 | tf_op jit(solution)/shard_map/pallas_call | solution.py:35
  172.5 20.6 %collective-permute-done.16.refs_2_ = bf16[1,768,768]{2,1,0:T(8,128)(2,1)S(1)} collective-permute-done((bf16[1,768,768]{2,1,0:T(8,128)(2,1)S(1)}, bf16[1,768,768]{2,1,0:T(8,128)(2,1)S(1)}, u32[]{:S(2)}, u32[]{:S(2)}) %collective-permute-start.16) | collective-permute-done | bytes 1179680 | tf_op jit(solution)/shard_map/ppermute | solution.py:300
  193.1 1.2 collective-permute-done.17.refs_4_
  194.4 3.2 %shard_map.125 = (f32[768,512]{1,0:T(8,128)}, f32[512,768]{1,0:T(8,128)}, f32[512,768]{1,0:T(8,128)}, f32[8,128]{1,0:T(8,128)}) custom-call(s32[2]{0:T(128)S(1)} %pad_add_fusion.refs_0_, bf16[1,768,768]{2,1,0:T(8,128)(2,1)S(1)} %get-tuple-element.115.refs_1_, bf16[1,768,768]{2,1,0:T(8,128)(2,1)S(1)} %collective-permute-done.16.refs_2_, ...), custom_call_target="tpu_custom_call" | custom-call | flops 1 | bytes 1 | tf_op jit(solution)/shard_map/pallas_call | solution.py:35
  (54 shorter events, 9.5 us)
Async XLA Ops:
  0.6 25.4 %copy-start.2 = (bf16[128,4096]{1,0:T(8,128)(2,1)S(1)}, bf16[128,4096]{1,0:T(8,128)(2,1)}, u32[]{:S(2)}) copy-start(bf16[128,4096]{1,0:T(8,128)(2,1)} %refs_3_.3) | copy-start | bytes 3145732
  0.7 1.3 copy-start.3
  2.0 0.7 copy-start.4
  4.0 22.0 %collective-permute-start = (bf16[64,4096]{1,0:T(8,128)(2,1)S(1)}, bf16[64,4096]{1,0:T(8,128)(2,1)S(1)}, u32[]{:S(2)}, u32[]{:S(2)}) collective-permute-start(bf16[64,4096]{1,0:T(8,128)(2,1)S(1)} %get-tuple-element.65), channel_id=1, source_target_pairs={{0,1},{1,0},{2,3},{3,2},{4,5},{5,4},{6,7},{7,6},{8,9},{9,8},{10,11... | collective-permute-start | bytes 1572872 | tf_op jit(solution)/shard_map/ppermute | solution.py:300
  4.1 37.9 %collective-permute-start.1 = (bf16[64,4096]{1,0:T(8,128)(2,1)S(1)}, bf16[64,4096]{1,0:T(8,128)(2,1)S(1)}, u32[]{:S(2)}, u32[]{:S(2)}) collective-permute-start(bf16[64,4096]{1,0:T(8,128)(2,1)S(1)} %get-tuple-element.68), channel_id=1, source_target_pairs={{0,2},{1,3},{2,0},{3,1},{4,6},{5,7},{6,4},{7,5},{8,10},{9,11},{10,... | collective-permute-start | bytes 1572872 | tf_op jit(solution)/shard_map/ppermute | solution.py:300
  7.2 69.5 %collective-permute-start.2 = (bf16[64,4096]{1,0:T(8,128)(2,1)S(1)}, bf16[64,4096]{1,0:T(8,128)(2,1)S(1)}, u32[]{:S(2)}, u32[]{:S(2)}) collective-permute-start(bf16[64,4096]{1,0:T(8,128)(2,1)S(1)} %get-tuple-element.69), channel_id=1, source_target_pairs={{0,3},{1,2},{2,1},{3,0},{4,7},{5,6},{6,5},{7,4},{8,11},{9,10},{10,... | collective-permute-start | bytes 1572872 | tf_op jit(solution)/shard_map/ppermute | solution.py:300
  26.1 0.7 copy-start.5
  27.4 72.4 %slice-start = ((s8[6291456]{0:T(1024)(128)(4,1)}), s8[4194304]{0:T(1024)(128)(4,1)S(1)}, s32[]{:S(2)}) async-start(s8[6291456]{0:T(1024)(128)(4,1)} %bitcast.8), calls=%async_computation | async-start | bytes 8388608
  28.8 61.0 %collective-permute-start.3 = (bf16[64,4096]{1,0:T(8,128)(2,1)S(1)}, bf16[64,4096]{1,0:T(8,128)(2,1)S(1)}, u32[]{:S(2)}, u32[]{:S(2)}) collective-permute-start(bf16[64,4096]{1,0:T(8,128)(2,1)S(1)} %get-tuple-element.73), channel_id=1, source_target_pairs={{0,1},{1,0},{2,3},{3,2},{4,5},{5,4},{6,7},{7,6},{8,9},{9,8},{10,11... | collective-permute-start | bytes 1572872 | tf_op jit(solution)/shard_map/ppermute | solution.py:300
  31.3 58.5 %collective-permute-start.4 = (bf16[64,4096]{1,0:T(8,128)(2,1)S(1)}, bf16[64,4096]{1,0:T(8,128)(2,1)S(1)}, u32[]{:S(2)}, u32[]{:S(2)}) collective-permute-start(bf16[64,4096]{1,0:T(8,128)(2,1)S(1)} %get-tuple-element.74), channel_id=1, source_target_pairs={{0,2},{1,3},{2,0},{3,1},{4,6},{5,7},{6,4},{7,5},{8,10},{9,11},{10,... | collective-permute-start | bytes 1572872 | tf_op jit(solution)/shard_map/ppermute | solution.py:300
  33.1 64.6 %collective-permute-start.5 = (bf16[64,4096]{1,0:T(8,128)(2,1)S(1)}, bf16[64,4096]{1,0:T(8,128)(2,1)S(1)}, u32[]{:S(2)}, u32[]{:S(2)}) collective-permute-start(bf16[64,4096]{1,0:T(8,128)(2,1)S(1)} %get-tuple-element.75), channel_id=1, source_target_pairs={{0,3},{1,2},{2,1},{3,0},{4,7},{5,6},{6,5},{7,4},{8,11},{9,10},{10,... | collective-permute-start | bytes 1572872 | tf_op jit(solution)/shard_map/ppermute | solution.py:300
  76.6 2.8 %copy-start = (bf16[1,4096,768]{2,1,0:T(8,128)(2,1)S(1)}, bf16[1,4096,768]{2,1,0:T(8,128)(2,1)}, u32[]{:S(2)}) copy-start(bf16[1,4096,768]{2,1,0:T(8,128)(2,1)} %refs_3_.5) | copy-start | bytes 18874372
  79.4 2.8 %copy-start.1 = (bf16[1,4096,768]{2,1,0:T(8,128)(2,1)S(1)}, bf16[1,4096,768]{2,1,0:T(8,128)(2,1)}, u32[]{:S(2)}) copy-start(bf16[1,4096,768]{2,1,0:T(8,128)(2,1)} %refs_4_.3) | copy-start | bytes 18874372
  82.2 17.6 %slice-start.1 = ((s8[6291456]{0:T(1024)(128)(4,1)}), s8[2097152]{0:T(1024)(128)(4,1)S(1)}, s32[]{:S(2)}) async-start(s8[6291456]{0:T(1024)(128)(4,1)} %bitcast.8), calls=%async_computation.1 | async-start | bytes 4194304
  97.7 14.0 %slice-start.2 = ((s8[6291456]{0:T(1024)(128)(4,1)}), s8[4194304]{0:T(1024)(128)(4,1)S(1)}, s32[]{:S(2)}) async-start(s8[6291456]{0:T(1024)(128)(4,1)} %bitcast.10), calls=%async_computation.2 | async-start | bytes 8388608
  97.7 14.0 %slice-start.4 = ((s8[6291456]{0:T(1024)(128)(4,1)}), s8[4194304]{0:T(1024)(128)(4,1)S(1)}, s32[]{:S(2)}) async-start(s8[6291456]{0:T(1024)(128)(4,1)} %bitcast.12), calls=%async_computation.4 | async-start | bytes 8388608
  99.7 7.0 %collective-permute-start.6 = (bf16[2048,768]{1,0:T(8,128)(2,1)S(1)}, bf16[2048,768]{1,0:T(8,128)(2,1)S(1)}, u32[]{:S(2)}, u32[]{:S(2)}) collective-permute-start(bf16[2048,768]{1,0:T(8,128)(2,1)S(1)} %get-tuple-element.86), channel_id=1, source_target_pairs={{0,4},{4,0},{8,12},{12,8},{16,20},{20,16},{24,28},{28,24},{1,5},{5... | collective-permute-start | bytes 9437192 | tf_op jit(solution)/shard_map/ppermute | solution.py:300
  99.9 11.9 %slice-start.3 = ((s8[6291456]{0:T(1024)(128)(4,1)}), s8[2097152]{0:T(1024)(128)(4,1)S(1)}, s32[]{:S(2)}) async-start(s8[6291456]{0:T(1024)(128)(4,1)} %bitcast.10), calls=%async_computation.3 | async-start | bytes 4194304
  99.9 11.9 %slice-start.5 = ((s8[6291456]{0:T(1024)(128)(4,1)}), s8[2097152]{0:T(1024)(128)(4,1)S(1)}, s32[]{:S(2)}) async-start(s8[6291456]{0:T(1024)(128)(4,1)} %bitcast.12), calls=%async_computation.5 | async-start | bytes 4194304
  106.1 10.6 %collective-permute-start.12 = (bf16[2048,768]{1,0:T(8,128)(2,1)S(1)}, bf16[2048,768]{1,0:T(8,128)(2,1)S(1)}, u32[]{:S(2)}, u32[]{:S(2)}) collective-permute-start(bf16[2048,768]{1,0:T(8,128)(2,1)S(1)} %get-tuple-element.100), channel_id=1, source_target_pairs={{0,4},{4,0},{8,12},{12,8},{16,20},{20,16},{24,28},{28,24},{1,5},{5... | collective-permute-start | bytes 9437192 | tf_op jit(solution)/shard_map/ppermute | solution.py:300
  106.6 13.0 %collective-permute-start.13 = (bf16[2048,768]{1,0:T(8,128)(2,1)S(1)}, bf16[2048,768]{1,0:T(8,128)(2,1)S(1)}, u32[]{:S(2)}, u32[]{:S(2)}) collective-permute-start(bf16[2048,768]{1,0:T(8,128)(2,1)S(1)} %get-tuple-element.101), channel_id=1, source_target_pairs={{0,4},{4,0},{8,12},{12,8},{16,20},{20,16},{24,28},{28,24},{1,5},{5... | collective-permute-start | bytes 9437192 | tf_op jit(solution)/shard_map/ppermute | solution.py:300
  108.6 20.0 %collective-permute-start.10 = (bf16[2,256,768]{2,1,0:T(8,128)(2,1)S(1)}, bf16[2,256,768]{2,1,0:T(8,128)(2,1)S(1)}, u32[]{:S(2)}, u32[]{:S(2)}) collective-permute-start(bf16[2,256,768]{2,1,0:T(8,128)(2,1)S(1)} %get-tuple-element.97), channel_id=1, source_target_pairs={{0,8},{4,12},{8,0},{12,4},{16,24},{20,28},{24,16},{28,20},{1,9},{5... | collective-permute-start | bytes 2359304 | tf_op jit(solution)/shard_map/ppermute | solution.py:300
  110.2 19.9 %collective-permute-start.11 = (bf16[2,256,768]{2,1,0:T(8,128)(2,1)S(1)}, bf16[2,256,768]{2,1,0:T(8,128)(2,1)S(1)}, u32[]{:S(2)}, u32[]{:S(2)}) collective-permute-start(bf16[2,256,768]{2,1,0:T(8,128)(2,1)S(1)} %get-tuple-element.99), channel_id=1, source_target_pairs={{0,16},{4,20},{8,24},{12,28},{16,0},{20,4},{24,8},{28,12},{1,17},{... | collective-permute-start | bytes 2359304 | tf_op jit(solution)/shard_map/ppermute | solution.py:300
  116.6 53.2 %collective-permute-start.7 = (bf16[64,4224]{1,0:T(8,128)(2,1)S(1)}, bf16[64,4224]{1,0:T(8,128)(2,1)S(1)}, u32[]{:S(2)}, u32[]{:S(2)}) collective-permute-start(bf16[64,4224]{1,0:T(8,128)(2,1)S(1)} %get-tuple-element.93), channel_id=1, source_target_pairs={{0,1},{1,0},{2,3},{3,2},{4,5},{5,4},{6,7},{7,6},{8,9},{9,8},{10,11... | collective-permute-start | bytes 1622024 | tf_op jit(solution)/shard_map/ppermute | solution.py:300
  116.7 53.1 %collective-permute-start.8 = (bf16[64,4224]{1,0:T(8,128)(2,1)S(1)}, bf16[64,4224]{1,0:T(8,128)(2,1)S(1)}, u32[]{:S(2)}, u32[]{:S(2)}) collective-permute-start(bf16[64,4224]{1,0:T(8,128)(2,1)S(1)} %get-tuple-element.94), channel_id=1, source_target_pairs={{0,2},{1,3},{2,0},{3,1},{4,6},{5,7},{6,4},{7,5},{8,10},{9,11},{10,... | collective-permute-start | bytes 1622024 | tf_op jit(solution)/shard_map/ppermute | solution.py:300
  119.7 50.2 %collective-permute-start.9 = (bf16[64,4224]{1,0:T(8,128)(2,1)S(1)}, bf16[64,4224]{1,0:T(8,128)(2,1)S(1)}, u32[]{:S(2)}, u32[]{:S(2)}) collective-permute-start(bf16[64,4224]{1,0:T(8,128)(2,1)S(1)} %get-tuple-element.95), channel_id=1, source_target_pairs={{0,3},{1,2},{2,1},{3,0},{4,7},{5,6},{6,5},{7,4},{8,11},{9,10},{10,... | collective-permute-start | bytes 1622024 | tf_op jit(solution)/shard_map/ppermute | solution.py:300
  128.6 36.0 %collective-permute-start.14 = (bf16[2,512,768]{2,1,0:T(8,128)(2,1)S(1)}, bf16[2,512,768]{2,1,0:T(8,128)(2,1)S(1)}, u32[]{:S(2)}, u32[]{:S(2)}) collective-permute-start(bf16[2,512,768]{2,1,0:T(8,128)(2,1)S(1)} %get-tuple-element.106), channel_id=1, source_target_pairs={{0,8},{4,12},{8,0},{12,4},{16,24},{20,28},{24,16},{28,20},{1,9},{5... | collective-permute-start | bytes 4718600 | tf_op jit(solution)/shard_map/ppermute | solution.py:300
  130.1 35.7 %collective-permute-start.15 = (bf16[2,512,768]{2,1,0:T(8,128)(2,1)S(1)}, bf16[2,512,768]{2,1,0:T(8,128)(2,1)S(1)}, u32[]{:S(2)}, u32[]{:S(2)}) collective-permute-start(bf16[2,512,768]{2,1,0:T(8,128)(2,1)S(1)} %get-tuple-element.109), channel_id=1, source_target_pairs={{0,16},{4,20},{8,24},{12,28},{16,0},{20,4},{24,8},{28,12},{1,17},{... | collective-permute-start | bytes 4718600 | tf_op jit(solution)/shard_map/ppermute | solution.py:300
  166.7 26.4 %collective-permute-start.16 = (bf16[1,768,768]{2,1,0:T(8,128)(2,1)S(1)}, bf16[1,768,768]{2,1,0:T(8,128)(2,1)S(1)}, u32[]{:S(2)}, u32[]{:S(2)}) collective-permute-start(bf16[1,768,768]{2,1,0:T(8,128)(2,1)S(1)} %get-tuple-element.116), channel_id=1, source_target_pairs={{0,16},{4,20},{8,24},{12,28},{16,0},{20,4},{24,8},{28,12},{1,17},{... | collective-permute-start | bytes 3538952 | tf_op jit(solution)/shard_map/ppermute | solution.py:300
  168.3 26.1 %collective-permute-start.17 = (bf16[1,768,768]{2,1,0:T(8,128)(2,1)S(1)}, bf16[1,768,768]{2,1,0:T(8,128)(2,1)S(1)}, u32[]{:S(2)}, u32[]{:S(2)}) collective-permute-start(bf16[1,768,768]{2,1,0:T(8,128)(2,1)S(1)} %get-tuple-element.118), channel_id=1, source_target_pairs={{0,8},{4,12},{8,0},{12,4},{16,24},{20,28},{24,16},{28,20},{1,9},{5... | collective-permute-start | bytes 3538952 | tf_op jit(solution)/shard_map/ppermute | solution.py:300
  168.8 1.0 copy-start.6
  168.8 1.0 copy-start.8
  (1 other events, 0.7 us)

commit v4 on v3

v4 whole, which is shorter than its diff:
```python
import functools
import math

import jax
import jax.numpy as jnp
from jax import lax
from jax.experimental import pallas as pl
from jax.experimental.pallas import tpu as pltpu
from jax.sharding import PartitionSpec as P

CAP = 64
FIRST = 128
EXTRA = 128
F32 = jnp.float32
BF16 = jnp.bfloat16
LONG = 6 * 10**10
VMEM_SPARE = 4 * 1024 * 1024


IN_VMEM = pl.BlockSpec(memory_space=pltpu.VMEM)


def whole(shape):
    return pl.BlockSpec(shape, lambda i, pos: (0,) * len(shape))


def call(kernel, grid, in_specs, out_specs, out_shape, pos, args, after, scratch=(), cost=1):
    held = sum(math.prod(ref.shape) * ref.dtype.itemsize for ref in scratch)
    for spec, array in zip([*in_specs, *out_specs], [*args, *out_shape]):
        if spec.block_shape is not None:
            held += 2 * math.prod(spec.block_shape) * array.dtype.itemsize
    first, count, last = 1 + len(args), len(after), len(out_shape)

    def ordered(*refs):
        outs = refs[first + count :]
        kernel(*refs[:first], *outs[:last], *outs[last + 1 :])
        outs[last][...] = jnp.zeros(outs[last].shape, F32)

    return pl.pallas_call(
        ordered,
        grid_spec=pltpu.PrefetchScalarGridSpec(
            num_scalar_prefetch=1,
            grid=grid,
            in_specs=list(in_specs) + [pl.BlockSpec(memory_space=pl.ANY)] * count,
            out_specs=[*out_specs, whole((8, 128))],
            scratch_shapes=list(scratch),
        ),
        out_shape=[*out_shape, shape_of((8, 128), F32)],
        compiler_params=pltpu.CompilerParams(vmem_limit_bytes=held + VMEM_SPARE),
        cost_estimate=pl.CostEstimate(flops=cost, bytes_accessed=1, transcendentals=0),
    )(pos, *args, *after)


def shape_of(shape, dtype=BF16):
    return jax.ShapeDtypeStruct(shape, dtype)


def dot(left, right):
    return jnp.dot(left, right, preferred_element_type=F32)


def shard_rows(relative, pos_ref, size):
    return pl.ds(pl.multiple_of((pos_ref[0] ^ relative) * size, size), size)


def slot_matrix(routes_ref, my_expert, slots):
    top, tok = routes_ref.shape
    index = lax.broadcasted_iota(jnp.int32, (slots, tok), 0)
    block = index // CAP
    expert = jnp.where(block == 0, 0, slots // CAP - block) ^ my_expert
    hit = jnp.zeros((slots, tok), jnp.bool_)
    for k in range(top):
        hit = hit | (routes_ref[k : k + 1, :] == expert)
    named = jnp.where(hit, 1.0, 0.0)
    before = lax.broadcasted_iota(jnp.int32, (tok, tok), 0) < lax.broadcasted_iota(
        jnp.int32, (tok, tok), 1
    )
    rank = dot(named.astype(BF16), jnp.where(before, 1.0, 0.0).astype(BF16))
    return jnp.where(rank == (index % CAP).astype(F32), named, 0.0), expert


def send_rows(place, ref, start, shard, outs):
    size = outs[0].shape[1] * shard // ref.shape[1]
    for i in range(ref.shape[1] // shard):
        rows = dot(place, ref[:, i * shard + start : i * shard + start + size]).astype(BF16)
        for j, out_ref in enumerate(outs):
            out_ref[:, i * size : (i + 1) * size] = rows[j * CAP : (j + 1) * CAP]


def send_tokens_kernel(shard, pos_ref, routes_ref, tok_ref, *outs):
    place, _ = slot_matrix(routes_ref, pos_ref[1], len(outs) * CAP)
    send_rows(place.astype(BF16), tok_ref, 0, shard, outs)


def send_cot_kernel(experts, shard, start, pos_ref, routes_ref, probs_ref, cot_ref, *rest):
    outs, place_t_ref = rest[:experts], rest[experts:]
    place, expert = slot_matrix(routes_ref, pos_ref[1], experts * CAP)
    probs = probs_ref[...].astype(F32)
    weight = jnp.zeros_like(place)
    for k in range(routes_ref.shape[0]):
        weight += jnp.where(routes_ref[k : k + 1, :] == expert, probs[k : k + 1, :], 0.0)
    send_rows((place * weight).astype(BF16), cot_ref, start, shard, outs)
    if place_t_ref:
        place_t_ref[0][...] = place.T.astype(BF16)


def joined(refs):
    return jnp.concatenate([ref[...] for ref in refs], axis=0)


def forward_kernel(experts, blocks, pos_ref, *rest):
    xs, (wg_ref, wu_ref), outs, x_ref = (
        rest[:experts],
        rest[experts : experts + 2],
        rest[experts + 2 : -1],
        rest[-1],
    )
    act_ref, act_t_ref, for_gate_ref, for_up_ref = outs
    for j in range(experts):
        x_ref[j * CAP : (j + 1) * CAP, :] = xs[j][...]
    size = wg_ref.shape[2] // blocks
    for i in range(blocks):
        at = slice(i * size, (i + 1) * size)
        gate = dot(x_ref[...], wg_ref[0, :, at]).T
        up = dot(x_ref[...], wu_ref[0, :, at]).T
        sig = jax.nn.sigmoid(gate)
        silu = gate * sig
        act = (silu * up).astype(BF16)
        act_ref[:, at] = act.T
        act_t_ref[at] = act
        for_gate_ref[at] = up * sig * (1.0 + gate * (1.0 - sig))
        for_up_ref[at] = silu


def transpose_kernel(pos_ref, *rest):
    ins, out_ref = rest[:-1], rest[-1]
    size = 512
    for at in range(0, out_ref.shape[0], size):
        rows = [ref[:, at : at + size] for ref in ins]
        out_ref[at : at + size] = jnp.concatenate(rows, axis=0).T


def grad_far_kernel(scale, replicas, pos_ref, rows_ref, right_ref, *outs):
    size = rows_ref.shape[0] // replicas
    cols = outs[0].shape[1]
    for i in range(replicas // 2):
        rows = rows_ref[shard_rows(2 * i + 1, pos_ref, size), :]
        part = (dot(rows, right_ref[...]) * scale).astype(BF16)
        for at, out_ref in enumerate(outs):
            out_ref[i * size : (i + 1) * size] = part[:, at * cols : (at + 1) * cols]


def grad_near_kernel(scale, replicas, pos_ref, rows_ref, right_ref, *rest):
    others, (low_send, low_keep, high_send, high_keep) = rest[:-4], rest[-4:]
    size = rows_ref.shape[0] // replicas
    cols = low_keep.shape[2]
    half, count = size // 2, replicas // 4
    for q in range(replicas // 2):
        rows = rows_ref[shard_rows(2 * q, pos_ref, size), :]
        low_ref = low_send if q % 2 else low_keep
        high_ref, place = (high_send, q - count) if q >= count else (high_keep, q)
        came = [ref[q * size : (q + 1) * size] for ref in others]
        came = jnp.concatenate(came, axis=1).astype(F32)
        total = (dot(rows, right_ref[...]) * scale + came).astype(BF16)
        for at in range(total.shape[1] // cols):
            part = total[:, at * cols : (at + 1) * cols]
            low_ref[q // 2, at * half : (at + 1) * half] = part[:half]
            high_ref[place, at * half : (at + 1) * half] = part[half:]


def back_sum(wd_ref, rows_ref, start, shard):
    count = wd_ref.shape[2] // shard
    size = rows_ref.shape[0] // count
    return sum(
        dot(
            wd_ref[0, :, i * shard + start : i * shard + start + size],
            rows_ref[i * size : (i + 1) * size],
        )
        for i in range(count)
    )


def back_first_kernel(shard, pos_ref, wd_ref, rows_ref, out_ref):
    out_ref[...] = back_sum(wd_ref, rows_ref, 0, shard)


def back_hidden_kernel(
    shard,
    pos_ref,
    prev_ref,
    wd_ref,
    rows_ref,
    act_ref,
    for_gate_ref,
    for_up_ref,
    delta_ref,
    delta_t_ref,
    prob_ref,
):
    back = prev_ref[...] + back_sum(wd_ref, rows_ref, FIRST, shard)
    dh = (back * for_gate_ref[...]).astype(BF16)
    du = (back * for_up_ref[...]).astype(BF16)
    hidden = back.shape[0]
    delta_t_ref[:hidden] = dh
    delta_t_ref[hidden:] = du
    delta_ref[:, :hidden] = dh.T
    delta_ref[:, hidden:] = du.T
    prob_ref[...] = jnp.sum(act_ref[...].astype(F32) * back, axis=0, keepdims=True)


def row_grad_kernel(pos_ref, delta_t_ref, prob_ref, wg_ref, wu_ref, *outs):
    width, hidden = wg_ref.shape[1:]
    size = 512
    for start in range(0, width, size):
        at = slice(start, start + size)
        rows_t = dot(wg_ref[0, at], delta_t_ref[:hidden]) + dot(wu_ref[0, at], delta_t_ref[hidden:])
        rows = rows_t.astype(BF16).T
        for j, out_ref in enumerate(outs):
            out_ref[:, at] = rows[j * CAP : (j + 1) * CAP]
    full = prob_ref[...]
    high = full.astype(BF16).astype(F32)
    lane = lax.broadcasted_iota(jnp.int32, (EXTRA, full.shape[1]), 0)
    both = jnp.where(lane == 0, high, jnp.where(lane == 1, full - high, 0.0)).T.astype(BF16)
    for j, out_ref in enumerate(outs):
        out_ref[:, width:] = both[j * CAP : (j + 1) * CAP]


def total_of(refs):
    down, *rest = [ref[0].astype(F32) for ref in refs]
    first = [down, rest[0] + rest[1], rest[2] + rest[3]]
    return sum(rest[4:], jnp.concatenate(first, axis=0))


def add_kernel(pos_ref, *rest):
    ins, outs = rest[:-2], rest[-2:]
    middle = len(ins) // 2
    for refs, out_ref in zip((ins[:middle], ins[middle:]), outs):
        out_ref[0] = total_of(refs).astype(BF16)


def add_pairs_kernel(pos_ref, a_ref, b_ref, c_ref, d_ref, low_ref, high_ref):
    low_ref[...] = (a_ref[...].astype(F32) + b_ref[...].astype(F32)).astype(BF16)
    high_ref[...] = (c_ref[...].astype(F32) + d_ref[...].astype(F32)).astype(BF16)


def add_all_kernel(pos_ref, *rest):
    ins, outs = rest[:-2], rest[-2:]
    middle = len(ins) // 2
    for refs, out_ref in zip((ins[:middle], ins[middle:]), outs):
        out_ref[...] = sum(ref[...].astype(F32) for ref in refs).astype(BF16)


def finish_first_kernel(pos_ref, *rest):
    ins, out_ref = rest[:-1], rest[-1]
    middle, half = len(ins) // 2, out_ref.shape[0] // 2
    out_ref[:half] = sum(ref[0].astype(F32) for ref in ins[:middle])
    out_ref[half:] = sum(ref[0].astype(F32) for ref in ins[middle:])


def combine_kernel(scale, pos_ref, place_ref, routes_ref, probs_ref, *rest):
    experts = (len(rest) - 2) // 2
    x_ref, prob_ref = rest[2 * experts :]
    rows = joined(rest[:experts])
    x_ref[...] = dot(place_ref[...], rows).astype(BF16)

    @pl.when(pl.program_id(0) == 0)
    def _():
        extra = joined(rest[experts : 2 * experts])
        tok, slots = place_ref.shape
        top = routes_ref.shape[0]
        place, expert = slot_matrix(routes_ref, pos_ref[1], slots)
        value = jnp.sum(extra.astype(F32), axis=1, keepdims=True)
        probs = probs_ref[...].astype(F32)
        line = lax.broadcasted_iota(jnp.int32, probs.shape, 0)
        result = jnp.zeros(probs.shape, F32)
        for k in range(top):
            mine = jnp.where(routes_ref[k : k + 1, :] == expert, place, 0.0)
            found = jnp.sum(mine * value, axis=0, keepdims=True)
            result += jnp.where(line == k, found, 0.0)
        prob_ref[...] = (result * scale / probs).astype(BF16)


def finish_kernel(
    pos_ref, first_ref, low_ref, low_last_ref, high_ref, high_last_ref, down_ref, gate_ref, up_ref
):
    rows = gate_ref.shape[0]
    down_rows = low_ref.shape[1] - 2 * rows
    early = down_ref.shape[1] - FIRST

    def total(ref, last_ref, start, stop):
        return ref[0, start:stop].astype(F32) + last_ref[0, start:stop].astype(F32)

    def write(ref, last_ref):
        gate_ref[...] = total(ref, last_ref, down_rows, down_rows + rows)
        up_ref[...] = total(ref, last_ref, down_rows + rows, down_rows + 2 * rows)

    @pl.when(pl.program_id(0) == 0)
    def _():
        down_ref[:, :FIRST] = first_ref[...].T
        if early:
            down_ref[:, FIRST:] = total(low_ref, low_last_ref, 0, early).T
        write(low_ref, low_last_ref)

    @pl.when(pl.program_id(0) == 1)
    def _():
        down_ref[:, : down_rows - early] = total(low_ref, low_last_ref, early, down_rows).T
        down_ref[:, down_rows - early :] = total(high_ref, high_last_ref, 0, down_rows).T
        write(high_ref, high_last_ref)


def flip(x, axis, bit):
    count = lax.axis_size(axis)
    return lax.ppermute(x, axis, [(i, i ^ bit) for i in range(count)])


def body(tokens, out_grad, routes, gate_probs, w_gate, w_up, w_down):
    tok, width = tokens.shape
    experts = lax.axis_size("expert")
    replicas = lax.axis_size("dp")
    hidden = w_gate.shape[2]
    slots = experts * CAP
    shard = width // replicas
    pieces = replicas // 2
    levels = pieces.bit_length() - 1
    grad_scale = 1.0 / math.sqrt(tok * replicas * experts)
    prob_scale = 1.0 / math.sqrt(width)
    pos = jnp.stack([lax.axis_index("dp"), lax.axis_index("expert")]).astype(jnp.int32)
    chain = []

    def run(kernel, grid, in_specs, out_specs, out_shape, args, after=(), **kw):
        out = call(
            kernel, grid, in_specs, out_specs, out_shape, pos, args, [*chain[-1:], *after], **kw
        )
        chain.append(out[-1])
        return out[:-1]

    def exchange(blocks):
        return [blocks[0]] + [flip(blocks[j], "expert", experts - j) for j in range(1, experts)]

    def block_specs(cols, at):
        return [pl.BlockSpec((CAP, cols), at) for _ in range(experts)]

    def cross(low, high, level):
        return flip(low, "dp", 2 << level), flip(high, "dp", 2 << (levels - 1 - level))

    half = shard // 2
    merged = (shard - FIRST) // 2 + 2 * half

    def add(halves, level, count, places):
        specs, arrays = [], []
        for high, (down, keep, came, *later) in enumerate(halves):

            def spec(size, first, behind, high=high):
                shift = 0 if high else behind
                return pl.BlockSpec(
                    (1, size, hidden),
                    lambda i, pos: (places[high](i) << shift, first, 0),
                )

            specs += [spec(down.shape[1], 0, level - 1)]
            specs += [spec(half, at, level - 1) for at in (0, 0, 1, 1)]
            arrays += [down, keep, came, keep, came]
            for at, array in enumerate(later):
                specs.append(spec(array.shape[1], 0, level - 2 - at))
                arrays.append(array)
        return run(
            add_kernel,
            (count,),
            specs,
            [pl.BlockSpec((1, merged, hidden), lambda i, pos: (i, 0, 0))] * 2,
            [shape_of((count, merged, hidden))] * 2,
            arrays,
        )

    def add_first(low_state, high_state, level):
        count = pieces >> (level + 1)
        places = lambda i: 2 * i + 1, lambda i: count + i
        specs = []
        for high, state in enumerate((low_state, high_state)):
            for at, array in enumerate(state):
                shift = 0 if high else level - 1 - max(at - 1, 0)
                specs.append(
                    pl.BlockSpec(
                        (1, *array.shape[1:]),
                        lambda i, pos, high=high, shift=shift: (places[high](i) << shift, 0, 0),
                    )
                )
        block = (1, FIRST // 2, hidden)
        return run(
            add_all_kernel,
            (count,),
            specs,
            [pl.BlockSpec(block, lambda i, pos: (i, 0, 0))] * 2,
            [shape_of((count, *block[1:]))] * 2,
            low_state + high_state,
        )

    def mark(after, cost):
        run(lambda pos_ref: None, (1,), [], [], [], [], after, cost=cost)

    blocks = [whole((CAP, width)) for _ in range(experts)]
    routes, gate_probs = routes.T, gate_probs.T
    x_out = run(
        functools.partial(send_tokens_kernel, shard),
        (1,),
        [whole(routes.shape), whole(tokens.shape)],
        [IN_VMEM] * experts,
        [shape_of((CAP, width))] * experts,
        [routes, tokens],
    )
    x_in = exchange(x_out)

    mark([], LONG)

    def send_cot(start, size, after):
        cols = size * replicas
        placed = start == 0
        out = run(
            functools.partial(send_cot_kernel, experts, shard, start),
            (1,),
            [whole(routes.shape), whole(gate_probs.shape), whole(out_grad.shape)],
            [IN_VMEM] * (experts + placed),
            [shape_of((CAP, cols))] * experts + [shape_of((tok, slots))] * placed,
            [routes, gate_probs, out_grad],
            after,
        )
        return exchange(out[:experts]), out[experts:]

    second = shard - FIRST
    dy_first, (place,) = send_cot(0, FIRST, [x_in[2]])
    dy, _ = send_cot(FIRST, second, [])

    def grad_near(rows_t, right, others):
        size = rows_t.shape[0] // replicas // 2 * (right.shape[1] // hidden)
        return run(
            functools.partial(grad_near_kernel, grad_scale, replicas),
            (1,),
            [IN_VMEM] * (2 + len(others)),
            [IN_VMEM] * 4,
            [shape_of((pieces // 2, size, hidden))] * 4,
            [rows_t, right, *others],
        )

    def grad_far(rows_t, right, count):
        out = run(
            functools.partial(grad_far_kernel, grad_scale, replicas),
            (1,),
            [IN_VMEM] * 2,
            [IN_VMEM] * count,
            [shape_of((rows_t.shape[0] // 2, right.shape[1] // count))] * count,
            [rows_t, right],
        )
        return [flip(part, "dp", 1) for part in out]

    def transpose(rows):
        (out,) = run(
            transpose_kernel,
            (1,),
            [IN_VMEM] * experts,
            [IN_VMEM],
            [shape_of((rows[0].shape[1], slots))],
            rows,
        )
        return out

    act, act_t, for_gate, for_up = run(
        functools.partial(forward_kernel, experts, 3),
        (1,),
        [IN_VMEM] * (experts + 2),
        [IN_VMEM] * 4,
        [shape_of((slots, hidden))] + [shape_of((hidden, slots), t) for t in (BF16, F32, F32)],
        [*x_in, w_gate, w_up],
        scratch=[pltpu.VMEM((slots, width), BF16)],
    )

    dy_t = transpose(dy_first)
    others = grad_far(dy_t, act, 1)
    (prev,) = run(
        functools.partial(back_first_kernel, shard),
        (1,),
        [IN_VMEM] * 2,
        [IN_VMEM],
        [shape_of((hidden, slots), F32)],
        [w_down, dy_t],
    )
    low_send, low_keep, high_send, high_keep = grad_near(dy_t, act, others)
    low, high = cross(low_send, high_send, 0)
    x_t = transpose(x_in)
    low_state, high_state = [low_keep, low], [high_keep, high]
    for level in range(1, levels):
        low, high = cross(*add_first(low_state, high_state, level), level)
        low_state.append(low)
        high_state.append(high)
    (down_first,) = run(
        finish_first_kernel,
        (1,),
        [whole((1, *a.shape[1:])) for a in low_state + high_state],
        [whole((FIRST, hidden))],
        [shape_of((FIRST, hidden), F32)],
        low_state + high_state,
    )

    dy_t = transpose(dy)
    others = grad_far(dy_t, act, 1)
    delta, delta_t, prob = run(
        functools.partial(back_hidden_kernel, shard),
        (1,),
        [IN_VMEM] * 6,
        [IN_VMEM] * 3,
        [
            shape_of((slots, 2 * hidden)),
            shape_of((2 * hidden, slots)),
            shape_of((1, slots), F32),
        ],
        [prev, w_down, dy_t, act_t, for_gate, for_up],
    )
    others_both = grad_far(x_t, delta, 3)
    low_send, low_keep, high_send, high_keep = grad_near(dy_t, act, others)
    down_low, down_high = cross(low_send, high_send, 0)
    down_keep = low_keep, high_keep

    back_out = run(
        row_grad_kernel,
        (1,),
        [IN_VMEM] * 4,
        [IN_VMEM] * experts,
        [shape_of((CAP, width + EXTRA))] * experts,
        [delta_t, prob, w_gate, w_up],
    )
    back_in = exchange(back_out)

    low_send, low_keep, high_send, high_keep = grad_near(x_t, delta, others_both)
    low, high = cross(low_send, high_send, 0)
    down_low, down_high = run(
        add_pairs_kernel,
        (1,),
        [whole(down_keep[0].shape)] * 4,
        [whole(down_keep[0].shape)] * 2,
        [shape_of(down_keep[0].shape)] * 2,
        [down_keep[0], down_low, down_keep[1], down_high],
    )
    mark([], LONG)
    halves = [[down_low, low_keep, low], [down_high, high_keep, high]]
    for level in range(1, levels):
        count = pieces >> (level + 1)
        places = lambda i: 2 * i + 1, lambda i, count=count: count + i
        low, high = cross(*add(halves, level, count, places), level)
        if level + 1 < levels:
            halves[0].append(low)
            halves[1].append(high)
    mine = add(halves, levels, 1, (lambda i: i, lambda i: i))

    step = width // 2
    x_grad, prob_grad = run(
        functools.partial(combine_kernel, prob_scale),
        (2,),
        [whole((tok, slots)), whole(routes.shape), whole(gate_probs.shape)]
        + block_specs(step, lambda i, pos: (0, i))
        + block_specs(EXTRA, lambda i, pos: (0, width // EXTRA)),
        [pl.BlockSpec((tok, step), lambda i, pos: (0, i)), whole(gate_probs.shape)],
        [shape_of((tok, width)), shape_of(gate_probs.shape)],
        [place, routes, gate_probs, *back_in, *back_in],
        cost=LONG,
    )
    down_grad, gate_grad, up_grad = run(
        finish_kernel,
        (2,),
        [whole(down_first.shape)] + [whole((1, merged, hidden))] * 4,
        [pl.BlockSpec((hidden, half), lambda i, pos: (0, i))]
        + [pl.BlockSpec((half, hidden), lambda i, pos: (i, 0))] * 2,
        [shape_of((hidden, shard), F32)] + [shape_of((shard, hidden), F32)] * 2,
        [down_first, mine[0], low, mine[1], high],
    )
    return (x_grad, prob_grad.T, gate_grad[None], up_grad[None], down_grad[None])


def solution(mesh):
    return jax.shard_map(
        body,
        mesh=mesh,
        in_specs=(
            P(("dp", "expert"), None),
            P(("dp", "expert"), None),
            P(("dp", "expert"), None),
            P(("dp", "expert"), None),
            P("expert", None, None),
            P("expert", None, None),
            P("expert", None, None),
        ),
        out_specs=(
            P(("dp", "expert"), None),
            P(("dp", "expert"), None),
            P("expert", "dp", None),
            P("expert", "dp", None),
            P("expert", None, "dp"),
        ),
        check_vma=False,
    )
```

time: 198 us -> 195 us (0.985)
  the two profiles are of different devices: /device:TPU:8 before, /device:TPU:0 now
where the time goes in v4:
time: 195 us
  waiting for transfers between devices  119 us (61%)
  Pallas kernels  38.9 us (20%)
  starting transfers between devices  33.7 us (17%)
    ppermute x27, waiting for transfers between devices, flip(): return lax.ppermute(x, axis, [(i, i ^ bit) for i in range(count)])  119 us
    pallas_call x25, Pallas kernels, call(): pl.pallas_call(ordered, grid_spec=pltpu.PrefetchScalarGridSpec(num_scalar...  38.9 us
    ppermute x27, starting transfers between devices, flip(): return lax.ppermute(x, axis, [(i, i ^ bit) for i in range(count)])  33.7 us
  transfers between devices with their start and end apart: 27, of which 12 were waited for; matrix products, arithmetic and copies ran while one was open for 0% of the time, Pallas kernels for 16%

profile of v4, /device:TPU:0, one launch (start us, length us, event | category | flops | bytes accessed | tf_op | source)
XLA Modules:
  0.0 195.2 jit_solution(6238482897338169477)
XLA Ops:
  4.0 4.1 %collective-permute-start = (bf16[64,4096]{1,0:T(8,128)(2,1)S(1)}, bf16[64,4096]{1,0:T(8,128)(2,1)S(1)}, u32[]{:S(2)}, u32[]{:S(2)}) collective-permute-start(bf16[64,4096]{1,0:T(8,128)(2,1)S(1)} %get-tuple-element.87), channel_id=1, source_target_pairs={{0,2},{1,3},{2,0},{3,1},{4,6},{5,7},{6,4},{7,5},{8,10},{9,11},{10,... | collective-permute-start | bytes 1572872 | tf_op jit(solution)/shard_map/ppermute | solution.py:313
  10.2 33.1 %collective-permute-done.refs_5_.refs_3_ = bf16[64,4096]{1,0:T(8,128)(2,1)S(1)} collective-permute-done((bf16[64,4096]{1,0:T(8,128)(2,1)S(1)}, bf16[64,4096]{1,0:T(8,128)(2,1)S(1)}, u32[]{:S(2)}, u32[]{:S(2)}) %collective-permute-start) | collective-permute-done | bytes 524320 | tf_op jit(solution)/shard_map/ppermute | solution.py:313
  44.3 2.9 %collective-permute-start.1 = (bf16[64,1024]{1,0:T(8,128)(2,1)S(1)}, bf16[64,1024]{1,0:T(8,128)(2,1)S(1)}, u32[]{:S(2)}, u32[]{:S(2)}) collective-permute-start(bf16[64,1024]{1,0:T(8,128)(2,1)S(1)} %get-tuple-element.90), channel_id=1, source_target_pairs={{0,3},{1,2},{2,1},{3,0},{4,7},{5,6},{6,5},{7,4},{8,11},{9,10},{10,... | collective-permute-start | bytes 393224 | tf_op jit(solution)/shard_map/ppermute | solution.py:313
  47.2 1.6 collective-permute-start.3
  50.1 4.2 %shard_map.114 = (bf16[256,768]{1,0:T(8,128)(2,1)S(1)}, bf16[768,256]{1,0:T(8,128)(2,1)S(1)}, f32[768,256]{1,0:T(8,128)S(1)}, f32[768,256]{1,0:T(8,128)S(1)}, f32[8,128]{1,0:T(8,128)S(1)}) custom-call(s32[2]{0:T(128)S(1)} %pad_add_fusion.refs_0_, bf16[64,4096]{1,0:T(8,128)(2,1)S(1)} %get-tuple-element.93.refs_1_, ...), custom_call_target="tpu_custom_call" | custom-call | flops 1 | bytes 1 | tf_op jit(solution)/shard_map/pallas_call | solution.py:39
  54.3 10.6 %collective-permute-done.2.refs_3_ = bf16[64,1024]{1,0:T(8,128)(2,1)S(1)} collective-permute-done((bf16[64,1024]{1,0:T(8,128)(2,1)S(1)}, bf16[64,1024]{1,0:T(8,128)(2,1)S(1)}, u32[]{:S(2)}, u32[]{:S(2)}) %collective-permute-start.2) | collective-permute-done | bytes 131104 | tf_op jit(solution)/shard_map/ppermute | solution.py:313
  66.7 3.6 %collective-permute-start.6 = (bf16[64,3072]{1,0:T(8,128)(2,1)S(1)}, bf16[64,3072]{1,0:T(8,128)(2,1)S(1)}, u32[]{:S(2)}, u32[]{:S(2)}) collective-permute-start(bf16[64,3072]{1,0:T(8,128)(2,1)S(1)} %get-tuple-element.105), channel_id=1, source_target_pairs={{0,3},{1,2},{2,1},{3,0},{4,7},{5,6},{6,5},{7,4},{8,11},{9,10},{10,... | collective-permute-start | bytes 1179656 | tf_op jit(solution)/shard_map/ppermute | solution.py:313
  71.2 1.5 shard_map.117
  73.6 1.6 collective-permute-start.10
  75.2 1.5 collective-permute-start.11
  77.9 2.2 %collective-permute-done.10.refs_2_ = bf16[2,64,768]{2,1,0:T(8,128)(2,1)S(1)} collective-permute-done((bf16[2,64,768]{2,1,0:T(8,128)(2,1)S(1)}, bf16[2,64,768]{2,1,0:T(8,128)(2,1)S(1)}, u32[]{:S(2)}, u32[]{:S(2)}) %collective-permute-start.10) | collective-permute-done | bytes 196640 | tf_op jit(solution)/shard_map/ppermute | solution.py:313
  82.0 1.6 collective-permute-start.12
  84.1 2.6 %collective-permute-done.12.refs_3_ = bf16[1,64,768]{2,1,0:T(8,128)(2,1)S(1)} collective-permute-done((bf16[1,64,768]{2,1,0:T(8,128)(2,1)S(1)}, bf16[1,64,768]{2,1,0:T(8,128)(2,1)S(1)}, u32[]{:S(2)}, u32[]{:S(2)}) %collective-permute-start.12) | collective-permute-done | bytes 98336 | tf_op jit(solution)/shard_map/ppermute | solution.py:313
  86.6 1.5 collective-permute-done.13.refs_6_
  88.8 14.9 %collective-permute-done.7.refs_3_ = bf16[64,3072]{1,0:T(8,128)(2,1)S(1)} collective-permute-done((bf16[64,3072]{1,0:T(8,128)(2,1)S(1)}, bf16[64,3072]{1,0:T(8,128)(2,1)S(1)}, u32[]{:S(2)}, u32[]{:S(2)}) %collective-permute-start.7) | collective-permute-done | bytes 393248 | tf_op jit(solution)/shard_map/ppermute | solution.py:313
  106.1 2.5 %shard_map.124 = (bf16[256,1536]{1,0:T(8,128)(2,1)S(1)}, bf16[1536,256]{1,0:T(8,128)(2,1)S(1)}, f32[1,256]{1,0:T(1,128)S(1)}, f32[8,128]{1,0:T(8,128)S(1)}) custom-call(s32[2]{0:T(128)S(1)} %pad_add_fusion.refs_0_, f32[768,256]{1,0:T(8,128)S(1)} %get-tuple-element.103.refs_1_, bf16[1,768,4096]{2,1,0:T(8,128)(2,1)S(1)} %bitcast.9, ...), custom_call_target="tpu_custom_call" | custom-call | flops 1 | bytes 1 | tf_op jit(solution)/shard_map/pallas_call | solution.py:39
  108.7 2.3 %shard_map.125 = (bf16[2048,512]{1,0:T(8,128)(2,1)S(1)}, bf16[2048,512]{1,0:T(8,128)(2,1)S(1)}, bf16[2048,512]{1,0:T(8,128)(2,1)S(1)}, f32[8,128]{1,0:T(8,128)S(1)}) custom-call(s32[2]{0:T(128)S(1)} %pad_add_fusion.refs_0_, bf16[4096,256]{1,0:T(8,128)(2,1)S(1)} %get-tuple-element.129.refs_1_, bf16[256,1536]{1,0:T(8,128)(2,1)S(1)} %get-tuple-element.130.refs_2_, ...), custom_call_target="tpu_custom_call" | custom-call | flops 1 | bytes 1 | tf_op jit(solution)/shard_map/pallas_call | solution.py:39
  112.1 1.5 shard_map.126
  113.6 1.6 collective-permute-start.18
  115.2 1.5 collective-permute-start.19
  116.7 4.0 %shard_map.127 = (bf16[64,4224]{1,0:T(8,128)(2,1)S(1)}, bf16[64,4224]{1,0:T(8,128)(2,1)S(1)}, bf16[64,4224]{1,0:T(8,128)(2,1)S(1)}, bf16[64,4224]{1,0:T(8,128)(2,1)S(1)}, f32[8,128]{1,0:T(8,128)S(1)}) custom-call(s32[2]{0:T(128)S(1)} %pad_add_fusion.refs_0_, bf16[1536,256]{1,0:T(8,128)(2,1)S(1)} %get-tuple-element.126.refs_1_, ...), custom_call_target="tpu_custom_call" | custom-call | flops 1 | bytes 1 | tf_op jit(solution)/shard_map/pallas_call | solution.py:39
  120.7 2.2 %collective-permute-start.15 = (bf16[64,4224]{1,0:T(8,128)(2,1)S(1)}, bf16[64,4224]{1,0:T(8,128)(2,1)S(1)}, u32[]{:S(2)}, u32[]{:S(2)}) collective-permute-start(bf16[64,4224]{1,0:T(8,128)(2,1)S(1)} %get-tuple-element.135), channel_id=1, source_target_pairs={{0,3},{1,2},{2,1},{3,0},{4,7},{5,6},{6,5},{7,4},{8,11},{9,10},{10,... | collective-permute-start | bytes 1622024 | tf_op jit(solution)/shard_map/ppermute | solution.py:313
  123.0 2.2 %collective-permute-start.17 = (bf16[64,4224]{1,0:T(8,128)(2,1)S(1)}, bf16[64,4224]{1,0:T(8,128)(2,1)S(1)}, u32[]{:S(2)}, u32[]{:S(2)}) collective-permute-start(bf16[64,4224]{1,0:T(8,128)(2,1)S(1)} %get-tuple-element.137), channel_id=1, source_target_pairs={{0,1},{1,0},{2,3},{3,2},{4,5},{5,4},{6,7},{7,6},{8,9},{9,8},{10,11... | collective-permute-start | bytes 1622024 | tf_op jit(solution)/shard_map/ppermute | solution.py:313
  125.2 2.4 %shard_map.128 = (bf16[2,512,768]{2,1,0:T(8,128)(2,1)S(1)}, bf16[2,512,768]{2,1,0:T(8,128)(2,1)S(1)}, bf16[2,512,768]{2,1,0:T(8,128)(2,1)S(1)}, bf16[2,512,768]{2,1,0:T(8,128)(2,1)S(1)}, f32[8,128]{1,0:T(8,128)S(1)}) custom-call(s32[2]{0:T(128)S(1)} %pad_add_fusion.refs_0_, bf16[4096,256]{1,0:T(8,128)(2,1)S(1)} %get-tuple-element.129.refs_1_, ...), custom_call_target="tpu_custom_call" | custom-call | flops 1 | bytes 1 | tf_op jit(solution)/shard_map/pallas_call | solution.py:39
  127.6 1.4 collective-permute-done.18.refs_2_
  129.0 1.5 collective-permute-start.23
  130.5 1.5 collective-permute-start.24
  133.4 31.1 %collective-permute-done.23.refs_3_.refs_5_ = bf16[2,512,768]{2,1,0:T(8,128)(2,1)S(1)} collective-permute-done((bf16[2,512,768]{2,1,0:T(8,128)(2,1)S(1)}, bf16[2,512,768]{2,1,0:T(8,128)(2,1)S(1)}, u32[]{:S(2)}, u32[]{:S(2)}) %collective-permute-start.23) | collective-permute-done | bytes 1572896 | tf_op jit(solution)/shard_map/ppermute | solution.py:313
  166.7 1.6 collective-permute-start.25
  169.8 2.6 %shard_map.133 = (bf16[128,4096]{1,0:T(8,128)(2,1)}, bf16[2,128]{1,0:T(2,128)(2,1)}, f32[8,128]{1,0:T(8,128)S(1)}) custom-call(s32[2]{0:T(128)S(1)} %pad_add_fusion.refs_0_, bf16[128,256]{1,0:T(8,128)(2,1)S(1)} %get-tuple-element.88.refs_1_, s32[2,128]{1,0:T(2,128)S(1)} %bitcast.17, bf16[2,128]{1,0:T(2,128)(2,1)S(1)} %bitcast.20, ...), custom_call_target="tpu_custom_call" | custom-call | flops 60000002048 | bytes 1 | tf_op jit(solution)/shard_map/pallas_call | solution.py:39
  172.4 18.1 %collective-permute-done.25.refs_3_ = bf16[1,704,768]{2,1,0:T(8,128)(2,1)S(1)} collective-permute-done((bf16[1,704,768]{2,1,0:T(8,128)(2,1)S(1)}, bf16[1,704,768]{2,1,0:T(8,128)(2,1)S(1)}, u32[]{:S(2)}, u32[]{:S(2)}) %collective-permute-start.25) | collective-permute-done | bytes 1081376 | tf_op jit(solution)/shard_map/ppermute | solution.py:313
  191.8 3.2 %shard_map.134 = (f32[768,512]{1,0:T(8,128)}, f32[512,768]{1,0:T(8,128)}, f32[512,768]{1,0:T(8,128)}, f32[8,128]{1,0:T(8,128)}) custom-call(s32[2]{0:T(128)S(1)} %pad_add_fusion.refs_0_, f32[128,768]{1,0:T(8,128)S(1)} %get-tuple-element.158.refs_1_, bf16[1,704,768]{2,1,0:T(8,128)(2,1)S(1)} %get-tuple-element.159.refs_2_, ...), custom_call_target="tpu_custom_call" | custom-call | flops 1 | bytes 1 | tf_op jit(solution)/shard_map/pallas_call | solution.py:39
  (73 shorter events, 25.0 us)
Async XLA Ops:
  4.0 39.4 %collective-permute-start = (bf16[64,4096]{1,0:T(8,128)(2,1)S(1)}, bf16[64,4096]{1,0:T(8,128)(2,1)S(1)}, u32[]{:S(2)}, u32[]{:S(2)}) collective-permute-start(bf16[64,4096]{1,0:T(8,128)(2,1)S(1)} %get-tuple-element.87), channel_id=1, source_target_pairs={{0,2},{1,3},{2,0},{3,1},{4,6},{5,7},{6,4},{7,5},{8,10},{9,11},{10,... | collective-permute-start | bytes 1572872 | tf_op jit(solution)/shard_map/ppermute | solution.py:313
  8.1 41.9 %collective-permute-start.4 = (bf16[64,4096]{1,0:T(8,128)(2,1)S(1)}, bf16[64,4096]{1,0:T(8,128)(2,1)S(1)}, u32[]{:S(2)}, u32[]{:S(2)}) collective-permute-start(bf16[64,4096]{1,0:T(8,128)(2,1)S(1)} %get-tuple-element.94), channel_id=1, source_target_pairs={{0,3},{1,2},{2,1},{3,0},{4,7},{5,6},{6,5},{7,4},{8,11},{9,10},{10,... | collective-permute-start | bytes 1572872 | tf_op jit(solution)/shard_map/ppermute | solution.py:313
  9.4 40.6 %collective-permute-start.5 = (bf16[64,4096]{1,0:T(8,128)(2,1)S(1)}, bf16[64,4096]{1,0:T(8,128)(2,1)S(1)}, u32[]{:S(2)}, u32[]{:S(2)}) collective-permute-start(bf16[64,4096]{1,0:T(8,128)(2,1)S(1)} %get-tuple-element.95), channel_id=1, source_target_pairs={{0,1},{1,0},{2,3},{3,2},{4,5},{5,4},{6,7},{7,6},{8,9},{9,8},{10,11... | collective-permute-start | bytes 1572872 | tf_op jit(solution)/shard_map/ppermute | solution.py:313
  9.7 40.4 %slice-start.2 = ((s8[6291456]{0:T(1024)(128)(4,1)}), s8[4194304]{0:T(1024)(128)(4,1)S(1)}, s32[]{:S(2)}) async-start(s8[6291456]{0:T(1024)(128)(4,1)} %bitcast.10), calls=%async_computation.2 | async-start | bytes 8388608
  9.7 40.4 %slice-start.4 = ((s8[6291456]{0:T(1024)(128)(4,1)}), s8[4194304]{0:T(1024)(128)(4,1)S(1)}, s32[]{:S(2)}) async-start(s8[6291456]{0:T(1024)(128)(4,1)} %bitcast.12), calls=%async_computation.4 | async-start | bytes 8388608
  9.7 33.7 %copy-start.4 = (bf16[128,2]{0,1:T(2,128)(2,1)S(1)}, bf16[128,2]{0,1:T(2,128)(2,1)}, u32[]{:S(2)}) copy-start(bf16[128,2]{0,1:T(2,128)(2,1)} %param.10) | copy-start | bytes 1540
  9.7 40.4 %slice-start.3 = ((s8[6291456]{0:T(1024)(128)(4,1)}), s8[2097152]{0:T(1024)(128)(4,1)S(1)}, s32[]{:S(2)}) async-start(s8[6291456]{0:T(1024)(128)(4,1)} %bitcast.10), calls=%async_computation.3 | async-start | bytes 4194304
  9.7 40.4 %slice-start.5 = ((s8[6291456]{0:T(1024)(128)(4,1)}), s8[2097152]{0:T(1024)(128)(4,1)S(1)}, s32[]{:S(2)}) async-start(s8[6291456]{0:T(1024)(128)(4,1)} %bitcast.12), calls=%async_computation.5 | async-start | bytes 4194304
  44.3 10.0 %collective-permute-start.1 = (bf16[64,1024]{1,0:T(8,128)(2,1)S(1)}, bf16[64,1024]{1,0:T(8,128)(2,1)S(1)}, u32[]{:S(2)}, u32[]{:S(2)}) collective-permute-start(bf16[64,1024]{1,0:T(8,128)(2,1)S(1)} %get-tuple-element.90), channel_id=1, source_target_pairs={{0,3},{1,2},{2,1},{3,0},{4,7},{5,6},{6,5},{7,4},{8,11},{9,10},{10,... | collective-permute-start | bytes 393224 | tf_op jit(solution)/shard_map/ppermute | solution.py:313
  47.2 17.8 %collective-permute-start.2 = (bf16[64,1024]{1,0:T(8,128)(2,1)S(1)}, bf16[64,1024]{1,0:T(8,128)(2,1)S(1)}, u32[]{:S(2)}, u32[]{:S(2)}) collective-permute-start(bf16[64,1024]{1,0:T(8,128)(2,1)S(1)} %get-tuple-element.91), channel_id=1, source_target_pairs={{0,2},{1,3},{2,0},{3,1},{4,6},{5,7},{6,4},{7,5},{8,10},{9,11},{10,... | collective-permute-start | bytes 393224 | tf_op jit(solution)/shard_map/ppermute | solution.py:313
  47.2 17.8 %collective-permute-start.3 = (bf16[64,1024]{1,0:T(8,128)(2,1)S(1)}, bf16[64,1024]{1,0:T(8,128)(2,1)S(1)}, u32[]{:S(2)}, u32[]{:S(2)}) collective-permute-start(bf16[64,1024]{1,0:T(8,128)(2,1)S(1)} %get-tuple-element.92), channel_id=1, source_target_pairs={{0,1},{1,0},{2,3},{3,2},{4,5},{5,4},{6,7},{7,6},{8,9},{9,8},{10,11... | collective-permute-start | bytes 393224 | tf_op jit(solution)/shard_map/ppermute | solution.py:313
  66.6 6.0 %collective-permute-start.9 = (bf16[512,768]{1,0:T(8,128)(2,1)S(1)}, bf16[512,768]{1,0:T(8,128)(2,1)S(1)}, u32[]{:S(2)}, u32[]{:S(2)}) collective-permute-start(bf16[512,768]{1,0:T(8,128)(2,1)S(1)} %get-tuple-element.108), channel_id=1, source_target_pairs={{0,4},{4,0},{8,12},{12,8},{16,20},{20,16},{24,28},{28,24},{1,5},{5... | collective-permute-start | bytes 2359304 | tf_op jit(solution)/shard_map/ppermute | solution.py:313
  66.7 22.0 %collective-permute-start.6 = (bf16[64,3072]{1,0:T(8,128)(2,1)S(1)}, bf16[64,3072]{1,0:T(8,128)(2,1)S(1)}, u32[]{:S(2)}, u32[]{:S(2)}) collective-permute-start(bf16[64,3072]{1,0:T(8,128)(2,1)S(1)} %get-tuple-element.105), channel_id=1, source_target_pairs={{0,3},{1,2},{2,1},{3,0},{4,7},{5,6},{6,5},{7,4},{8,11},{9,10},{10,... | collective-permute-start | bytes 1179656 | tf_op jit(solution)/shard_map/ppermute | solution.py:313
  70.3 33.4 %collective-permute-start.7 = (bf16[64,3072]{1,0:T(8,128)(2,1)S(1)}, bf16[64,3072]{1,0:T(8,128)(2,1)S(1)}, u32[]{:S(2)}, u32[]{:S(2)}) collective-permute-start(bf16[64,3072]{1,0:T(8,128)(2,1)S(1)} %get-tuple-element.106), channel_id=1, source_target_pairs={{0,2},{1,3},{2,0},{3,1},{4,6},{5,7},{6,4},{7,5},{8,10},{9,11},{10,... | collective-permute-start | bytes 1179656 | tf_op jit(solution)/shard_map/ppermute | solution.py:313
  70.3 33.4 %collective-permute-start.8 = (bf16[64,3072]{1,0:T(8,128)(2,1)S(1)}, bf16[64,3072]{1,0:T(8,128)(2,1)S(1)}, u32[]{:S(2)}, u32[]{:S(2)}) collective-permute-start(bf16[64,3072]{1,0:T(8,128)(2,1)S(1)} %get-tuple-element.107), channel_id=1, source_target_pairs={{0,1},{1,0},{2,3},{3,2},{4,5},{5,4},{6,7},{7,6},{8,9},{9,8},{10,11... | collective-permute-start | bytes 1179656 | tf_op jit(solution)/shard_map/ppermute | solution.py:313
  73.6 6.5 %collective-permute-start.10 = (bf16[2,64,768]{2,1,0:T(8,128)(2,1)S(1)}, bf16[2,64,768]{2,1,0:T(8,128)(2,1)S(1)}, u32[]{:S(2)}, u32[]{:S(2)}) collective-permute-start(bf16[2,64,768]{2,1,0:T(8,128)(2,1)S(1)} %get-tuple-element.111), channel_id=1, source_target_pairs={{0,8},{4,12},{8,0},{12,4},{16,24},{20,28},{24,16},{28,20},{1,9},{5... | collective-permute-start | bytes 589832 | tf_op jit(solution)/shard_map/ppermute | solution.py:313
  75.2 6.1 %collective-permute-start.11 = (bf16[2,64,768]{2,1,0:T(8,128)(2,1)S(1)}, bf16[2,64,768]{2,1,0:T(8,128)(2,1)S(1)}, u32[]{:S(2)}, u32[]{:S(2)}) collective-permute-start(bf16[2,64,768]{2,1,0:T(8,128)(2,1)S(1)} %get-tuple-element.113), channel_id=1, source_target_pairs={{0,16},{4,20},{8,24},{12,28},{16,0},{20,4},{24,8},{28,12},{1,17},{... | collective-permute-start | bytes 589832 | tf_op jit(solution)/shard_map/ppermute | solution.py:313
  82.0 4.7 %collective-permute-start.12 = (bf16[1,64,768]{2,1,0:T(8,128)(2,1)S(1)}, bf16[1,64,768]{2,1,0:T(8,128)(2,1)S(1)}, u32[]{:S(2)}, u32[]{:S(2)}) collective-permute-start(bf16[1,64,768]{2,1,0:T(8,128)(2,1)S(1)} %get-tuple-element.116), channel_id=1, source_target_pairs={{0,16},{4,20},{8,24},{12,28},{16,0},{20,4},{24,8},{28,12},{1,17},{... | collective-permute-start | bytes 294920 | tf_op jit(solution)/shard_map/ppermute | solution.py:313
  83.5 4.6 %collective-permute-start.13 = (bf16[1,64,768]{2,1,0:T(8,128)(2,1)S(1)}, bf16[1,64,768]{2,1,0:T(8,128)(2,1)S(1)}, u32[]{:S(2)}, u32[]{:S(2)}) collective-permute-start(bf16[1,64,768]{2,1,0:T(8,128)(2,1)S(1)} %get-tuple-element.117), channel_id=1, source_target_pairs={{0,8},{4,12},{8,0},{12,4},{16,24},{20,28},{24,16},{28,20},{1,9},{5... | collective-permute-start | bytes 294920 | tf_op jit(solution)/shard_map/ppermute | solution.py:313
  106.0 6.0 %collective-permute-start.14 = (bf16[1536,768]{1,0:T(8,128)(2,1)S(1)}, bf16[1536,768]{1,0:T(8,128)(2,1)S(1)}, u32[]{:S(2)}, u32[]{:S(2)}) collective-permute-start(bf16[1536,768]{1,0:T(8,128)(2,1)S(1)} %get-tuple-element.128), channel_id=1, source_target_pairs={{0,4},{4,0},{8,12},{12,8},{16,20},{20,16},{24,28},{28,24},{1,5},{5... | collective-permute-start | bytes 7077896 | tf_op jit(solution)/shard_map/ppermute | solution.py:313
  111.0 9.7 %collective-permute-start.20 = (bf16[2048,512]{1,0:T(8,128)(2,1)S(1)}, bf16[2048,512]{1,0:T(8,128)(2,1)S(1)}, u32[]{:S(2)}, u32[]{:S(2)}) collective-permute-start(bf16[2048,512]{1,0:T(8,128)(2,1)S(1)} %get-tuple-element.142), channel_id=1, source_target_pairs={{0,4},{4,0},{8,12},{12,8},{16,20},{20,16},{24,28},{28,24},{1,5},{5... | collective-permute-start | bytes 6291464 | tf_op jit(solution)/shard_map/ppermute | solution.py:313
  111.6 11.4 %collective-permute-start.21 = (bf16[2048,512]{1,0:T(8,128)(2,1)S(1)}, bf16[2048,512]{1,0:T(8,128)(2,1)S(1)}, u32[]{:S(2)}, u32[]{:S(2)}) collective-permute-start(bf16[2048,512]{1,0:T(8,128)(2,1)S(1)} %get-tuple-element.143), channel_id=1, source_target_pairs={{0,4},{4,0},{8,12},{12,8},{16,20},{20,16},{24,28},{28,24},{1,5},{5... | collective-permute-start | bytes 6291464 | tf_op jit(solution)/shard_map/ppermute | solution.py:313
  111.6 11.3 %collective-permute-start.22 = (bf16[2048,512]{1,0:T(8,128)(2,1)S(1)}, bf16[2048,512]{1,0:T(8,128)(2,1)S(1)}, u32[]{:S(2)}, u32[]{:S(2)}) collective-permute-start(bf16[2048,512]{1,0:T(8,128)(2,1)S(1)} %get-tuple-element.144), channel_id=1, source_target_pairs={{0,4},{4,0},{8,12},{12,8},{16,20},{20,16},{24,28},{28,24},{1,5},{5... | collective-permute-start | bytes 6291464 | tf_op jit(solution)/shard_map/ppermute | solution.py:313
  113.6 15.4 %collective-permute-start.18 = (bf16[2,192,768]{2,1,0:T(8,128)(2,1)S(1)}, bf16[2,192,768]{2,1,0:T(8,128)(2,1)S(1)}, u32[]{:S(2)}, u32[]{:S(2)}) collective-permute-start(bf16[2,192,768]{2,1,0:T(8,128)(2,1)S(1)} %get-tuple-element.139), channel_id=1, source_target_pairs={{0,8},{4,12},{8,0},{12,4},{16,24},{20,28},{24,16},{28,20},{1,9},{5... | collective-permute-start | bytes 1769480 | tf_op jit(solution)/shard_map/ppermute | solution.py:313
  115.2 15.3 %collective-permute-start.19 = (bf16[2,192,768]{2,1,0:T(8,128)(2,1)S(1)}, bf16[2,192,768]{2,1,0:T(8,128)(2,1)S(1)}, u32[]{:S(2)}, u32[]{:S(2)}) collective-permute-start(bf16[2,192,768]{2,1,0:T(8,128)(2,1)S(1)} %get-tuple-element.141), channel_id=1, source_target_pairs={{0,16},{4,20},{8,24},{12,28},{16,0},{20,4},{24,8},{28,12},{1,17},{... | collective-permute-start | bytes 1769480 | tf_op jit(solution)/shard_map/ppermute | solution.py:313
  120.7 49.0 %collective-permute-start.15 = (bf16[64,4224]{1,0:T(8,128)(2,1)S(1)}, bf16[64,4224]{1,0:T(8,128)(2,1)S(1)}, u32[]{:S(2)}, u32[]{:S(2)}) collective-permute-start(bf16[64,4224]{1,0:T(8,128)(2,1)S(1)} %get-tuple-element.135), channel_id=1, source_target_pairs={{0,3},{1,2},{2,1},{3,0},{4,7},{5,6},{6,5},{7,4},{8,11},{9,10},{10,... | collective-permute-start | bytes 1622024 | tf_op jit(solution)/shard_map/ppermute | solution.py:313
  123.0 46.8 %collective-permute-start.16 = (bf16[64,4224]{1,0:T(8,128)(2,1)S(1)}, bf16[64,4224]{1,0:T(8,128)(2,1)S(1)}, u32[]{:S(2)}, u32[]{:S(2)}) collective-permute-start(bf16[64,4224]{1,0:T(8,128)(2,1)S(1)} %get-tuple-element.136), channel_id=1, source_target_pairs={{0,2},{1,3},{2,0},{3,1},{4,6},{5,7},{6,4},{7,5},{8,10},{9,11},{10,... | collective-permute-start | bytes 1622024 | tf_op jit(solution)/shard_map/ppermute | solution.py:313
  123.0 46.8 %collective-permute-start.17 = (bf16[64,4224]{1,0:T(8,128)(2,1)S(1)}, bf16[64,4224]{1,0:T(8,128)(2,1)S(1)}, u32[]{:S(2)}, u32[]{:S(2)}) collective-permute-start(bf16[64,4224]{1,0:T(8,128)(2,1)S(1)} %get-tuple-element.137), channel_id=1, source_target_pairs={{0,1},{1,0},{2,3},{3,2},{4,5},{5,4},{6,7},{7,6},{8,9},{9,8},{10,11... | collective-permute-start | bytes 1622024 | tf_op jit(solution)/shard_map/ppermute | solution.py:313
  129.0 35.5 %collective-permute-start.23 = (bf16[2,512,768]{2,1,0:T(8,128)(2,1)S(1)}, bf16[2,512,768]{2,1,0:T(8,128)(2,1)S(1)}, u32[]{:S(2)}, u32[]{:S(2)}) collective-permute-start(bf16[2,512,768]{2,1,0:T(8,128)(2,1)S(1)} %get-tuple-element.149), channel_id=1, source_target_pairs={{0,8},{4,12},{8,0},{12,4},{16,24},{20,28},{24,16},{28,20},{1,9},{5... | collective-permute-start | bytes 4718600 | tf_op jit(solution)/shard_map/ppermute | solution.py:313
  130.5 35.3 %collective-permute-start.24 = (bf16[2,512,768]{2,1,0:T(8,128)(2,1)S(1)}, bf16[2,512,768]{2,1,0:T(8,128)(2,1)S(1)}, u32[]{:S(2)}, u32[]{:S(2)}) collective-permute-start(bf16[2,512,768]{2,1,0:T(8,128)(2,1)S(1)} %get-tuple-element.152), channel_id=1, source_target_pairs={{0,16},{4,20},{8,24},{12,28},{16,0},{20,4},{24,8},{28,12},{1,17},{... | collective-permute-start | bytes 4718600 | tf_op jit(solution)/shard_map/ppermute | solution.py:313
  166.7 23.9 %collective-permute-start.25 = (bf16[1,704,768]{2,1,0:T(8,128)(2,1)S(1)}, bf16[1,704,768]{2,1,0:T(8,128)(2,1)S(1)}, u32[]{:S(2)}, u32[]{:S(2)}) collective-permute-start(bf16[1,704,768]{2,1,0:T(8,128)(2,1)S(1)} %get-tuple-element.160), channel_id=1, source_target_pairs={{0,16},{4,20},{8,24},{12,28},{16,0},{20,4},{24,8},{28,12},{1,17},{... | collective-permute-start | bytes 3244040 | tf_op jit(solution)/shard_map/ppermute | solution.py:313
  168.3 23.5 %collective-permute-start.26 = (bf16[1,704,768]{2,1,0:T(8,128)(2,1)S(1)}, bf16[1,704,768]{2,1,0:T(8,128)(2,1)S(1)}, u32[]{:S(2)}, u32[]{:S(2)}) collective-permute-start(bf16[1,704,768]{2,1,0:T(8,128)(2,1)S(1)} %get-tuple-element.162), channel_id=1, source_target_pairs={{0,8},{4,12},{8,0},{12,4},{16,24},{20,28},{24,16},{28,20},{1,9},{5... | collective-permute-start | bytes 3244040 | tf_op jit(solution)/shard_map/ppermute | solution.py:313
  (6 other events, 78.8 us)

commit v5 on v4

--- a/solution.py
+++ b/solution.py
@@ -138,6 +138,12 @@
     for at in range(0, out_ref.shape[0], size):
         rows = [ref[:, at : at + size] for ref in ins]
         out_ref[at : at + size] = jnp.concatenate(rows, axis=0).T
+
+
+def transpose_far_kernel(scale, replicas, pos_ref, right_ref, *rest):
+    ins, (out_ref, far_ref) = rest[:-2], rest[-2:]
+    transpose_kernel(pos_ref, *ins, out_ref)
+    grad_far_kernel(scale, replicas, pos_ref, out_ref, right_ref, far_ref)
 
 
 def grad_far_kernel(scale, replicas, pos_ref, rows_ref, right_ref, *outs):
@@ -427,7 +433,7 @@
         return exchange(out[:experts]), out[experts:]
 
     second = shard - FIRST
-    dy_first, (place,) = send_cot(0, FIRST, [x_in[2]])
+    dy_first, (place,) = send_cot(0, FIRST, [x_in[1]])
     dy, _ = send_cot(FIRST, second, [])
 
     def grad_near(rows_t, right, others):
@@ -441,16 +447,17 @@
             [rows_t, right, *others],
         )
 
-    def grad_far(rows_t, right, count):
-        out = run(
-            functools.partial(grad_far_kernel, grad_scale, replicas),
+    def transpose_far(rows):
+        cols = rows[0].shape[1]
+        rows_t, far = run(
+            functools.partial(transpose_far_kernel, grad_scale, replicas),
             (1,),
+            [IN_VMEM] * (1 + experts),
             [IN_VMEM] * 2,
-            [IN_VMEM] * count,
-            [shape_of((rows_t.shape[0] // 2, right.shape[1] // count))] * count,
-            [rows_t, right],
-        )
-        return [flip(part, "dp", 1) for part in out]
+            [shape_of((cols, slots)), shape_of((cols // 2, hidden))],
+            [act, *rows],
+        )
+        return rows_t, flip(far, "dp", 1)
 
     def transpose(rows):
         (out,) = run(
@@ -473,8 +480,7 @@
         scratch=[pltpu.VMEM((slots, width), BF16)],
     )
 
-    dy_t = transpose(dy_first)
-    others = grad_far(dy_t, act, 1)
+    dy_t, other = transpose_far(dy_first)
     (prev,) = run(
         functools.partial(back_first_kernel, shard),
         (1,),
@@ -483,7 +489,7 @@
         [shape_of((hidden, slots), F32)],
         [w_down, dy_t],
     )
-    low_send, low_keep, high_send, high_keep = grad_near(dy_t, act, others)
+    low_send, low_keep, high_send, high_keep = grad_near(dy_t, act, [other])
     low, high = cross(low_send, high_send, 0)
     x_t = transpose(x_in)
     low_state, high_state = [low_keep, low], [high_keep, high]
@@ -500,8 +506,7 @@
         low_state + high_state,
     )
 
-    dy_t = transpose(dy)
-    others = grad_far(dy_t, act, 1)
+    dy_t, other = transpose_far(dy)
     delta, delta_t, prob = run(
         functools.partial(back_hidden_kernel, shard),
         (1,),
@@ -514,8 +519,16 @@
         ],
         [prev, w_down, dy_t, act_t, for_gate, for_up],
     )
-    others_both = grad_far(x_t, delta, 3)
-    low_send, low_keep, high_send, high_keep = grad_near(dy_t, act, others)
+    far = run(
+        functools.partial(grad_far_kernel, grad_scale, replicas),
+        (1,),
+        [IN_VMEM] * 2,
+        [IN_VMEM] * 3,
+        [shape_of((width // 2, 2 * hidden // 3))] * 3,
+        [x_t, delta],
+    )
+    others = [flip(part, "dp", 1) for part in far]
+    low_send, low_keep, high_send, high_keep = grad_near(dy_t, act, [other])
     down_low, down_high = cross(low_send, high_send, 0)
     down_keep = low_keep, high_keep
 
@@ -529,7 +542,7 @@
     )
     back_in = exchange(back_out)
 
-    low_send, low_keep, high_send, high_keep = grad_near(x_t, delta, others_both)
+    low_send, low_keep, high_send, high_keep = grad_near(x_t, delta, others)
     low, high = cross(low_send, high_send, 0)
     down_low, down_high = run(
         add_pairs_kernel,

time: 195 us -> 193 us (0.990)
  waiting for transfers between devices: 119 us -> 98.4 us
  starting transfers between devices: 33.7 us -> 53.7 us
    ppermute x27, waiting for transfers between devices: 119 us -> 98.4 us  [flip(): return lax.ppermute(x, axis, [(i, i ^ bit) for i in range(count)])]
    ppermute x27, starting transfers between devices: 33.7 us -> 53.7 us  [flip(): return lax.ppermute(x, axis, [(i, i ^ bit) for i in range(count)])]
    pallas_call x25 -> x23, Pallas kernels: 38.9 us -> 37.8 us  [call(): pl.pallas_call(ordered, grid_spec=pltpu.PrefetchScalarGridSpec(num_scalar...]
  transfers between devices with their start and end apart: 27 -> 27, of which waited for: 12 -> 13; matrix products, arithmetic and copies ran while one was open for 0% -> 0% of each run, Pallas kernels for 16% -> 16%
where the time goes in v5:
time: 193 us
  waiting for transfers between devices  98.4 us (51%)
  starting transfers between devices  53.7 us (28%)
  Pallas kernels  37.8 us (20%)
  local copies, waits for them, and re-layouts  1.94 us (1%)
    ppermute x27, waiting for transfers between devices, flip(): return lax.ppermute(x, axis, [(i, i ^ bit) for i in range(count)])  98.4 us
    ppermute x27, starting transfers between devices, flip(): return lax.ppermute(x, axis, [(i, i ^ bit) for i in range(count)])  53.7 us
    pallas_call x23, Pallas kernels, call(): pl.pallas_call(ordered, grid_spec=pltpu.PrefetchScalarGridSpec(num_scalar...  37.8 us
  transfers between devices with their start and end apart: 27, of which 13 were waited for; matrix products, arithmetic and copies ran while one was open for 0% of the time, Pallas kernels for 16%

profile of v5, /device:TPU:0, one launch (start us, length us, event | category | flops | bytes accessed | tf_op | source)
XLA Modules:
  0.0 193.1 jit_solution(9743300581930825113)
XLA Ops:
  4.0 5.1 %collective-permute-start = (bf16[64,4096]{1,0:T(8,128)(2,1)S(1)}, bf16[64,4096]{1,0:T(8,128)(2,1)S(1)}, u32[]{:S(2)}, u32[]{:S(2)}) collective-permute-start(bf16[64,4096]{1,0:T(8,128)(2,1)S(1)} %get-tuple-element.85), channel_id=1, source_target_pairs={{0,3},{1,2},{2,1},{3,0},{4,7},{5,6},{6,5},{7,4},{8,11},{9,10},{10,... | collective-permute-start | bytes 1572872 | tf_op jit(solution)/shard_map/ppermute | solution.py:319
  10.3 11.7 %collective-permute-done.refs_5_.refs_2_ = bf16[64,4096]{1,0:T(8,128)(2,1)S(1)} collective-permute-done((bf16[64,4096]{1,0:T(8,128)(2,1)S(1)}, bf16[64,4096]{1,0:T(8,128)(2,1)S(1)}, u32[]{:S(2)}, u32[]{:S(2)}) %collective-permute-start) | collective-permute-done | bytes 524320 | tf_op jit(solution)/shard_map/ppermute | solution.py:319
  23.0 3.9 %collective-permute-start.3 = (bf16[64,1024]{1,0:T(8,128)(2,1)S(1)}, bf16[64,1024]{1,0:T(8,128)(2,1)S(1)}, u32[]{:S(2)}, u32[]{:S(2)}) collective-permute-start(bf16[64,1024]{1,0:T(8,128)(2,1)S(1)} %get-tuple-element.94), channel_id=1, source_target_pairs={{0,3},{1,2},{2,1},{3,0},{4,7},{5,6},{6,5},{7,4},{8,11},{9,10},{10,... | collective-permute-start | bytes 393224 | tf_op jit(solution)/shard_map/ppermute | solution.py:319
  26.8 20.7 %collective-permute-start.4 = (bf16[64,1024]{1,0:T(8,128)(2,1)S(1)}, bf16[64,1024]{1,0:T(8,128)(2,1)S(1)}, u32[]{:S(2)}, u32[]{:S(2)}) collective-permute-start(bf16[64,1024]{1,0:T(8,128)(2,1)S(1)} %get-tuple-element.95), channel_id=1, source_target_pairs={{0,2},{1,3},{2,0},{3,1},{4,6},{5,7},{6,4},{7,5},{8,10},{9,11},{10,... | collective-permute-start | bytes 393224 | tf_op jit(solution)/shard_map/ppermute | solution.py:319
  48.7 11.7 %collective-permute-done.1.refs_3_ = bf16[64,4096]{1,0:T(8,128)(2,1)S(1)} collective-permute-done((bf16[64,4096]{1,0:T(8,128)(2,1)S(1)}, bf16[64,4096]{1,0:T(8,128)(2,1)S(1)}, u32[]{:S(2)}, u32[]{:S(2)}) %collective-permute-start.1) | collective-permute-done | bytes 524320 | tf_op jit(solution)/shard_map/ppermute | solution.py:319
  60.5 4.2 %shard_map.114 = (bf16[256,768]{1,0:T(8,128)(2,1)S(1)}, bf16[768,256]{1,0:T(8,128)(2,1)S(1)}, f32[768,256]{1,0:T(8,128)S(1)}, f32[768,256]{1,0:T(8,128)S(1)}, f32[8,128]{1,0:T(8,128)S(1)}) custom-call(s32[2]{0:T(128)S(1)} %pad_add_fusion.refs_0_, bf16[64,4096]{1,0:T(8,128)(2,1)S(1)} %get-tuple-element.87.refs_1_, ...), custom_call_target="tpu_custom_call" | custom-call | flops 1 | bytes 1 | tf_op jit(solution)/shard_map/pallas_call | solution.py:39
  66.3 2.6 %collective-permute-start.6 = (bf16[64,3072]{1,0:T(8,128)(2,1)S(1)}, bf16[64,3072]{1,0:T(8,128)(2,1)S(1)}, u32[]{:S(2)}, u32[]{:S(2)}) collective-permute-start(bf16[64,3072]{1,0:T(8,128)(2,1)S(1)} %get-tuple-element.102), channel_id=1, source_target_pairs={{0,3},{1,2},{2,1},{3,0},{4,7},{5,6},{6,5},{7,4},{8,11},{9,10},{10,... | collective-permute-start | bytes 1179656 | tf_op jit(solution)/shard_map/ppermute | solution.py:319
  68.8 1.9 collective-permute-start.8
  70.7 1.5 shard_map.116
  73.2 1.5 collective-permute-start.10
  74.7 1.5 collective-permute-start.11
  77.4 2.2 %collective-permute-done.10.refs_2_ = bf16[2,64,768]{2,1,0:T(8,128)(2,1)S(1)} collective-permute-done((bf16[2,64,768]{2,1,0:T(8,128)(2,1)S(1)}, bf16[2,64,768]{2,1,0:T(8,128)(2,1)S(1)}, u32[]{:S(2)}, u32[]{:S(2)}) %collective-permute-start.10) | collective-permute-done | bytes 196640 | tf_op jit(solution)/shard_map/ppermute | solution.py:319
  81.4 1.6 collective-permute-start.12
  83.6 2.6 %collective-permute-done.12.refs_3_ = bf16[1,64,768]{2,1,0:T(8,128)(2,1)S(1)} collective-permute-done((bf16[1,64,768]{2,1,0:T(8,128)(2,1)S(1)}, bf16[1,64,768]{2,1,0:T(8,128)(2,1)S(1)}, u32[]{:S(2)}, u32[]{:S(2)}) %collective-permute-start.12) | collective-permute-done | bytes 98336 | tf_op jit(solution)/shard_map/ppermute | solution.py:319
  86.1 1.5 collective-permute-done.13.refs_6_
  88.3 13.9 %collective-permute-done.7.refs_4_ = bf16[64,3072]{1,0:T(8,128)(2,1)S(1)} collective-permute-done((bf16[64,3072]{1,0:T(8,128)(2,1)S(1)}, bf16[64,3072]{1,0:T(8,128)(2,1)S(1)}, u32[]{:S(2)}, u32[]{:S(2)}) %collective-permute-start.7) | collective-permute-done | bytes 393248 | tf_op jit(solution)/shard_map/ppermute | solution.py:319
  102.2 1.8 shard_map.121
  104.1 2.5 %shard_map.122 = (bf16[256,1536]{1,0:T(8,128)(2,1)S(1)}, bf16[1536,256]{1,0:T(8,128)(2,1)S(1)}, f32[1,256]{1,0:T(1,128)S(1)}, f32[8,128]{1,0:T(8,128)S(1)}) custom-call(s32[2]{0:T(128)S(1)} %pad_add_fusion.refs_0_, f32[768,256]{1,0:T(8,128)S(1)} %get-tuple-element.100.refs_1_, bf16[1,768,4096]{2,1,0:T(8,128)(2,1)S(1)} %bitcast.9, ...), custom_call_target="tpu_custom_call" | custom-call | flops 1 | bytes 1 | tf_op jit(solution)/shard_map/pallas_call | solution.py:39
  106.6 2.3 %shard_map.123 = (bf16[2048,512]{1,0:T(8,128)(2,1)S(1)}, bf16[2048,512]{1,0:T(8,128)(2,1)S(1)}, bf16[2048,512]{1,0:T(8,128)(2,1)S(1)}, f32[8,128]{1,0:T(8,128)S(1)}) custom-call(s32[2]{0:T(128)S(1)} %pad_add_fusion.refs_0_, bf16[4096,256]{1,0:T(8,128)(2,1)S(1)} %get-tuple-element.125.refs_1_, bf16[256,1536]{1,0:T(8,128)(2,1)S(1)} %get-tuple-element.126.refs_2_, ...), custom_call_target="tpu_custom_call" | custom-call | flops 1 | bytes 1 | tf_op jit(solution)/shard_map/pallas_call | solution.py:39
  110.0 1.5 shard_map.124
  111.6 1.5 collective-permute-start.18
  113.1 1.5 collective-permute-start.19
  114.6 4.0 %shard_map.125 = (bf16[64,4224]{1,0:T(8,128)(2,1)S(1)}, bf16[64,4224]{1,0:T(8,128)(2,1)S(1)}, bf16[64,4224]{1,0:T(8,128)(2,1)S(1)}, bf16[64,4224]{1,0:T(8,128)(2,1)S(1)}, f32[8,128]{1,0:T(8,128)S(1)}) custom-call(s32[2]{0:T(128)S(1)} %pad_add_fusion.refs_0_, bf16[1536,256]{1,0:T(8,128)(2,1)S(1)} %get-tuple-element.122.refs_1_, ...), custom_call_target="tpu_custom_call" | custom-call | flops 1 | bytes 1 | tf_op jit(solution)/shard_map/pallas_call | solution.py:39
  118.6 1.8 collective-permute-start.15
  120.4 2.7 %collective-permute-start.17 = (bf16[64,4224]{1,0:T(8,128)(2,1)S(1)}, bf16[64,4224]{1,0:T(8,128)(2,1)S(1)}, u32[]{:S(2)}, u32[]{:S(2)}) collective-permute-start(bf16[64,4224]{1,0:T(8,128)(2,1)S(1)} %get-tuple-element.133), channel_id=1, source_target_pairs={{0,1},{1,0},{2,3},{3,2},{4,5},{5,4},{6,7},{7,6},{8,9},{9,8},{10,11... | collective-permute-start | bytes 1622024 | tf_op jit(solution)/shard_map/ppermute | solution.py:319
  123.1 2.4 %shard_map.126 = (bf16[2,512,768]{2,1,0:T(8,128)(2,1)S(1)}, bf16[2,512,768]{2,1,0:T(8,128)(2,1)S(1)}, bf16[2,512,768]{2,1,0:T(8,128)(2,1)S(1)}, bf16[2,512,768]{2,1,0:T(8,128)(2,1)S(1)}, f32[8,128]{1,0:T(8,128)S(1)}) custom-call(s32[2]{0:T(128)S(1)} %pad_add_fusion.refs_0_, bf16[4096,256]{1,0:T(8,128)(2,1)S(1)} %get-tuple-element.125.refs_1_, ...), custom_call_target="tpu_custom_call" | custom-call | flops 1 | bytes 1 | tf_op jit(solution)/shard_map/pallas_call | solution.py:39
  128.4 1.5 collective-permute-start.24
  131.3 31.2 %collective-permute-done.23.refs_3_.refs_5_ = bf16[2,512,768]{2,1,0:T(8,128)(2,1)S(1)} collective-permute-done((bf16[2,512,768]{2,1,0:T(8,128)(2,1)S(1)}, bf16[2,512,768]{2,1,0:T(8,128)(2,1)S(1)}, u32[]{:S(2)}, u32[]{:S(2)}) %collective-permute-start.23) | collective-permute-done | bytes 1572896 | tf_op jit(solution)/shard_map/ppermute | solution.py:319
  164.6 1.6 collective-permute-start.25
  167.7 2.7 %shard_map.131 = (bf16[128,4096]{1,0:T(8,128)(2,1)}, bf16[2,128]{1,0:T(2,128)(2,1)}, f32[8,128]{1,0:T(8,128)S(1)}) custom-call(s32[2]{0:T(128)S(1)} %pad_add_fusion.refs_0_, bf16[128,256]{1,0:T(8,128)(2,1)S(1)} %get-tuple-element.86.refs_1_, s32[2,128]{1,0:T(2,128)S(1)} %bitcast.17, bf16[2,128]{1,0:T(2,128)(2,1)S(1)} %bitcast.20, ...), custom_call_target="tpu_custom_call" | custom-call | flops 60000002048 | bytes 1 | tf_op jit(solution)/shard_map/pallas_call | solution.py:39
  170.3 18.1 %collective-permute-done.25.refs_3_ = bf16[1,704,768]{2,1,0:T(8,128)(2,1)S(1)} collective-permute-done((bf16[1,704,768]{2,1,0:T(8,128)(2,1)S(1)}, bf16[1,704,768]{2,1,0:T(8,128)(2,1)S(1)}, u32[]{:S(2)}, u32[]{:S(2)}) %collective-permute-start.25) | collective-permute-done | bytes 1081376 | tf_op jit(solution)/shard_map/ppermute | solution.py:319
  189.7 3.2 %shard_map.132 = (f32[768,512]{1,0:T(8,128)}, f32[512,768]{1,0:T(8,128)}, f32[512,768]{1,0:T(8,128)}, f32[8,128]{1,0:T(8,128)}) custom-call(s32[2]{0:T(128)S(1)} %pad_add_fusion.refs_0_, f32[128,768]{1,0:T(8,128)S(1)} %get-tuple-element.154.refs_1_, bf16[1,704,768]{2,1,0:T(8,128)(2,1)S(1)} %get-tuple-element.155.refs_2_, ...), custom_call_target="tpu_custom_call" | custom-call | flops 1 | bytes 1 | tf_op jit(solution)/shard_map/pallas_call | solution.py:39
  (71 shorter events, 23.6 us)
Async XLA Ops:
  4.0 18.0 %collective-permute-start = (bf16[64,4096]{1,0:T(8,128)(2,1)S(1)}, bf16[64,4096]{1,0:T(8,128)(2,1)S(1)}, u32[]{:S(2)}, u32[]{:S(2)}) collective-permute-start(bf16[64,4096]{1,0:T(8,128)(2,1)S(1)} %get-tuple-element.85), channel_id=1, source_target_pairs={{0,3},{1,2},{2,1},{3,0},{4,7},{5,6},{6,5},{7,4},{8,11},{9,10},{10,... | collective-permute-start | bytes 1572872 | tf_op jit(solution)/shard_map/ppermute | solution.py:319
  9.1 51.4 %collective-permute-start.1 = (bf16[64,4096]{1,0:T(8,128)(2,1)S(1)}, bf16[64,4096]{1,0:T(8,128)(2,1)S(1)}, u32[]{:S(2)}, u32[]{:S(2)}) collective-permute-start(bf16[64,4096]{1,0:T(8,128)(2,1)S(1)} %get-tuple-element.88), channel_id=1, source_target_pairs={{0,2},{1,3},{2,0},{3,1},{4,6},{5,7},{6,4},{7,5},{8,10},{9,11},{10,... | collective-permute-start | bytes 1572872 | tf_op jit(solution)/shard_map/ppermute | solution.py:319
  9.1 51.4 %collective-permute-start.2 = (bf16[64,4096]{1,0:T(8,128)(2,1)S(1)}, bf16[64,4096]{1,0:T(8,128)(2,1)S(1)}, u32[]{:S(2)}, u32[]{:S(2)}) collective-permute-start(bf16[64,4096]{1,0:T(8,128)(2,1)S(1)} %get-tuple-element.89), channel_id=1, source_target_pairs={{0,1},{1,0},{2,3},{3,2},{4,5},{5,4},{6,7},{7,6},{8,9},{9,8},{10,11... | collective-permute-start | bytes 1572872 | tf_op jit(solution)/shard_map/ppermute | solution.py:319
  9.7 50.7 %slice-start.2 = ((s8[6291456]{0:T(1024)(128)(4,1)}), s8[4194304]{0:T(1024)(128)(4,1)S(1)}, s32[]{:S(2)}) async-start(s8[6291456]{0:T(1024)(128)(4,1)} %bitcast.10), calls=%async_computation.2 | async-start | bytes 8388608
  9.7 50.7 %slice-start.4 = ((s8[6291456]{0:T(1024)(128)(4,1)}), s8[4194304]{0:T(1024)(128)(4,1)S(1)}, s32[]{:S(2)}) async-start(s8[6291456]{0:T(1024)(128)(4,1)} %bitcast.12), calls=%async_computation.4 | async-start | bytes 8388608
  9.7 12.3 %copy-start.4 = (bf16[128,2]{0,1:T(2,128)(2,1)S(1)}, bf16[128,2]{0,1:T(2,128)(2,1)}, u32[]{:S(2)}) copy-start(bf16[128,2]{0,1:T(2,128)(2,1)} %param.10) | copy-start | bytes 1540
  9.7 50.7 %slice-start.3 = ((s8[6291456]{0:T(1024)(128)(4,1)}), s8[2097152]{0:T(1024)(128)(4,1)S(1)}, s32[]{:S(2)}) async-start(s8[6291456]{0:T(1024)(128)(4,1)} %bitcast.10), calls=%async_computation.3 | async-start | bytes 4194304
  9.8 50.7 %slice-start.5 = ((s8[6291456]{0:T(1024)(128)(4,1)}), s8[2097152]{0:T(1024)(128)(4,1)S(1)}, s32[]{:S(2)}) async-start(s8[6291456]{0:T(1024)(128)(4,1)} %bitcast.12), calls=%async_computation.5 | async-start | bytes 4194304
  23.0 41.8 %collective-permute-start.3 = (bf16[64,1024]{1,0:T(8,128)(2,1)S(1)}, bf16[64,1024]{1,0:T(8,128)(2,1)S(1)}, u32[]{:S(2)}, u32[]{:S(2)}) collective-permute-start(bf16[64,1024]{1,0:T(8,128)(2,1)S(1)} %get-tuple-element.94), channel_id=1, source_target_pairs={{0,3},{1,2},{2,1},{3,0},{4,7},{5,6},{6,5},{7,4},{8,11},{9,10},{10,... | collective-permute-start | bytes 393224 | tf_op jit(solution)/shard_map/ppermute | solution.py:319
  26.8 38.3 %collective-permute-start.4 = (bf16[64,1024]{1,0:T(8,128)(2,1)S(1)}, bf16[64,1024]{1,0:T(8,128)(2,1)S(1)}, u32[]{:S(2)}, u32[]{:S(2)}) collective-permute-start(bf16[64,1024]{1,0:T(8,128)(2,1)S(1)} %get-tuple-element.95), channel_id=1, source_target_pairs={{0,2},{1,3},{2,0},{3,1},{4,6},{5,7},{6,4},{7,5},{8,10},{9,11},{10,... | collective-permute-start | bytes 393224 | tf_op jit(solution)/shard_map/ppermute | solution.py:319
  47.5 17.6 %collective-permute-start.5 = (bf16[64,1024]{1,0:T(8,128)(2,1)S(1)}, bf16[64,1024]{1,0:T(8,128)(2,1)S(1)}, u32[]{:S(2)}, u32[]{:S(2)}) collective-permute-start(bf16[64,1024]{1,0:T(8,128)(2,1)S(1)} %get-tuple-element.96), channel_id=1, source_target_pairs={{0,1},{1,0},{2,3},{3,2},{4,5},{5,4},{6,7},{7,6},{8,9},{9,8},{10,11... | collective-permute-start | bytes 393224 | tf_op jit(solution)/shard_map/ppermute | solution.py:319
  66.2 6.0 %collective-permute-start.9 = (bf16[512,768]{1,0:T(8,128)(2,1)S(1)}, bf16[512,768]{1,0:T(8,128)(2,1)S(1)}, u32[]{:S(2)}, u32[]{:S(2)}) collective-permute-start(bf16[512,768]{1,0:T(8,128)(2,1)S(1)} %get-tuple-element.105), channel_id=1, source_target_pairs={{0,4},{4,0},{8,12},{12,8},{16,20},{20,16},{24,28},{28,24},{1,5},{5... | collective-permute-start | bytes 2359304 | tf_op jit(solution)/shard_map/ppermute | solution.py:319
  66.3 22.0 %collective-permute-start.6 = (bf16[64,3072]{1,0:T(8,128)(2,1)S(1)}, bf16[64,3072]{1,0:T(8,128)(2,1)S(1)}, u32[]{:S(2)}, u32[]{:S(2)}) collective-permute-start(bf16[64,3072]{1,0:T(8,128)(2,1)S(1)} %get-tuple-element.102), channel_id=1, source_target_pairs={{0,3},{1,2},{2,1},{3,0},{4,7},{5,6},{6,5},{7,4},{8,11},{9,10},{10,... | collective-permute-start | bytes 1179656 | tf_op jit(solution)/shard_map/ppermute | solution.py:319
  68.8 33.4 %collective-permute-start.7 = (bf16[64,3072]{1,0:T(8,128)(2,1)S(1)}, bf16[64,3072]{1,0:T(8,128)(2,1)S(1)}, u32[]{:S(2)}, u32[]{:S(2)}) collective-permute-start(bf16[64,3072]{1,0:T(8,128)(2,1)S(1)} %get-tuple-element.103), channel_id=1, source_target_pairs={{0,2},{1,3},{2,0},{3,1},{4,6},{5,7},{6,4},{7,5},{8,10},{9,11},{10,... | collective-permute-start | bytes 1179656 | tf_op jit(solution)/shard_map/ppermute | solution.py:319
  68.8 33.4 %collective-permute-start.8 = (bf16[64,3072]{1,0:T(8,128)(2,1)S(1)}, bf16[64,3072]{1,0:T(8,128)(2,1)S(1)}, u32[]{:S(2)}, u32[]{:S(2)}) collective-permute-start(bf16[64,3072]{1,0:T(8,128)(2,1)S(1)} %get-tuple-element.104), channel_id=1, source_target_pairs={{0,1},{1,0},{2,3},{3,2},{4,5},{5,4},{6,7},{7,6},{8,9},{9,8},{10,11... | collective-permute-start | bytes 1179656 | tf_op jit(solution)/shard_map/ppermute | solution.py:319
  73.2 6.5 %collective-permute-start.10 = (bf16[2,64,768]{2,1,0:T(8,128)(2,1)S(1)}, bf16[2,64,768]{2,1,0:T(8,128)(2,1)S(1)}, u32[]{:S(2)}, u32[]{:S(2)}) collective-permute-start(bf16[2,64,768]{2,1,0:T(8,128)(2,1)S(1)} %get-tuple-element.108), channel_id=1, source_target_pairs={{0,8},{4,12},{8,0},{12,4},{16,24},{20,28},{24,16},{28,20},{1,9},{5... | collective-permute-start | bytes 589832 | tf_op jit(solution)/shard_map/ppermute | solution.py:319
  74.7 6.1 %collective-permute-start.11 = (bf16[2,64,768]{2,1,0:T(8,128)(2,1)S(1)}, bf16[2,64,768]{2,1,0:T(8,128)(2,1)S(1)}, u32[]{:S(2)}, u32[]{:S(2)}) collective-permute-start(bf16[2,64,768]{2,1,0:T(8,128)(2,1)S(1)} %get-tuple-element.110), channel_id=1, source_target_pairs={{0,16},{4,20},{8,24},{12,28},{16,0},{20,4},{24,8},{28,12},{1,17},{... | collective-permute-start | bytes 589832 | tf_op jit(solution)/shard_map/ppermute | solution.py:319
  81.4 4.7 %collective-permute-start.12 = (bf16[1,64,768]{2,1,0:T(8,128)(2,1)S(1)}, bf16[1,64,768]{2,1,0:T(8,128)(2,1)S(1)}, u32[]{:S(2)}, u32[]{:S(2)}) collective-permute-start(bf16[1,64,768]{2,1,0:T(8,128)(2,1)S(1)} %get-tuple-element.113), channel_id=1, source_target_pairs={{0,16},{4,20},{8,24},{12,28},{16,0},{20,4},{24,8},{28,12},{1,17},{... | collective-permute-start | bytes 294920 | tf_op jit(solution)/shard_map/ppermute | solution.py:319
  83.0 4.6 %collective-permute-start.13 = (bf16[1,64,768]{2,1,0:T(8,128)(2,1)S(1)}, bf16[1,64,768]{2,1,0:T(8,128)(2,1)S(1)}, u32[]{:S(2)}, u32[]{:S(2)}) collective-permute-start(bf16[1,64,768]{2,1,0:T(8,128)(2,1)S(1)} %get-tuple-element.114), channel_id=1, source_target_pairs={{0,8},{4,12},{8,0},{12,4},{16,24},{20,28},{24,16},{28,20},{1,9},{5... | collective-permute-start | bytes 294920 | tf_op jit(solution)/shard_map/ppermute | solution.py:319
  104.0 6.0 %collective-permute-start.14 = (bf16[1536,768]{1,0:T(8,128)(2,1)S(1)}, bf16[1536,768]{1,0:T(8,128)(2,1)S(1)}, u32[]{:S(2)}, u32[]{:S(2)}) collective-permute-start(bf16[1536,768]{1,0:T(8,128)(2,1)S(1)} %get-tuple-element.124), channel_id=1, source_target_pairs={{0,4},{4,0},{8,12},{12,8},{16,20},{20,16},{24,28},{28,24},{1,5},{5... | collective-permute-start | bytes 7077896 | tf_op jit(solution)/shard_map/ppermute | solution.py:319
  109.0 9.7 %collective-permute-start.20 = (bf16[2048,512]{1,0:T(8,128)(2,1)S(1)}, bf16[2048,512]{1,0:T(8,128)(2,1)S(1)}, u32[]{:S(2)}, u32[]{:S(2)}) collective-permute-start(bf16[2048,512]{1,0:T(8,128)(2,1)S(1)} %get-tuple-element.138), channel_id=1, source_target_pairs={{0,4},{4,0},{8,12},{12,8},{16,20},{20,16},{24,28},{28,24},{1,5},{5... | collective-permute-start | bytes 6291464 | tf_op jit(solution)/shard_map/ppermute | solution.py:319
  109.5 10.9 %collective-permute-start.21 = (bf16[2048,512]{1,0:T(8,128)(2,1)S(1)}, bf16[2048,512]{1,0:T(8,128)(2,1)S(1)}, u32[]{:S(2)}, u32[]{:S(2)}) collective-permute-start(bf16[2048,512]{1,0:T(8,128)(2,1)S(1)} %get-tuple-element.139), channel_id=1, source_target_pairs={{0,4},{4,0},{8,12},{12,8},{16,20},{20,16},{24,28},{28,24},{1,5},{5... | collective-permute-start | bytes 6291464 | tf_op jit(solution)/shard_map/ppermute | solution.py:319
  109.6 10.8 %collective-permute-start.22 = (bf16[2048,512]{1,0:T(8,128)(2,1)S(1)}, bf16[2048,512]{1,0:T(8,128)(2,1)S(1)}, u32[]{:S(2)}, u32[]{:S(2)}) collective-permute-start(bf16[2048,512]{1,0:T(8,128)(2,1)S(1)} %get-tuple-element.140), channel_id=1, source_target_pairs={{0,4},{4,0},{8,12},{12,8},{16,20},{20,16},{24,28},{28,24},{1,5},{5... | collective-permute-start | bytes 6291464 | tf_op jit(solution)/shard_map/ppermute | solution.py:319
  111.6 15.4 %collective-permute-start.18 = (bf16[2,192,768]{2,1,0:T(8,128)(2,1)S(1)}, bf16[2,192,768]{2,1,0:T(8,128)(2,1)S(1)}, u32[]{:S(2)}, u32[]{:S(2)}) collective-permute-start(bf16[2,192,768]{2,1,0:T(8,128)(2,1)S(1)} %get-tuple-element.135), channel_id=1, source_target_pairs={{0,8},{4,12},{8,0},{12,4},{16,24},{20,28},{24,16},{28,20},{1,9},{5... | collective-permute-start | bytes 1769480 | tf_op jit(solution)/shard_map/ppermute | solution.py:319
  113.1 15.3 %collective-permute-start.19 = (bf16[2,192,768]{2,1,0:T(8,128)(2,1)S(1)}, bf16[2,192,768]{2,1,0:T(8,128)(2,1)S(1)}, u32[]{:S(2)}, u32[]{:S(2)}) collective-permute-start(bf16[2,192,768]{2,1,0:T(8,128)(2,1)S(1)} %get-tuple-element.137), channel_id=1, source_target_pairs={{0,16},{4,20},{8,24},{12,28},{16,0},{20,4},{24,8},{28,12},{1,17},{... | collective-permute-start | bytes 1769480 | tf_op jit(solution)/shard_map/ppermute | solution.py:319
  118.6 49.0 %collective-permute-start.15 = (bf16[64,4224]{1,0:T(8,128)(2,1)S(1)}, bf16[64,4224]{1,0:T(8,128)(2,1)S(1)}, u32[]{:S(2)}, u32[]{:S(2)}) collective-permute-start(bf16[64,4224]{1,0:T(8,128)(2,1)S(1)} %get-tuple-element.131), channel_id=1, source_target_pairs={{0,3},{1,2},{2,1},{3,0},{4,7},{5,6},{6,5},{7,4},{8,11},{9,10},{10,... | collective-permute-start | bytes 1622024 | tf_op jit(solution)/shard_map/ppermute | solution.py:319
  120.4 47.2 %collective-permute-start.16 = (bf16[64,4224]{1,0:T(8,128)(2,1)S(1)}, bf16[64,4224]{1,0:T(8,128)(2,1)S(1)}, u32[]{:S(2)}, u32[]{:S(2)}) collective-permute-start(bf16[64,4224]{1,0:T(8,128)(2,1)S(1)} %get-tuple-element.132), channel_id=1, source_target_pairs={{0,2},{1,3},{2,0},{3,1},{4,6},{5,7},{6,4},{7,5},{8,10},{9,11},{10,... | collective-permute-start | bytes 1622024 | tf_op jit(solution)/shard_map/ppermute | solution.py:319
  120.4 47.2 %collective-permute-start.17 = (bf16[64,4224]{1,0:T(8,128)(2,1)S(1)}, bf16[64,4224]{1,0:T(8,128)(2,1)S(1)}, u32[]{:S(2)}, u32[]{:S(2)}) collective-permute-start(bf16[64,4224]{1,0:T(8,128)(2,1)S(1)} %get-tuple-element.133), channel_id=1, source_target_pairs={{0,1},{1,0},{2,3},{3,2},{4,5},{5,4},{6,7},{7,6},{8,9},{9,8},{10,11... | collective-permute-start | bytes 1622024 | tf_op jit(solution)/shard_map/ppermute | solution.py:319
  127.0 35.5 %collective-permute-start.23 = (bf16[2,512,768]{2,1,0:T(8,128)(2,1)S(1)}, bf16[2,512,768]{2,1,0:T(8,128)(2,1)S(1)}, u32[]{:S(2)}, u32[]{:S(2)}) collective-permute-start(bf16[2,512,768]{2,1,0:T(8,128)(2,1)S(1)} %get-tuple-element.145), channel_id=1, source_target_pairs={{0,8},{4,12},{8,0},{12,4},{16,24},{20,28},{24,16},{28,20},{1,9},{5... | collective-permute-start | bytes 4718600 | tf_op jit(solution)/shard_map/ppermute | solution.py:319
  128.4 35.3 %collective-permute-start.24 = (bf16[2,512,768]{2,1,0:T(8,128)(2,1)S(1)}, bf16[2,512,768]{2,1,0:T(8,128)(2,1)S(1)}, u32[]{:S(2)}, u32[]{:S(2)}) collective-permute-start(bf16[2,512,768]{2,1,0:T(8,128)(2,1)S(1)} %get-tuple-element.148), channel_id=1, source_target_pairs={{0,16},{4,20},{8,24},{12,28},{16,0},{20,4},{24,8},{28,12},{1,17},{... | collective-permute-start | bytes 4718600 | tf_op jit(solution)/shard_map/ppermute | solution.py:319
  164.6 23.9 %collective-permute-start.25 = (bf16[1,704,768]{2,1,0:T(8,128)(2,1)S(1)}, bf16[1,704,768]{2,1,0:T(8,128)(2,1)S(1)}, u32[]{:S(2)}, u32[]{:S(2)}) collective-permute-start(bf16[1,704,768]{2,1,0:T(8,128)(2,1)S(1)} %get-tuple-element.156), channel_id=1, source_target_pairs={{0,16},{4,20},{8,24},{12,28},{16,0},{20,4},{24,8},{28,12},{1,17},{... | collective-permute-start | bytes 3244040 | tf_op jit(solution)/shard_map/ppermute | solution.py:319
  166.2 23.5 %collective-permute-start.26 = (bf16[1,704,768]{2,1,0:T(8,128)(2,1)S(1)}, bf16[1,704,768]{2,1,0:T(8,128)(2,1)S(1)}, u32[]{:S(2)}, u32[]{:S(2)}) collective-permute-start(bf16[1,704,768]{2,1,0:T(8,128)(2,1)S(1)} %get-tuple-element.158), channel_id=1, source_target_pairs={{0,8},{4,12},{8,0},{12,4},{16,24},{20,28},{24,16},{28,20},{1,9},{5... | collective-permute-start | bytes 3244040 | tf_op jit(solution)/shard_map/ppermute | solution.py:319
  (6 other events, 35.6 us)

commit v6 on v5

--- a/solution.py
+++ b/solution.py
@@ -59,8 +59,9 @@
     return jnp.dot(left, right, preferred_element_type=F32)
 
 
-def shard_rows(relative, pos_ref, size):
-    return pl.ds(pl.multiple_of((pos_ref[0] ^ relative) * size, size), size)
+def shard_rows(relative, pos_ref, stride, start):
+    at = (pos_ref[0] ^ relative) * stride + start
+    return pl.ds(pl.multiple_of(at, math.gcd(stride, start)), stride - start)
 
 
 def slot_matrix(routes_ref, my_expert, slots):
@@ -143,26 +144,38 @@
 def transpose_far_kernel(scale, replicas, pos_ref, right_ref, *rest):
     ins, (out_ref, far_ref) = rest[:-2], rest[-2:]
     transpose_kernel(pos_ref, *ins, out_ref)
-    grad_far_kernel(scale, replicas, pos_ref, out_ref, right_ref, far_ref)
-
-
-def grad_far_kernel(scale, replicas, pos_ref, rows_ref, right_ref, *outs):
-    size = rows_ref.shape[0] // replicas
-    cols = outs[0].shape[1]
+    grad_far_kernel(scale, replicas, 0, pos_ref, out_ref, right_ref, far_ref)
+
+
+def transpose_rest_kernel(scale, replicas, pos_ref, right_ref, first_ref, *rest):
+    ins, (out_ref, far_ref) = rest[:-2], rest[-2:]
+    stride = out_ref.shape[0] // replicas
+    size = stride - FIRST
+    for i in range(replicas):
+        at = i * stride
+        out_ref[at : at + FIRST] = first_ref[i * FIRST : (i + 1) * FIRST]
+        rows = [ref[:, i * size : (i + 1) * size] for ref in ins]
+        out_ref[at + FIRST : at + stride] = jnp.concatenate(rows, axis=0).T
+    grad_far_kernel(scale, replicas, FIRST, pos_ref, out_ref, right_ref, far_ref)
+
+
+def grad_far_kernel(scale, replicas, start, pos_ref, rows_ref, right_ref, *outs):
+    stride = rows_ref.shape[0] // replicas
+    size, cols = stride - start, outs[0].shape[1]
     for i in range(replicas // 2):
-        rows = rows_ref[shard_rows(2 * i + 1, pos_ref, size), :]
+        rows = rows_ref[shard_rows(2 * i + 1, pos_ref, stride, start), :]
         part = (dot(rows, right_ref[...]) * scale).astype(BF16)
         for at, out_ref in enumerate(outs):
             out_ref[i * size : (i + 1) * size] = part[:, at * cols : (at + 1) * cols]
 
 
-def grad_near_kernel(scale, replicas, pos_ref, rows_ref, right_ref, *rest):
+def grad_near_kernel(scale, replicas, start, pos_ref, rows_ref, right_ref, *rest):
     others, (low_send, low_keep, high_send, high_keep) = rest[:-4], rest[-4:]
-    size = rows_ref.shape[0] // replicas
-    cols = low_keep.shape[2]
+    stride = rows_ref.shape[0] // replicas
+    size, cols = stride - start, low_keep.shape[2]
     half, count = size // 2, replicas // 4
     for q in range(replicas // 2):
-        rows = rows_ref[shard_rows(2 * q, pos_ref, size), :]
+        rows = rows_ref[shard_rows(2 * q, pos_ref, stride, start), :]
         low_ref = low_send if q % 2 else low_keep
         high_ref, place = (high_send, q - count) if q >= count else (high_keep, q)
         came = [ref[q * size : (q + 1) * size] for ref in others]
@@ -174,26 +187,8 @@
             high_ref[place, at * half : (at + 1) * half] = part[half:]
 
 
-def back_sum(wd_ref, rows_ref, start, shard):
-    count = wd_ref.shape[2] // shard
-    size = rows_ref.shape[0] // count
-    return sum(
-        dot(
-            wd_ref[0, :, i * shard + start : i * shard + start + size],
-            rows_ref[i * size : (i + 1) * size],
-        )
-        for i in range(count)
-    )
-
-
-def back_first_kernel(shard, pos_ref, wd_ref, rows_ref, out_ref):
-    out_ref[...] = back_sum(wd_ref, rows_ref, 0, shard)
-
-
 def back_hidden_kernel(
-    shard,
     pos_ref,
-    prev_ref,
     wd_ref,
     rows_ref,
     act_ref,
@@ -203,7 +198,7 @@
     delta_t_ref,
     prob_ref,
 ):
-    back = prev_ref[...] + back_sum(wd_ref, rows_ref, FIRST, shard)
+    back = dot(wd_ref[0], rows_ref[...])
     dh = (back * for_gate_ref[...]).astype(BF16)
     du = (back * for_up_ref[...]).astype(BF16)
     hidden = back.shape[0]
@@ -406,6 +401,7 @@
 
     blocks = [whole((CAP, width)) for _ in range(experts)]
     routes, gate_probs = routes.T, gate_probs.T
+    mark([], LONG)
     x_out = run(
         functools.partial(send_tokens_kernel, shard),
         (1,),
@@ -436,10 +432,10 @@
     dy_first, (place,) = send_cot(0, FIRST, [x_in[1]])
     dy, _ = send_cot(FIRST, second, [])
 
-    def grad_near(rows_t, right, others):
-        size = rows_t.shape[0] // replicas // 2 * (right.shape[1] // hidden)
+    def grad_near(rows_t, start, right, others):
+        size = (rows_t.shape[0] // replicas - start) // 2 * (right.shape[1] // hidden)
         return run(
-            functools.partial(grad_near_kernel, grad_scale, replicas),
+            functools.partial(grad_near_kernel, grad_scale, replicas, start),
             (1,),
             [IN_VMEM] * (2 + len(others)),
             [IN_VMEM] * 4,
@@ -447,15 +443,14 @@
             [rows_t, right, *others],
         )
 
-    def transpose_far(rows):
-        cols = rows[0].shape[1]
+    def transpose_far(kernel, cols, size, args):
         rows_t, far = run(
-            functools.partial(transpose_far_kernel, grad_scale, replicas),
+            functools.partial(kernel, grad_scale, replicas),
             (1,),
-            [IN_VMEM] * (1 + experts),
+            [IN_VMEM] * len(args),
             [IN_VMEM] * 2,
-            [shape_of((cols, slots)), shape_of((cols // 2, hidden))],
-            [act, *rows],
+            [shape_of((cols, slots)), shape_of((pieces * size, hidden))],
+            args,
         )
         return rows_t, flip(far, "dp", 1)
 
@@ -480,16 +475,10 @@
         scratch=[pltpu.VMEM((slots, width), BF16)],
     )
 
-    dy_t, other = transpose_far(dy_first)
-    (prev,) = run(
-        functools.partial(back_first_kernel, shard),
-        (1,),
-        [IN_VMEM] * 2,
-        [IN_VMEM],
-        [shape_of((hidden, slots), F32)],
-        [w_down, dy_t],
-    )
-    low_send, low_keep, high_send, high_keep = grad_near(dy_t, act, [other])
+    first_t, other = transpose_far(
+        transpose_far_kernel, replicas * FIRST, FIRST, [act, *dy_first]
+    )
+    low_send, low_keep, high_send, high_keep = grad_near(first_t, 0, act, [other])
     low, high = cross(low_send, high_send, 0)
     x_t = transpose(x_in)
     low_state, high_state = [low_keep, low], [high_keep, high]
@@ -506,21 +495,21 @@
         low_state + high_state,
     )
 
-    dy_t, other = transpose_far(dy)
+    dy_t, other = transpose_far(transpose_rest_kernel, width, second, [act, first_t, *dy])
     delta, delta_t, prob = run(
-        functools.partial(back_hidden_kernel, shard),
+        back_hidden_kernel,
         (1,),
-        [IN_VMEM] * 6,
+        [IN_VMEM] * 5,
         [IN_VMEM] * 3,
         [
             shape_of((slots, 2 * hidden)),
             shape_of((2 * hidden, slots)),
             shape_of((1, slots), F32),
         ],
-        [prev, w_down, dy_t, act_t, for_gate, for_up],
+        [w_down, dy_t, act_t, for_gate, for_up],
     )
     far = run(
-        functools.partial(grad_far_kernel, grad_scale, replicas),
+        functools.partial(grad_far_kernel, grad_scale, replicas, 0),
         (1,),
         [IN_VMEM] * 2,
         [IN_VMEM] * 3,
@@ -528,7 +517,7 @@
         [x_t, delta],
     )
     others = [flip(part, "dp", 1) for part in far]
-    low_send, low_keep, high_send, high_keep = grad_near(dy_t, act, [other])
+    low_send, low_keep, high_send, high_keep = grad_near(dy_t, FIRST, act, [other])
     down_low, down_high = cross(low_send, high_send, 0)
     down_keep = low_keep, high_keep
 
@@ -542,7 +531,7 @@
     )
     back_in = exchange(back_out)
 
-    low_send, low_keep, high_send, high_keep = grad_near(x_t, delta, others)
+    low_send, low_keep, high_send, high_keep = grad_near(x_t, 0, delta, others)
     low, high = cross(low_send, high_send, 0)
     down_low, down_high = run(
         add_pairs_kernel,

time: 193 us -> 192 us (level)
  transfers between devices with their start and end apart: 27 -> 27, of which waited for: 13 -> 13; matrix products, arithmetic and copies ran while one was open for 0% -> 0% of each run, Pallas kernels for 16% -> 15%
where the time goes in v6:
time: 192 us
  waiting for transfers between devices  100 us (52%)
  starting transfers between devices  53.7 us (28%)
  Pallas kernels  36.5 us (19%)
    ppermute x27, waiting for transfers between devices, flip(): return lax.ppermute(x, axis, [(i, i ^ bit) for i in range(count)])  100 us
    ppermute x27, starting transfers between devices, flip(): return lax.ppermute(x, axis, [(i, i ^ bit) for i in range(count)])  53.7 us
    pallas_call x23, Pallas kernels, call(): pl.pallas_call(ordered, grid_spec=pltpu.PrefetchScalarGridSpec(num_scalar...  36.5 us
  transfers between devices with their start and end apart: 27, of which 13 were waited for; matrix products, arithmetic and copies ran while one was open for 0% of the time, Pallas kernels for 15%

profile of v6, /device:TPU:0, one launch (start us, length us, event | category | flops | bytes accessed | tf_op | source)
XLA Modules:
  0.0 192.1 jit_solution(8031980908381455987)
XLA Ops:
  3.3 5.1 %collective-permute-start = (bf16[64,4096]{1,0:T(8,128)(2,1)S(1)}, bf16[64,4096]{1,0:T(8,128)(2,1)S(1)}, u32[]{:S(2)}, u32[]{:S(2)}) collective-permute-start(bf16[64,4096]{1,0:T(8,128)(2,1)S(1)} %get-tuple-element.83), channel_id=1, source_target_pairs={{0,3},{1,2},{2,1},{3,0},{4,7},{5,6},{6,5},{7,4},{8,11},{9,10},{10,... | collective-permute-start | bytes 1572872 | tf_op jit(solution)/shard_map/ppermute | solution.py:314
  9.6 11.7 %collective-permute-done.refs_5_.refs_2_ = bf16[64,4096]{1,0:T(8,128)(2,1)S(1)} collective-permute-done((bf16[64,4096]{1,0:T(8,128)(2,1)S(1)}, bf16[64,4096]{1,0:T(8,128)(2,1)S(1)}, u32[]{:S(2)}, u32[]{:S(2)}) %collective-permute-start) | collective-permute-done | bytes 524320 | tf_op jit(solution)/shard_map/ppermute | solution.py:314
  22.3 3.9 %collective-permute-start.3 = (bf16[64,1024]{1,0:T(8,128)(2,1)S(1)}, bf16[64,1024]{1,0:T(8,128)(2,1)S(1)}, u32[]{:S(2)}, u32[]{:S(2)}) collective-permute-start(bf16[64,1024]{1,0:T(8,128)(2,1)S(1)} %get-tuple-element.92), channel_id=1, source_target_pairs={{0,3},{1,2},{2,1},{3,0},{4,7},{5,6},{6,5},{7,4},{8,11},{9,10},{10,... | collective-permute-start | bytes 393224 | tf_op jit(solution)/shard_map/ppermute | solution.py:314
  26.2 20.7 %collective-permute-start.4 = (bf16[64,1024]{1,0:T(8,128)(2,1)S(1)}, bf16[64,1024]{1,0:T(8,128)(2,1)S(1)}, u32[]{:S(2)}, u32[]{:S(2)}) collective-permute-start(bf16[64,1024]{1,0:T(8,128)(2,1)S(1)} %get-tuple-element.93), channel_id=1, source_target_pairs={{0,2},{1,3},{2,0},{3,1},{4,6},{5,7},{6,4},{7,5},{8,10},{9,11},{10,... | collective-permute-start | bytes 393224 | tf_op jit(solution)/shard_map/ppermute | solution.py:314
  48.1 11.7 %collective-permute-done.1.refs_3_ = bf16[64,4096]{1,0:T(8,128)(2,1)S(1)} collective-permute-done((bf16[64,4096]{1,0:T(8,128)(2,1)S(1)}, bf16[64,4096]{1,0:T(8,128)(2,1)S(1)}, u32[]{:S(2)}, u32[]{:S(2)}) %collective-permute-start.1) | collective-permute-done | bytes 524320 | tf_op jit(solution)/shard_map/ppermute | solution.py:314
  59.8 4.2 %shard_map.115 = (bf16[256,768]{1,0:T(8,128)(2,1)S(1)}, bf16[768,256]{1,0:T(8,128)(2,1)S(1)}, f32[768,256]{1,0:T(8,128)S(1)}, f32[768,256]{1,0:T(8,128)S(1)}, f32[8,128]{1,0:T(8,128)S(1)}) custom-call(s32[2]{0:T(128)S(1)} %pad_add_fusion.refs_0_, bf16[64,4096]{1,0:T(8,128)(2,1)S(1)} %get-tuple-element.85.refs_1_, ...), custom_call_target="tpu_custom_call" | custom-call | flops 1 | bytes 1 | tf_op jit(solution)/shard_map/pallas_call | solution.py:39
  65.6 2.6 %collective-permute-start.6 = (bf16[64,3072]{1,0:T(8,128)(2,1)S(1)}, bf16[64,3072]{1,0:T(8,128)(2,1)S(1)}, u32[]{:S(2)}, u32[]{:S(2)}) collective-permute-start(bf16[64,3072]{1,0:T(8,128)(2,1)S(1)} %get-tuple-element.98), channel_id=1, source_target_pairs={{0,3},{1,2},{2,1},{3,0},{4,7},{5,6},{6,5},{7,4},{8,11},{9,10},{10,... | collective-permute-start | bytes 1179656 | tf_op jit(solution)/shard_map/ppermute | solution.py:314
  68.2 1.9 collective-permute-start.8
  71.0 1.6 collective-permute-start.10
  72.5 1.5 collective-permute-start.11
  75.2 2.2 %collective-permute-done.10.refs_2_ = bf16[2,64,768]{2,1,0:T(8,128)(2,1)S(1)} collective-permute-done((bf16[2,64,768]{2,1,0:T(8,128)(2,1)S(1)}, bf16[2,64,768]{2,1,0:T(8,128)(2,1)S(1)}, u32[]{:S(2)}, u32[]{:S(2)}) %collective-permute-start.10) | collective-permute-done | bytes 196640 | tf_op jit(solution)/shard_map/ppermute | solution.py:314
  79.3 1.6 collective-permute-start.12
  81.4 2.6 %collective-permute-done.12.refs_3_ = bf16[1,64,768]{2,1,0:T(8,128)(2,1)S(1)} collective-permute-done((bf16[1,64,768]{2,1,0:T(8,128)(2,1)S(1)}, bf16[1,64,768]{2,1,0:T(8,128)(2,1)S(1)}, u32[]{:S(2)}, u32[]{:S(2)}) %collective-permute-start.12) | collective-permute-done | bytes 98336 | tf_op jit(solution)/shard_map/ppermute | solution.py:314
  83.9 1.5 collective-permute-done.13.refs_6_
  86.1 15.5 %collective-permute-done.7.refs_5_ = bf16[64,3072]{1,0:T(8,128)(2,1)S(1)} collective-permute-done((bf16[64,3072]{1,0:T(8,128)(2,1)S(1)}, bf16[64,3072]{1,0:T(8,128)(2,1)S(1)}, u32[]{:S(2)}, u32[]{:S(2)}) %collective-permute-start.7) | collective-permute-done | bytes 393248 | tf_op jit(solution)/shard_map/ppermute | solution.py:314
  101.5 1.8 shard_map.121
  103.4 2.5 %shard_map.122 = (bf16[256,1536]{1,0:T(8,128)(2,1)S(1)}, bf16[1536,256]{1,0:T(8,128)(2,1)S(1)}, f32[1,256]{1,0:T(1,128)S(1)}, f32[8,128]{1,0:T(8,128)S(1)}) custom-call(s32[2]{0:T(128)S(1)} %pad_add_fusion.refs_0_, bf16[1,768,4096]{2,1,0:T(8,128)(2,1)S(1)} %bitcast.13, bf16[4096,256]{1,0:T(8,128)(2,1)S(1)} %get-tuple-element.113.refs_2_.refs_1_, ...), custom_call_target="tpu_custom_call" | custom-call | flops 1 | bytes 1 | tf_op jit(solution)/shard_map/pallas_call | solution.py:39
  105.9 2.3 %shard_map.123 = (bf16[2048,512]{1,0:T(8,128)(2,1)S(1)}, bf16[2048,512]{1,0:T(8,128)(2,1)S(1)}, bf16[2048,512]{1,0:T(8,128)(2,1)S(1)}, f32[8,128]{1,0:T(8,128)S(1)}) custom-call(s32[2]{0:T(128)S(1)} %pad_add_fusion.refs_0_, bf16[4096,256]{1,0:T(8,128)(2,1)S(1)} %get-tuple-element.121.refs_1_, bf16[256,1536]{1,0:T(8,128)(2,1)S(1)} %get-tuple-element.122.refs_2_, ...), custom_call_target="tpu_custom_call" | custom-call | flops 1 | bytes 1 | tf_op jit(solution)/shard_map/pallas_call | solution.py:39
  110.6 1.5 collective-permute-start.18
  112.1 1.5 collective-permute-start.19
  113.7 4.0 %shard_map.125 = (bf16[64,4224]{1,0:T(8,128)(2,1)S(1)}, bf16[64,4224]{1,0:T(8,128)(2,1)S(1)}, bf16[64,4224]{1,0:T(8,128)(2,1)S(1)}, bf16[64,4224]{1,0:T(8,128)(2,1)S(1)}, f32[8,128]{1,0:T(8,128)S(1)}) custom-call(s32[2]{0:T(128)S(1)} %pad_add_fusion.refs_0_, bf16[1536,256]{1,0:T(8,128)(2,1)S(1)} %get-tuple-element.118.refs_1_, ...), custom_call_target="tpu_custom_call" | custom-call | flops 1 | bytes 1 | tf_op jit(solution)/shard_map/pallas_call | solution.py:39
  117.7 1.8 collective-permute-start.15
  119.5 2.7 %collective-permute-start.17 = (bf16[64,4224]{1,0:T(8,128)(2,1)S(1)}, bf16[64,4224]{1,0:T(8,128)(2,1)S(1)}, u32[]{:S(2)}, u32[]{:S(2)}) collective-permute-start(bf16[64,4224]{1,0:T(8,128)(2,1)S(1)} %get-tuple-element.129), channel_id=1, source_target_pairs={{0,1},{1,0},{2,3},{3,2},{4,5},{5,4},{6,7},{7,6},{8,9},{9,8},{10,11... | collective-permute-start | bytes 1622024 | tf_op jit(solution)/shard_map/ppermute | solution.py:314
  122.2 2.4 %shard_map.126 = (bf16[2,512,768]{2,1,0:T(8,128)(2,1)S(1)}, bf16[2,512,768]{2,1,0:T(8,128)(2,1)S(1)}, bf16[2,512,768]{2,1,0:T(8,128)(2,1)S(1)}, bf16[2,512,768]{2,1,0:T(8,128)(2,1)S(1)}, f32[8,128]{1,0:T(8,128)S(1)}) custom-call(s32[2]{0:T(128)S(1)} %pad_add_fusion.refs_0_, bf16[4096,256]{1,0:T(8,128)(2,1)S(1)} %get-tuple-element.121.refs_1_, ...), custom_call_target="tpu_custom_call" | custom-call | flops 1 | bytes 1 | tf_op jit(solution)/shard_map/pallas_call | solution.py:39
  124.5 1.5 collective-permute-done.18.refs_2_
  126.0 1.4 collective-permute-start.23
  127.4 1.5 collective-permute-start.24
  130.4 31.2 %collective-permute-done.23.refs_3_.refs_5_ = bf16[2,512,768]{2,1,0:T(8,128)(2,1)S(1)} collective-permute-done((bf16[2,512,768]{2,1,0:T(8,128)(2,1)S(1)}, bf16[2,512,768]{2,1,0:T(8,128)(2,1)S(1)}, u32[]{:S(2)}, u32[]{:S(2)}) %collective-permute-start.23) | collective-permute-done | bytes 1572896 | tf_op jit(solution)/shard_map/ppermute | solution.py:314
  163.6 1.6 collective-permute-start.25
  166.7 2.6 %shard_map.131 = (bf16[128,4096]{1,0:T(8,128)(2,1)}, bf16[2,128]{1,0:T(2,128)(2,1)}, f32[8,128]{1,0:T(8,128)S(1)}) custom-call(s32[2]{0:T(128)S(1)} %pad_add_fusion.refs_0_, bf16[128,256]{1,0:T(8,128)(2,1)S(1)} %get-tuple-element.84.refs_1_, s32[2,128]{1,0:T(2,128)S(1)} %bitcast.17, bf16[2,128]{1,0:T(2,128)(2,1)S(1)} %bitcast.20, ...), custom_call_target="tpu_custom_call" | custom-call | flops 60000002048 | bytes 1 | tf_op jit(solution)/shard_map/pallas_call | solution.py:39
  169.4 18.1 %collective-permute-done.25.refs_3_ = bf16[1,704,768]{2,1,0:T(8,128)(2,1)S(1)} collective-permute-done((bf16[1,704,768]{2,1,0:T(8,128)(2,1)S(1)}, bf16[1,704,768]{2,1,0:T(8,128)(2,1)S(1)}, u32[]{:S(2)}, u32[]{:S(2)}) %collective-permute-start.25) | collective-permute-done | bytes 1081376 | tf_op jit(solution)/shard_map/ppermute | solution.py:314
  188.8 3.2 %shard_map.132 = (f32[768,512]{1,0:T(8,128)}, f32[512,768]{1,0:T(8,128)}, f32[512,768]{1,0:T(8,128)}, f32[8,128]{1,0:T(8,128)}) custom-call(s32[2]{0:T(128)S(1)} %pad_add_fusion.refs_0_, f32[128,768]{1,0:T(8,128)S(1)} %get-tuple-element.150.refs_1_, bf16[1,704,768]{2,1,0:T(8,128)(2,1)S(1)} %get-tuple-element.151.refs_2_, ...), custom_call_target="tpu_custom_call" | custom-call | flops 1 | bytes 1 | tf_op jit(solution)/shard_map/pallas_call | solution.py:39
  (69 shorter events, 21.2 us)
Async XLA Ops:
  0.7 102.7 %slice-start.4 = ((s8[6291456]{0:T(1024)(128)(4,1)}), s8[4194304]{0:T(1024)(128)(4,1)S(1)}, s32[]{:S(2)}) async-start(s8[6291456]{0:T(1024)(128)(4,1)} %bitcast.12), calls=%async_computation.4 | async-start | bytes 8388608
  3.3 18.0 %collective-permute-start = (bf16[64,4096]{1,0:T(8,128)(2,1)S(1)}, bf16[64,4096]{1,0:T(8,128)(2,1)S(1)}, u32[]{:S(2)}, u32[]{:S(2)}) collective-permute-start(bf16[64,4096]{1,0:T(8,128)(2,1)S(1)} %get-tuple-element.83), channel_id=1, source_target_pairs={{0,3},{1,2},{2,1},{3,0},{4,7},{5,6},{6,5},{7,4},{8,11},{9,10},{10,... | collective-permute-start | bytes 1572872 | tf_op jit(solution)/shard_map/ppermute | solution.py:314
  8.4 51.4 %collective-permute-start.1 = (bf16[64,4096]{1,0:T(8,128)(2,1)S(1)}, bf16[64,4096]{1,0:T(8,128)(2,1)S(1)}, u32[]{:S(2)}, u32[]{:S(2)}) collective-permute-start(bf16[64,4096]{1,0:T(8,128)(2,1)S(1)} %get-tuple-element.86), channel_id=1, source_target_pairs={{0,2},{1,3},{2,0},{3,1},{4,6},{5,7},{6,4},{7,5},{8,10},{9,11},{10,... | collective-permute-start | bytes 1572872 | tf_op jit(solution)/shard_map/ppermute | solution.py:314
  8.4 51.4 %collective-permute-start.2 = (bf16[64,4096]{1,0:T(8,128)(2,1)S(1)}, bf16[64,4096]{1,0:T(8,128)(2,1)S(1)}, u32[]{:S(2)}, u32[]{:S(2)}) collective-permute-start(bf16[64,4096]{1,0:T(8,128)(2,1)S(1)} %get-tuple-element.87), channel_id=1, source_target_pairs={{0,1},{1,0},{2,3},{3,2},{4,5},{5,4},{6,7},{7,6},{8,9},{9,8},{10,11... | collective-permute-start | bytes 1572872 | tf_op jit(solution)/shard_map/ppermute | solution.py:314
  9.0 50.7 %slice-start = ((s8[6291456]{0:T(1024)(128)(4,1)}), s8[4194304]{0:T(1024)(128)(4,1)S(1)}, s32[]{:S(2)}) async-start(s8[6291456]{0:T(1024)(128)(4,1)} %bitcast.8), calls=%async_computation | async-start | bytes 8388608
  9.0 50.7 %slice-start.2 = ((s8[6291456]{0:T(1024)(128)(4,1)}), s8[4194304]{0:T(1024)(128)(4,1)S(1)}, s32[]{:S(2)}) async-start(s8[6291456]{0:T(1024)(128)(4,1)} %bitcast.10), calls=%async_computation.2 | async-start | bytes 8388608
  9.1 50.7 %slice-start.1 = ((s8[6291456]{0:T(1024)(128)(4,1)}), s8[2097152]{0:T(1024)(128)(4,1)S(1)}, s32[]{:S(2)}) async-start(s8[6291456]{0:T(1024)(128)(4,1)} %bitcast.8), calls=%async_computation.1 | async-start | bytes 4194304
  9.1 94.3 %slice-start.5 = ((s8[6291456]{0:T(1024)(128)(4,1)}), s8[2097152]{0:T(1024)(128)(4,1)S(1)}, s32[]{:S(2)}) async-start(s8[6291456]{0:T(1024)(128)(4,1)} %bitcast.12), calls=%async_computation.5 | async-start | bytes 4194304
  22.3 41.8 %collective-permute-start.3 = (bf16[64,1024]{1,0:T(8,128)(2,1)S(1)}, bf16[64,1024]{1,0:T(8,128)(2,1)S(1)}, u32[]{:S(2)}, u32[]{:S(2)}) collective-permute-start(bf16[64,1024]{1,0:T(8,128)(2,1)S(1)} %get-tuple-element.92), channel_id=1, source_target_pairs={{0,3},{1,2},{2,1},{3,0},{4,7},{5,6},{6,5},{7,4},{8,11},{9,10},{10,... | collective-permute-start | bytes 393224 | tf_op jit(solution)/shard_map/ppermute | solution.py:314
  26.2 38.3 %collective-permute-start.4 = (bf16[64,1024]{1,0:T(8,128)(2,1)S(1)}, bf16[64,1024]{1,0:T(8,128)(2,1)S(1)}, u32[]{:S(2)}, u32[]{:S(2)}) collective-permute-start(bf16[64,1024]{1,0:T(8,128)(2,1)S(1)} %get-tuple-element.93), channel_id=1, source_target_pairs={{0,2},{1,3},{2,0},{3,1},{4,6},{5,7},{6,4},{7,5},{8,10},{9,11},{10,... | collective-permute-start | bytes 393224 | tf_op jit(solution)/shard_map/ppermute | solution.py:314
  46.8 17.6 %collective-permute-start.5 = (bf16[64,1024]{1,0:T(8,128)(2,1)S(1)}, bf16[64,1024]{1,0:T(8,128)(2,1)S(1)}, u32[]{:S(2)}, u32[]{:S(2)}) collective-permute-start(bf16[64,1024]{1,0:T(8,128)(2,1)S(1)} %get-tuple-element.94), channel_id=1, source_target_pairs={{0,1},{1,0},{2,3},{3,2},{4,5},{5,4},{6,7},{7,6},{8,9},{9,8},{10,11... | collective-permute-start | bytes 393224 | tf_op jit(solution)/shard_map/ppermute | solution.py:314
  65.5 4.5 %collective-permute-start.9 = (bf16[512,768]{1,0:T(8,128)(2,1)S(1)}, bf16[512,768]{1,0:T(8,128)(2,1)S(1)}, u32[]{:S(2)}, u32[]{:S(2)}) collective-permute-start(bf16[512,768]{1,0:T(8,128)(2,1)S(1)} %get-tuple-element.101), channel_id=1, source_target_pairs={{0,4},{4,0},{8,12},{12,8},{16,20},{20,16},{24,28},{28,24},{1,5},{5... | collective-permute-start | bytes 2359304 | tf_op jit(solution)/shard_map/ppermute | solution.py:314
  65.6 20.5 %collective-permute-start.6 = (bf16[64,3072]{1,0:T(8,128)(2,1)S(1)}, bf16[64,3072]{1,0:T(8,128)(2,1)S(1)}, u32[]{:S(2)}, u32[]{:S(2)}) collective-permute-start(bf16[64,3072]{1,0:T(8,128)(2,1)S(1)} %get-tuple-element.98), channel_id=1, source_target_pairs={{0,3},{1,2},{2,1},{3,0},{4,7},{5,6},{6,5},{7,4},{8,11},{9,10},{10,... | collective-permute-start | bytes 1179656 | tf_op jit(solution)/shard_map/ppermute | solution.py:314
  68.2 33.4 %collective-permute-start.7 = (bf16[64,3072]{1,0:T(8,128)(2,1)S(1)}, bf16[64,3072]{1,0:T(8,128)(2,1)S(1)}, u32[]{:S(2)}, u32[]{:S(2)}) collective-permute-start(bf16[64,3072]{1,0:T(8,128)(2,1)S(1)} %get-tuple-element.99), channel_id=1, source_target_pairs={{0,2},{1,3},{2,0},{3,1},{4,6},{5,7},{6,4},{7,5},{8,10},{9,11},{10,... | collective-permute-start | bytes 1179656 | tf_op jit(solution)/shard_map/ppermute | solution.py:314
  68.2 33.4 %collective-permute-start.8 = (bf16[64,3072]{1,0:T(8,128)(2,1)S(1)}, bf16[64,3072]{1,0:T(8,128)(2,1)S(1)}, u32[]{:S(2)}, u32[]{:S(2)}) collective-permute-start(bf16[64,3072]{1,0:T(8,128)(2,1)S(1)} %get-tuple-element.100), channel_id=1, source_target_pairs={{0,1},{1,0},{2,3},{3,2},{4,5},{5,4},{6,7},{7,6},{8,9},{9,8},{10,11... | collective-permute-start | bytes 1179656 | tf_op jit(solution)/shard_map/ppermute | solution.py:314
  71.0 6.5 %collective-permute-start.10 = (bf16[2,64,768]{2,1,0:T(8,128)(2,1)S(1)}, bf16[2,64,768]{2,1,0:T(8,128)(2,1)S(1)}, u32[]{:S(2)}, u32[]{:S(2)}) collective-permute-start(bf16[2,64,768]{2,1,0:T(8,128)(2,1)S(1)} %get-tuple-element.104), channel_id=1, source_target_pairs={{0,8},{4,12},{8,0},{12,4},{16,24},{20,28},{24,16},{28,20},{1,9},{5... | collective-permute-start | bytes 589832 | tf_op jit(solution)/shard_map/ppermute | solution.py:314
  72.5 6.1 %collective-permute-start.11 = (bf16[2,64,768]{2,1,0:T(8,128)(2,1)S(1)}, bf16[2,64,768]{2,1,0:T(8,128)(2,1)S(1)}, u32[]{:S(2)}, u32[]{:S(2)}) collective-permute-start(bf16[2,64,768]{2,1,0:T(8,128)(2,1)S(1)} %get-tuple-element.106), channel_id=1, source_target_pairs={{0,16},{4,20},{8,24},{12,28},{16,0},{20,4},{24,8},{28,12},{1,17},{... | collective-permute-start | bytes 589832 | tf_op jit(solution)/shard_map/ppermute | solution.py:314
  79.3 4.7 %collective-permute-start.12 = (bf16[1,64,768]{2,1,0:T(8,128)(2,1)S(1)}, bf16[1,64,768]{2,1,0:T(8,128)(2,1)S(1)}, u32[]{:S(2)}, u32[]{:S(2)}) collective-permute-start(bf16[1,64,768]{2,1,0:T(8,128)(2,1)S(1)} %get-tuple-element.109), channel_id=1, source_target_pairs={{0,16},{4,20},{8,24},{12,28},{16,0},{20,4},{24,8},{28,12},{1,17},{... | collective-permute-start | bytes 294920 | tf_op jit(solution)/shard_map/ppermute | solution.py:314
  80.8 4.6 %collective-permute-start.13 = (bf16[1,64,768]{2,1,0:T(8,128)(2,1)S(1)}, bf16[1,64,768]{2,1,0:T(8,128)(2,1)S(1)}, u32[]{:S(2)}, u32[]{:S(2)}) collective-permute-start(bf16[1,64,768]{2,1,0:T(8,128)(2,1)S(1)} %get-tuple-element.110), channel_id=1, source_target_pairs={{0,8},{4,12},{8,0},{12,4},{16,24},{20,28},{24,16},{28,20},{1,9},{5... | collective-permute-start | bytes 294920 | tf_op jit(solution)/shard_map/ppermute | solution.py:314
  103.3 6.0 %collective-permute-start.14 = (bf16[1536,768]{1,0:T(8,128)(2,1)S(1)}, bf16[1536,768]{1,0:T(8,128)(2,1)S(1)}, u32[]{:S(2)}, u32[]{:S(2)}) collective-permute-start(bf16[1536,768]{1,0:T(8,128)(2,1)S(1)} %get-tuple-element.120), channel_id=1, source_target_pairs={{0,4},{4,0},{8,12},{12,8},{16,20},{20,16},{24,28},{28,24},{1,5},{5... | collective-permute-start | bytes 7077896 | tf_op jit(solution)/shard_map/ppermute | solution.py:314
  108.2 9.5 %collective-permute-start.20 = (bf16[2048,512]{1,0:T(8,128)(2,1)S(1)}, bf16[2048,512]{1,0:T(8,128)(2,1)S(1)}, u32[]{:S(2)}, u32[]{:S(2)}) collective-permute-start(bf16[2048,512]{1,0:T(8,128)(2,1)S(1)} %get-tuple-element.134), channel_id=1, source_target_pairs={{0,4},{4,0},{8,12},{12,8},{16,20},{20,16},{24,28},{28,24},{1,5},{5... | collective-permute-start | bytes 6291464 | tf_op jit(solution)/shard_map/ppermute | solution.py:314
  108.8 10.7 %collective-permute-start.21 = (bf16[2048,512]{1,0:T(8,128)(2,1)S(1)}, bf16[2048,512]{1,0:T(8,128)(2,1)S(1)}, u32[]{:S(2)}, u32[]{:S(2)}) collective-permute-start(bf16[2048,512]{1,0:T(8,128)(2,1)S(1)} %get-tuple-element.135), channel_id=1, source_target_pairs={{0,4},{4,0},{8,12},{12,8},{16,20},{20,16},{24,28},{28,24},{1,5},{5... | collective-permute-start | bytes 6291464 | tf_op jit(solution)/shard_map/ppermute | solution.py:314
  108.9 10.6 %collective-permute-start.22 = (bf16[2048,512]{1,0:T(8,128)(2,1)S(1)}, bf16[2048,512]{1,0:T(8,128)(2,1)S(1)}, u32[]{:S(2)}, u32[]{:S(2)}) collective-permute-start(bf16[2048,512]{1,0:T(8,128)(2,1)S(1)} %get-tuple-element.136), channel_id=1, source_target_pairs={{0,4},{4,0},{8,12},{12,8},{16,20},{20,16},{24,28},{28,24},{1,5},{5... | collective-permute-start | bytes 6291464 | tf_op jit(solution)/shard_map/ppermute | solution.py:314
  110.6 15.4 %collective-permute-start.18 = (bf16[2,192,768]{2,1,0:T(8,128)(2,1)S(1)}, bf16[2,192,768]{2,1,0:T(8,128)(2,1)S(1)}, u32[]{:S(2)}, u32[]{:S(2)}) collective-permute-start(bf16[2,192,768]{2,1,0:T(8,128)(2,1)S(1)} %get-tuple-element.131), channel_id=1, source_target_pairs={{0,8},{4,12},{8,0},{12,4},{16,24},{20,28},{24,16},{28,20},{1,9},{5... | collective-permute-start | bytes 1769480 | tf_op jit(solution)/shard_map/ppermute | solution.py:314
  112.1 15.3 %collective-permute-start.19 = (bf16[2,192,768]{2,1,0:T(8,128)(2,1)S(1)}, bf16[2,192,768]{2,1,0:T(8,128)(2,1)S(1)}, u32[]{:S(2)}, u32[]{:S(2)}) collective-permute-start(bf16[2,192,768]{2,1,0:T(8,128)(2,1)S(1)} %get-tuple-element.133), channel_id=1, source_target_pairs={{0,16},{4,20},{8,24},{12,28},{16,0},{20,4},{24,8},{28,12},{1,17},{... | collective-permute-start | bytes 1769480 | tf_op jit(solution)/shard_map/ppermute | solution.py:314
  117.7 49.0 %collective-permute-start.15 = (bf16[64,4224]{1,0:T(8,128)(2,1)S(1)}, bf16[64,4224]{1,0:T(8,128)(2,1)S(1)}, u32[]{:S(2)}, u32[]{:S(2)}) collective-permute-start(bf16[64,4224]{1,0:T(8,128)(2,1)S(1)} %get-tuple-element.127), channel_id=1, source_target_pairs={{0,3},{1,2},{2,1},{3,0},{4,7},{5,6},{6,5},{7,4},{8,11},{9,10},{10,... | collective-permute-start | bytes 1622024 | tf_op jit(solution)/shard_map/ppermute | solution.py:314
  119.5 47.2 %collective-permute-start.16 = (bf16[64,4224]{1,0:T(8,128)(2,1)S(1)}, bf16[64,4224]{1,0:T(8,128)(2,1)S(1)}, u32[]{:S(2)}, u32[]{:S(2)}) collective-permute-start(bf16[64,4224]{1,0:T(8,128)(2,1)S(1)} %get-tuple-element.128), channel_id=1, source_target_pairs={{0,2},{1,3},{2,0},{3,1},{4,6},{5,7},{6,4},{7,5},{8,10},{9,11},{10,... | collective-permute-start | bytes 1622024 | tf_op jit(solution)/shard_map/ppermute | solution.py:314
  119.5 47.2 %collective-permute-start.17 = (bf16[64,4224]{1,0:T(8,128)(2,1)S(1)}, bf16[64,4224]{1,0:T(8,128)(2,1)S(1)}, u32[]{:S(2)}, u32[]{:S(2)}) collective-permute-start(bf16[64,4224]{1,0:T(8,128)(2,1)S(1)} %get-tuple-element.129), channel_id=1, source_target_pairs={{0,1},{1,0},{2,3},{3,2},{4,5},{5,4},{6,7},{7,6},{8,9},{9,8},{10,11... | collective-permute-start | bytes 1622024 | tf_op jit(solution)/shard_map/ppermute | solution.py:314
  126.0 35.5 %collective-permute-start.23 = (bf16[2,512,768]{2,1,0:T(8,128)(2,1)S(1)}, bf16[2,512,768]{2,1,0:T(8,128)(2,1)S(1)}, u32[]{:S(2)}, u32[]{:S(2)}) collective-permute-start(bf16[2,512,768]{2,1,0:T(8,128)(2,1)S(1)} %get-tuple-element.141), channel_id=1, source_target_pairs={{0,8},{4,12},{8,0},{12,4},{16,24},{20,28},{24,16},{28,20},{1,9},{5... | collective-permute-start | bytes 4718600 | tf_op jit(solution)/shard_map/ppermute | solution.py:314
  127.4 35.3 %collective-permute-start.24 = (bf16[2,512,768]{2,1,0:T(8,128)(2,1)S(1)}, bf16[2,512,768]{2,1,0:T(8,128)(2,1)S(1)}, u32[]{:S(2)}, u32[]{:S(2)}) collective-permute-start(bf16[2,512,768]{2,1,0:T(8,128)(2,1)S(1)} %get-tuple-element.144), channel_id=1, source_target_pairs={{0,16},{4,20},{8,24},{12,28},{16,0},{20,4},{24,8},{28,12},{1,17},{... | collective-permute-start | bytes 4718600 | tf_op jit(solution)/shard_map/ppermute | solution.py:314
  163.6 23.9 %collective-permute-start.25 = (bf16[1,704,768]{2,1,0:T(8,128)(2,1)S(1)}, bf16[1,704,768]{2,1,0:T(8,128)(2,1)S(1)}, u32[]{:S(2)}, u32[]{:S(2)}) collective-permute-start(bf16[1,704,768]{2,1,0:T(8,128)(2,1)S(1)} %get-tuple-element.152), channel_id=1, source_target_pairs={{0,16},{4,20},{8,24},{12,28},{16,0},{20,4},{24,8},{28,12},{1,17},{... | collective-permute-start | bytes 3244040 | tf_op jit(solution)/shard_map/ppermute | solution.py:314
  165.2 23.5 %collective-permute-start.26 = (bf16[1,704,768]{2,1,0:T(8,128)(2,1)S(1)}, bf16[1,704,768]{2,1,0:T(8,128)(2,1)S(1)}, u32[]{:S(2)}, u32[]{:S(2)}) collective-permute-start(bf16[1,704,768]{2,1,0:T(8,128)(2,1)S(1)} %get-tuple-element.154), channel_id=1, source_target_pairs={{0,8},{4,12},{8,0},{12,4},{16,24},{20,28},{24,16},{28,20},{1,9},{5... | collective-permute-start | bytes 3244040 | tf_op jit(solution)/shard_map/ppermute | solution.py:314
  (5 other events, 77.7 us)

commit v7 on v6

--- a/solution.py
+++ b/solution.py
@@ -68,7 +68,9 @@
     top, tok = routes_ref.shape
     index = lax.broadcasted_iota(jnp.int32, (slots, tok), 0)
     block = index // CAP
-    expert = jnp.where(block == 0, 0, slots // CAP - block) ^ my_expert
+    experts = slots // CAP
+    turned = jnp.where(block == 1, experts - 2, jnp.where(block == 2, experts - 1, experts - block))
+    expert = jnp.where(block == 0, 0, turned) ^ my_expert
     hit = jnp.zeros((slots, tok), jnp.bool_)
     for k in range(top):
         hit = hit | (routes_ref[k : k + 1, :] == expert)
@@ -336,7 +338,9 @@
         return out[:-1]
 
     def exchange(blocks):
-        return [blocks[0]] + [flip(blocks[j], "expert", experts - j) for j in range(1, experts)]
+        places = [experts - 2, experts - 1] + [experts - j for j in range(3, experts)]
+        moved = [flip(block, "expert", at) for block, at in zip(blocks[1:], places)]
+        return [blocks[0]] + moved
 
     def block_specs(cols, at):
         return [pl.BlockSpec((CAP, cols), at) for _ in range(experts)]

time: 192 us -> 192 us (level)
  starting transfers between devices: 53.7 us -> 37.5 us
  waiting for transfers between devices: 100 us -> 115 us
    ppermute x27, starting transfers between devices: 53.7 us -> 37.5 us  [flip(): return lax.ppermute(x, axis, [(i, i ^ bit) for i in range(count)])]
    ppermute x27, waiting for transfers between devices: 100 us -> 115 us  [flip(): return lax.ppermute(x, axis, [(i, i ^ bit) for i in range(count)])]
  transfers between devices with their start and end apart: 27 -> 27, of which waited for: 13 -> 12; matrix products, arithmetic and copies ran while one was open for 0% -> 0% of each run, Pallas kernels for 15% -> 15%
where the time goes in v7:
time: 192 us; the launch traced here: 191 us
  waiting for transfers between devices  115 us (60%)
  starting transfers between devices  37.5 us (20%)
  Pallas kernels  36.7 us (19%)
    ppermute x27, waiting for transfers between devices, flip(): return lax.ppermute(x, axis, [(i, i ^ bit) for i in range(count)])  115 us
    ppermute x27, starting transfers between devices, flip(): return lax.ppermute(x, axis, [(i, i ^ bit) for i in range(count)])  37.5 us
    pallas_call x23, Pallas kernels, call(): pl.pallas_call(ordered, grid_spec=pltpu.PrefetchScalarGridSpec(num_scalar...  36.7 us
  transfers between devices with their start and end apart: 27, of which 12 were waited for; matrix products, arithmetic and copies ran while one was open for 0% of the time, Pallas kernels for 15%

profile of v7, /device:TPU:0, one launch (start us, length us, event | category | flops | bytes accessed | tf_op | source)
XLA Modules:
  0.0 191.1 jit_solution(9058325165968782773)
XLA Ops:
  1.9 1.4 shard_map.111
  3.3 4.1 %collective-permute-start = (bf16[64,4096]{1,0:T(8,128)(2,1)S(1)}, bf16[64,4096]{1,0:T(8,128)(2,1)S(1)}, u32[]{:S(2)}, u32[]{:S(2)}) collective-permute-start(bf16[64,4096]{1,0:T(8,128)(2,1)S(1)} %get-tuple-element.83), channel_id=1, source_target_pairs={{0,2},{1,3},{2,0},{3,1},{4,6},{5,7},{6,4},{7,5},{8,10},{9,11},{10,... | collective-permute-start | bytes 1572872 | tf_op jit(solution)/shard_map/ppermute | solution.py:316
  7.4 1.3 collective-permute-start.1
  9.6 33.1 %collective-permute-done.refs_5_.refs_2_ = bf16[64,4096]{1,0:T(8,128)(2,1)S(1)} collective-permute-done((bf16[64,4096]{1,0:T(8,128)(2,1)S(1)}, bf16[64,4096]{1,0:T(8,128)(2,1)S(1)}, u32[]{:S(2)}, u32[]{:S(2)}) %collective-permute-start) | collective-permute-done | bytes 524320 | tf_op jit(solution)/shard_map/ppermute | solution.py:316
  43.7 2.9 %collective-permute-start.4 = (bf16[64,1024]{1,0:T(8,128)(2,1)S(1)}, bf16[64,1024]{1,0:T(8,128)(2,1)S(1)}, u32[]{:S(2)}, u32[]{:S(2)}) collective-permute-start(bf16[64,1024]{1,0:T(8,128)(2,1)S(1)} %get-tuple-element.93), channel_id=1, source_target_pairs={{0,3},{1,2},{2,1},{3,0},{4,7},{5,6},{6,5},{7,4},{8,11},{9,10},{10,... | collective-permute-start | bytes 393224 | tf_op jit(solution)/shard_map/ppermute | solution.py:316
  47.2 1.2 shard_map.114
  48.5 4.2 %shard_map.115 = (bf16[256,768]{1,0:T(8,128)(2,1)S(1)}, bf16[768,256]{1,0:T(8,128)(2,1)S(1)}, f32[768,256]{1,0:T(8,128)S(1)}, f32[768,256]{1,0:T(8,128)S(1)}, f32[8,128]{1,0:T(8,128)S(1)}) custom-call(s32[2]{0:T(128)S(1)} %pad_add_fusion.refs_0_, bf16[64,4096]{1,0:T(8,128)(2,1)S(1)} %get-tuple-element.85.refs_1_, ...), custom_call_target="tpu_custom_call" | custom-call | flops 1 | bytes 1 | tf_op jit(solution)/shard_map/pallas_call | solution.py:39
  52.7 9.6 %collective-permute-done.3.refs_3_ = bf16[64,1024]{1,0:T(8,128)(2,1)S(1)} collective-permute-done((bf16[64,1024]{1,0:T(8,128)(2,1)S(1)}, bf16[64,1024]{1,0:T(8,128)(2,1)S(1)}, u32[]{:S(2)}, u32[]{:S(2)}) %collective-permute-start.3) | collective-permute-done | bytes 131104 | tf_op jit(solution)/shard_map/ppermute | solution.py:316
  63.5 4.7 %collective-permute-start.6 = (bf16[64,3072]{1,0:T(8,128)(2,1)S(1)}, bf16[64,3072]{1,0:T(8,128)(2,1)S(1)}, u32[]{:S(2)}, u32[]{:S(2)}) collective-permute-start(bf16[64,3072]{1,0:T(8,128)(2,1)S(1)} %get-tuple-element.98), channel_id=1, source_target_pairs={{0,2},{1,3},{2,0},{3,1},{4,6},{5,7},{6,4},{7,5},{8,10},{9,11},{10,... | collective-permute-start | bytes 1179656 | tf_op jit(solution)/shard_map/ppermute | solution.py:316
  69.7 1.5 collective-permute-start.10
  71.3 1.5 collective-permute-start.11
  74.0 2.4 %collective-permute-done.10.refs_2_ = bf16[2,64,768]{2,1,0:T(8,128)(2,1)S(1)} collective-permute-done((bf16[2,64,768]{2,1,0:T(8,128)(2,1)S(1)}, bf16[2,64,768]{2,1,0:T(8,128)(2,1)S(1)}, u32[]{:S(2)}, u32[]{:S(2)}) %collective-permute-start.10) | collective-permute-done | bytes 196640 | tf_op jit(solution)/shard_map/ppermute | solution.py:316
  78.2 1.6 collective-permute-start.12
  80.3 2.6 %collective-permute-done.12.refs_3_ = bf16[1,64,768]{2,1,0:T(8,128)(2,1)S(1)} collective-permute-done((bf16[1,64,768]{2,1,0:T(8,128)(2,1)S(1)}, bf16[1,64,768]{2,1,0:T(8,128)(2,1)S(1)}, u32[]{:S(2)}, u32[]{:S(2)}) %collective-permute-start.12) | collective-permute-done | bytes 98336 | tf_op jit(solution)/shard_map/ppermute | solution.py:316
  82.9 1.5 collective-permute-done.13.refs_6_
  85.0 10.0 %collective-permute-done.6.refs_4_ = bf16[64,3072]{1,0:T(8,128)(2,1)S(1)} collective-permute-done((bf16[64,3072]{1,0:T(8,128)(2,1)S(1)}, bf16[64,3072]{1,0:T(8,128)(2,1)S(1)}, u32[]{:S(2)}, u32[]{:S(2)}) %collective-permute-start.6) | collective-permute-done | bytes 393248 | tf_op jit(solution)/shard_map/ppermute | solution.py:316
  96.1 1.8 shard_map.121
  98.0 2.5 %shard_map.122 = (bf16[256,1536]{1,0:T(8,128)(2,1)S(1)}, bf16[1536,256]{1,0:T(8,128)(2,1)S(1)}, f32[1,256]{1,0:T(1,128)S(1)}, f32[8,128]{1,0:T(8,128)S(1)}) custom-call(s32[2]{0:T(128)S(1)} %pad_add_fusion.refs_0_, bf16[1,768,4096]{2,1,0:T(8,128)(2,1)S(1)} %bitcast.13, bf16[4096,256]{1,0:T(8,128)(2,1)S(1)} %get-tuple-element.113.refs_2_.refs_1_, ...), custom_call_target="tpu_custom_call" | custom-call | flops 1 | bytes 1 | tf_op jit(solution)/shard_map/pallas_call | solution.py:39
  100.4 2.3 %shard_map.123 = (bf16[2048,512]{1,0:T(8,128)(2,1)S(1)}, bf16[2048,512]{1,0:T(8,128)(2,1)S(1)}, bf16[2048,512]{1,0:T(8,128)(2,1)S(1)}, f32[8,128]{1,0:T(8,128)S(1)}) custom-call(s32[2]{0:T(128)S(1)} %pad_add_fusion.refs_0_, bf16[4096,256]{1,0:T(8,128)(2,1)S(1)} %get-tuple-element.121.refs_1_, bf16[256,1536]{1,0:T(8,128)(2,1)S(1)} %get-tuple-element.122.refs_2_, ...), custom_call_target="tpu_custom_call" | custom-call | flops 1 | bytes 1 | tf_op jit(solution)/shard_map/pallas_call | solution.py:39
  103.8 1.3 shard_map.124
  105.2 1.6 collective-permute-start.18
  106.7 1.5 collective-permute-start.19
  108.3 4.2 %shard_map.125 = (bf16[64,4224]{1,0:T(8,128)(2,1)S(1)}, bf16[64,4224]{1,0:T(8,128)(2,1)S(1)}, bf16[64,4224]{1,0:T(8,128)(2,1)S(1)}, bf16[64,4224]{1,0:T(8,128)(2,1)S(1)}, f32[8,128]{1,0:T(8,128)S(1)}) custom-call(s32[2]{0:T(128)S(1)} %pad_add_fusion.refs_0_, bf16[1536,256]{1,0:T(8,128)(2,1)S(1)} %get-tuple-element.118.refs_1_, ...), custom_call_target="tpu_custom_call" | custom-call | flops 1 | bytes 1 | tf_op jit(solution)/shard_map/pallas_call | solution.py:39
  112.5 7.1 %collective-permute-start.15 = (bf16[64,4224]{1,0:T(8,128)(2,1)S(1)}, bf16[64,4224]{1,0:T(8,128)(2,1)S(1)}, u32[]{:S(2)}, u32[]{:S(2)}) collective-permute-start(bf16[64,4224]{1,0:T(8,128)(2,1)S(1)} %get-tuple-element.127), channel_id=1, source_target_pairs={{0,2},{1,3},{2,0},{3,1},{4,6},{5,7},{6,4},{7,5},{8,10},{9,11},{10,... | collective-permute-start | bytes 1622024 | tf_op jit(solution)/shard_map/ppermute | solution.py:316
  119.6 3.0 %collective-permute-start.16 = (bf16[64,4224]{1,0:T(8,128)(2,1)S(1)}, bf16[64,4224]{1,0:T(8,128)(2,1)S(1)}, u32[]{:S(2)}, u32[]{:S(2)}) collective-permute-start(bf16[64,4224]{1,0:T(8,128)(2,1)S(1)} %get-tuple-element.128), channel_id=1, source_target_pairs={{0,3},{1,2},{2,1},{3,0},{4,7},{5,6},{6,5},{7,4},{8,11},{9,10},{10,... | collective-permute-start | bytes 1622024 | tf_op jit(solution)/shard_map/ppermute | solution.py:316
  122.6 2.4 %shard_map.126 = (bf16[2,512,768]{2,1,0:T(8,128)(2,1)S(1)}, bf16[2,512,768]{2,1,0:T(8,128)(2,1)S(1)}, bf16[2,512,768]{2,1,0:T(8,128)(2,1)S(1)}, bf16[2,512,768]{2,1,0:T(8,128)(2,1)S(1)}, f32[8,128]{1,0:T(8,128)S(1)}) custom-call(s32[2]{0:T(128)S(1)} %pad_add_fusion.refs_0_, bf16[4096,256]{1,0:T(8,128)(2,1)S(1)} %get-tuple-element.121.refs_1_, ...), custom_call_target="tpu_custom_call" | custom-call | flops 1 | bytes 1 | tf_op jit(solution)/shard_map/pallas_call | solution.py:39
  127.7 32.6 %collective-permute-done.23.refs_3_.refs_5_ = bf16[2,512,768]{2,1,0:T(8,128)(2,1)S(1)} collective-permute-done((bf16[2,512,768]{2,1,0:T(8,128)(2,1)S(1)}, bf16[2,512,768]{2,1,0:T(8,128)(2,1)S(1)}, u32[]{:S(2)}, u32[]{:S(2)}) %collective-permute-start.23) | collective-permute-done | bytes 1572896 | tf_op jit(solution)/shard_map/ppermute | solution.py:316
  161.8 1.6 collective-permute-start.25
  164.9 2.6 %shard_map.131 = (bf16[128,4096]{1,0:T(8,128)(2,1)}, bf16[2,128]{1,0:T(2,128)(2,1)}, f32[8,128]{1,0:T(8,128)S(1)}) custom-call(s32[2]{0:T(128)S(1)} %pad_add_fusion.refs_0_, bf16[128,256]{1,0:T(8,128)(2,1)S(1)} %get-tuple-element.84.refs_1_, s32[2,128]{1,0:T(2,128)S(1)} %bitcast.17, bf16[2,128]{1,0:T(2,128)(2,1)S(1)} %bitcast.20, ...), custom_call_target="tpu_custom_call" | custom-call | flops 60000002048 | bytes 1 | tf_op jit(solution)/shard_map/pallas_call | solution.py:39
  167.5 18.8 %collective-permute-done.25.refs_3_ = bf16[1,704,768]{2,1,0:T(8,128)(2,1)S(1)} collective-permute-done((bf16[1,704,768]{2,1,0:T(8,128)(2,1)S(1)}, bf16[1,704,768]{2,1,0:T(8,128)(2,1)S(1)}, u32[]{:S(2)}, u32[]{:S(2)}) %collective-permute-start.25) | collective-permute-done | bytes 1081376 | tf_op jit(solution)/shard_map/ppermute | solution.py:316
  186.3 1.5 collective-permute-done.26.refs_5_
  187.8 3.2 %shard_map.132 = (f32[768,512]{1,0:T(8,128)}, f32[512,768]{1,0:T(8,128)}, f32[512,768]{1,0:T(8,128)}, f32[8,128]{1,0:T(8,128)}) custom-call(s32[2]{0:T(128)S(1)} %pad_add_fusion.refs_0_, f32[128,768]{1,0:T(8,128)S(1)} %get-tuple-element.150.refs_1_, bf16[1,704,768]{2,1,0:T(8,128)(2,1)S(1)} %get-tuple-element.151.refs_2_, ...), custom_call_target="tpu_custom_call" | custom-call | flops 1 | bytes 1 | tf_op jit(solution)/shard_map/pallas_call | solution.py:39
  (69 shorter events, 18.4 us)
Async XLA Ops:
  0.7 97.2 %slice-start.4 = ((s8[6291456]{0:T(1024)(128)(4,1)}), s8[4194304]{0:T(1024)(128)(4,1)S(1)}, s32[]{:S(2)}) async-start(s8[6291456]{0:T(1024)(128)(4,1)} %bitcast.12), calls=%async_computation.4 | async-start | bytes 8388608
  3.3 39.4 %collective-permute-start = (bf16[64,4096]{1,0:T(8,128)(2,1)S(1)}, bf16[64,4096]{1,0:T(8,128)(2,1)S(1)}, u32[]{:S(2)}, u32[]{:S(2)}) collective-permute-start(bf16[64,4096]{1,0:T(8,128)(2,1)S(1)} %get-tuple-element.83), channel_id=1, source_target_pairs={{0,2},{1,3},{2,0},{3,1},{4,6},{5,7},{6,4},{7,5},{8,10},{9,11},{10,... | collective-permute-start | bytes 1572872 | tf_op jit(solution)/shard_map/ppermute | solution.py:316
  7.4 41.0 %collective-permute-start.1 = (bf16[64,4096]{1,0:T(8,128)(2,1)S(1)}, bf16[64,4096]{1,0:T(8,128)(2,1)S(1)}, u32[]{:S(2)}, u32[]{:S(2)}) collective-permute-start(bf16[64,4096]{1,0:T(8,128)(2,1)S(1)} %get-tuple-element.86), channel_id=1, source_target_pairs={{0,3},{1,2},{2,1},{3,0},{4,7},{5,6},{6,5},{7,4},{8,11},{9,10},{10,... | collective-permute-start | bytes 1572872 | tf_op jit(solution)/shard_map/ppermute | solution.py:316
  8.7 39.7 %collective-permute-start.2 = (bf16[64,4096]{1,0:T(8,128)(2,1)S(1)}, bf16[64,4096]{1,0:T(8,128)(2,1)S(1)}, u32[]{:S(2)}, u32[]{:S(2)}) collective-permute-start(bf16[64,4096]{1,0:T(8,128)(2,1)S(1)} %get-tuple-element.87), channel_id=1, source_target_pairs={{0,1},{1,0},{2,3},{3,2},{4,5},{5,4},{6,7},{7,6},{8,9},{9,8},{10,11... | collective-permute-start | bytes 1572872 | tf_op jit(solution)/shard_map/ppermute | solution.py:316
  9.0 39.5 %slice-start.2 = ((s8[6291456]{0:T(1024)(128)(4,1)}), s8[4194304]{0:T(1024)(128)(4,1)S(1)}, s32[]{:S(2)}) async-start(s8[6291456]{0:T(1024)(128)(4,1)} %bitcast.10), calls=%async_computation.2 | async-start | bytes 8388608
  9.0 39.5 %slice-start.1 = ((s8[6291456]{0:T(1024)(128)(4,1)}), s8[2097152]{0:T(1024)(128)(4,1)S(1)}, s32[]{:S(2)}) async-start(s8[6291456]{0:T(1024)(128)(4,1)} %bitcast.8), calls=%async_computation.1 | async-start | bytes 4194304
  9.0 39.5 %slice-start.3 = ((s8[6291456]{0:T(1024)(128)(4,1)}), s8[2097152]{0:T(1024)(128)(4,1)S(1)}, s32[]{:S(2)}) async-start(s8[6291456]{0:T(1024)(128)(4,1)} %bitcast.10), calls=%async_computation.3 | async-start | bytes 4194304
  9.0 88.9 %slice-start.5 = ((s8[6291456]{0:T(1024)(128)(4,1)}), s8[2097152]{0:T(1024)(128)(4,1)S(1)}, s32[]{:S(2)}) async-start(s8[6291456]{0:T(1024)(128)(4,1)} %bitcast.12), calls=%async_computation.5 | async-start | bytes 4194304
  43.6 18.7 %collective-permute-start.3 = (bf16[64,1024]{1,0:T(8,128)(2,1)S(1)}, bf16[64,1024]{1,0:T(8,128)(2,1)S(1)}, u32[]{:S(2)}, u32[]{:S(2)}) collective-permute-start(bf16[64,1024]{1,0:T(8,128)(2,1)S(1)} %get-tuple-element.92), channel_id=1, source_target_pairs={{0,2},{1,3},{2,0},{3,1},{4,6},{5,7},{6,4},{7,5},{8,10},{9,11},{10,... | collective-permute-start | bytes 393224 | tf_op jit(solution)/shard_map/ppermute | solution.py:316
  43.7 18.6 %collective-permute-start.4 = (bf16[64,1024]{1,0:T(8,128)(2,1)S(1)}, bf16[64,1024]{1,0:T(8,128)(2,1)S(1)}, u32[]{:S(2)}, u32[]{:S(2)}) collective-permute-start(bf16[64,1024]{1,0:T(8,128)(2,1)S(1)} %get-tuple-element.93), channel_id=1, source_target_pairs={{0,3},{1,2},{2,1},{3,0},{4,7},{5,6},{6,5},{7,4},{8,11},{9,10},{10,... | collective-permute-start | bytes 393224 | tf_op jit(solution)/shard_map/ppermute | solution.py:316
  46.6 15.7 %collective-permute-start.5 = (bf16[64,1024]{1,0:T(8,128)(2,1)S(1)}, bf16[64,1024]{1,0:T(8,128)(2,1)S(1)}, u32[]{:S(2)}, u32[]{:S(2)}) collective-permute-start(bf16[64,1024]{1,0:T(8,128)(2,1)S(1)} %get-tuple-element.94), channel_id=1, source_target_pairs={{0,1},{1,0},{2,3},{3,2},{4,5},{5,4},{6,7},{7,6},{8,9},{9,8},{10,11... | collective-permute-start | bytes 393224 | tf_op jit(solution)/shard_map/ppermute | solution.py:316
  63.4 5.4 %collective-permute-start.9 = (bf16[512,768]{1,0:T(8,128)(2,1)S(1)}, bf16[512,768]{1,0:T(8,128)(2,1)S(1)}, u32[]{:S(2)}, u32[]{:S(2)}) collective-permute-start(bf16[512,768]{1,0:T(8,128)(2,1)S(1)} %get-tuple-element.101), channel_id=1, source_target_pairs={{0,4},{4,0},{8,12},{12,8},{16,20},{20,16},{24,28},{28,24},{1,5},{5... | collective-permute-start | bytes 2359304 | tf_op jit(solution)/shard_map/ppermute | solution.py:316
  63.5 31.5 %collective-permute-start.6 = (bf16[64,3072]{1,0:T(8,128)(2,1)S(1)}, bf16[64,3072]{1,0:T(8,128)(2,1)S(1)}, u32[]{:S(2)}, u32[]{:S(2)}) collective-permute-start(bf16[64,3072]{1,0:T(8,128)(2,1)S(1)} %get-tuple-element.98), channel_id=1, source_target_pairs={{0,2},{1,3},{2,0},{3,1},{4,6},{5,7},{6,4},{7,5},{8,10},{9,11},{10,... | collective-permute-start | bytes 1179656 | tf_op jit(solution)/shard_map/ppermute | solution.py:316
  68.2 26.9 %collective-permute-start.7 = (bf16[64,3072]{1,0:T(8,128)(2,1)S(1)}, bf16[64,3072]{1,0:T(8,128)(2,1)S(1)}, u32[]{:S(2)}, u32[]{:S(2)}) collective-permute-start(bf16[64,3072]{1,0:T(8,128)(2,1)S(1)} %get-tuple-element.99), channel_id=1, source_target_pairs={{0,3},{1,2},{2,1},{3,0},{4,7},{5,6},{6,5},{7,4},{8,11},{9,10},{10,... | collective-permute-start | bytes 1179656 | tf_op jit(solution)/shard_map/ppermute | solution.py:316
  68.6 27.5 %collective-permute-start.8 = (bf16[64,3072]{1,0:T(8,128)(2,1)S(1)}, bf16[64,3072]{1,0:T(8,128)(2,1)S(1)}, u32[]{:S(2)}, u32[]{:S(2)}) collective-permute-start(bf16[64,3072]{1,0:T(8,128)(2,1)S(1)} %get-tuple-element.100), channel_id=1, source_target_pairs={{0,1},{1,0},{2,3},{3,2},{4,5},{5,4},{6,7},{7,6},{8,9},{9,8},{10,11... | collective-permute-start | bytes 1179656 | tf_op jit(solution)/shard_map/ppermute | solution.py:316
  69.7 6.7 %collective-permute-start.10 = (bf16[2,64,768]{2,1,0:T(8,128)(2,1)S(1)}, bf16[2,64,768]{2,1,0:T(8,128)(2,1)S(1)}, u32[]{:S(2)}, u32[]{:S(2)}) collective-permute-start(bf16[2,64,768]{2,1,0:T(8,128)(2,1)S(1)} %get-tuple-element.104), channel_id=1, source_target_pairs={{0,8},{4,12},{8,0},{12,4},{16,24},{20,28},{24,16},{28,20},{1,9},{5... | collective-permute-start | bytes 589832 | tf_op jit(solution)/shard_map/ppermute | solution.py:316
  71.3 6.3 %collective-permute-start.11 = (bf16[2,64,768]{2,1,0:T(8,128)(2,1)S(1)}, bf16[2,64,768]{2,1,0:T(8,128)(2,1)S(1)}, u32[]{:S(2)}, u32[]{:S(2)}) collective-permute-start(bf16[2,64,768]{2,1,0:T(8,128)(2,1)S(1)} %get-tuple-element.106), channel_id=1, source_target_pairs={{0,16},{4,20},{8,24},{12,28},{16,0},{20,4},{24,8},{28,12},{1,17},{... | collective-permute-start | bytes 589832 | tf_op jit(solution)/shard_map/ppermute | solution.py:316
  78.2 4.7 %collective-permute-start.12 = (bf16[1,64,768]{2,1,0:T(8,128)(2,1)S(1)}, bf16[1,64,768]{2,1,0:T(8,128)(2,1)S(1)}, u32[]{:S(2)}, u32[]{:S(2)}) collective-permute-start(bf16[1,64,768]{2,1,0:T(8,128)(2,1)S(1)} %get-tuple-element.109), channel_id=1, source_target_pairs={{0,16},{4,20},{8,24},{12,28},{16,0},{20,4},{24,8},{28,12},{1,17},{... | collective-permute-start | bytes 294920 | tf_op jit(solution)/shard_map/ppermute | solution.py:316
  79.8 4.6 %collective-permute-start.13 = (bf16[1,64,768]{2,1,0:T(8,128)(2,1)S(1)}, bf16[1,64,768]{2,1,0:T(8,128)(2,1)S(1)}, u32[]{:S(2)}, u32[]{:S(2)}) collective-permute-start(bf16[1,64,768]{2,1,0:T(8,128)(2,1)S(1)} %get-tuple-element.110), channel_id=1, source_target_pairs={{0,8},{4,12},{8,0},{12,4},{16,24},{20,28},{24,16},{28,20},{1,9},{5... | collective-permute-start | bytes 294920 | tf_op jit(solution)/shard_map/ppermute | solution.py:316
  97.9 6.0 %collective-permute-start.14 = (bf16[1536,768]{1,0:T(8,128)(2,1)S(1)}, bf16[1536,768]{1,0:T(8,128)(2,1)S(1)}, u32[]{:S(2)}, u32[]{:S(2)}) collective-permute-start(bf16[1536,768]{1,0:T(8,128)(2,1)S(1)} %get-tuple-element.120), channel_id=1, source_target_pairs={{0,4},{4,0},{8,12},{12,8},{16,20},{20,16},{24,28},{28,24},{1,5},{5... | collective-permute-start | bytes 7077896 | tf_op jit(solution)/shard_map/ppermute | solution.py:316
  102.8 9.7 %collective-permute-start.20 = (bf16[2048,512]{1,0:T(8,128)(2,1)S(1)}, bf16[2048,512]{1,0:T(8,128)(2,1)S(1)}, u32[]{:S(2)}, u32[]{:S(2)}) collective-permute-start(bf16[2048,512]{1,0:T(8,128)(2,1)S(1)} %get-tuple-element.134), channel_id=1, source_target_pairs={{0,4},{4,0},{8,12},{12,8},{16,20},{20,16},{24,28},{28,24},{1,5},{5... | collective-permute-start | bytes 6291464 | tf_op jit(solution)/shard_map/ppermute | solution.py:316
  103.3 16.3 %collective-permute-start.21 = (bf16[2048,512]{1,0:T(8,128)(2,1)S(1)}, bf16[2048,512]{1,0:T(8,128)(2,1)S(1)}, u32[]{:S(2)}, u32[]{:S(2)}) collective-permute-start(bf16[2048,512]{1,0:T(8,128)(2,1)S(1)} %get-tuple-element.135), channel_id=1, source_target_pairs={{0,4},{4,0},{8,12},{12,8},{16,20},{20,16},{24,28},{28,24},{1,5},{5... | collective-permute-start | bytes 6291464 | tf_op jit(solution)/shard_map/ppermute | solution.py:316
  103.4 19.2 %collective-permute-start.22 = (bf16[2048,512]{1,0:T(8,128)(2,1)S(1)}, bf16[2048,512]{1,0:T(8,128)(2,1)S(1)}, u32[]{:S(2)}, u32[]{:S(2)}) collective-permute-start(bf16[2048,512]{1,0:T(8,128)(2,1)S(1)} %get-tuple-element.136), channel_id=1, source_target_pairs={{0,4},{4,0},{8,12},{12,8},{16,20},{20,16},{24,28},{28,24},{1,5},{5... | collective-permute-start | bytes 6291464 | tf_op jit(solution)/shard_map/ppermute | solution.py:316
  105.2 19.8 %collective-permute-start.18 = (bf16[2,192,768]{2,1,0:T(8,128)(2,1)S(1)}, bf16[2,192,768]{2,1,0:T(8,128)(2,1)S(1)}, u32[]{:S(2)}, u32[]{:S(2)}) collective-permute-start(bf16[2,192,768]{2,1,0:T(8,128)(2,1)S(1)} %get-tuple-element.131), channel_id=1, source_target_pairs={{0,8},{4,12},{8,0},{12,4},{16,24},{20,28},{24,16},{28,20},{1,9},{5... | collective-permute-start | bytes 1769480 | tf_op jit(solution)/shard_map/ppermute | solution.py:316
  106.7 18.8 %collective-permute-start.19 = (bf16[2,192,768]{2,1,0:T(8,128)(2,1)S(1)}, bf16[2,192,768]{2,1,0:T(8,128)(2,1)S(1)}, u32[]{:S(2)}, u32[]{:S(2)}) collective-permute-start(bf16[2,192,768]{2,1,0:T(8,128)(2,1)S(1)} %get-tuple-element.133), channel_id=1, source_target_pairs={{0,16},{4,20},{8,24},{12,28},{16,0},{20,4},{24,8},{28,12},{1,17},{... | collective-permute-start | bytes 1769480 | tf_op jit(solution)/shard_map/ppermute | solution.py:316
  112.5 52.4 %collective-permute-start.15 = (bf16[64,4224]{1,0:T(8,128)(2,1)S(1)}, bf16[64,4224]{1,0:T(8,128)(2,1)S(1)}, u32[]{:S(2)}, u32[]{:S(2)}) collective-permute-start(bf16[64,4224]{1,0:T(8,128)(2,1)S(1)} %get-tuple-element.127), channel_id=1, source_target_pairs={{0,2},{1,3},{2,0},{3,1},{4,6},{5,7},{6,4},{7,5},{8,10},{9,11},{10,... | collective-permute-start | bytes 1622024 | tf_op jit(solution)/shard_map/ppermute | solution.py:316
  119.6 45.2 %collective-permute-start.16 = (bf16[64,4224]{1,0:T(8,128)(2,1)S(1)}, bf16[64,4224]{1,0:T(8,128)(2,1)S(1)}, u32[]{:S(2)}, u32[]{:S(2)}) collective-permute-start(bf16[64,4224]{1,0:T(8,128)(2,1)S(1)} %get-tuple-element.128), channel_id=1, source_target_pairs={{0,3},{1,2},{2,1},{3,0},{4,7},{5,6},{6,5},{7,4},{8,11},{9,10},{10,... | collective-permute-start | bytes 1622024 | tf_op jit(solution)/shard_map/ppermute | solution.py:316
  122.6 42.3 %collective-permute-start.17 = (bf16[64,4224]{1,0:T(8,128)(2,1)S(1)}, bf16[64,4224]{1,0:T(8,128)(2,1)S(1)}, u32[]{:S(2)}, u32[]{:S(2)}) collective-permute-start(bf16[64,4224]{1,0:T(8,128)(2,1)S(1)} %get-tuple-element.129), channel_id=1, source_target_pairs={{0,1},{1,0},{2,3},{3,2},{4,5},{5,4},{6,7},{7,6},{8,9},{9,8},{10,11... | collective-permute-start | bytes 1622024 | tf_op jit(solution)/shard_map/ppermute | solution.py:316
  125.0 35.3 %collective-permute-start.23 = (bf16[2,512,768]{2,1,0:T(8,128)(2,1)S(1)}, bf16[2,512,768]{2,1,0:T(8,128)(2,1)S(1)}, u32[]{:S(2)}, u32[]{:S(2)}) collective-permute-start(bf16[2,512,768]{2,1,0:T(8,128)(2,1)S(1)} %get-tuple-element.141), channel_id=1, source_target_pairs={{0,8},{4,12},{8,0},{12,4},{16,24},{20,28},{24,16},{28,20},{1,9},{5... | collective-permute-start | bytes 4718600 | tf_op jit(solution)/shard_map/ppermute | solution.py:316
  125.6 35.3 %collective-permute-start.24 = (bf16[2,512,768]{2,1,0:T(8,128)(2,1)S(1)}, bf16[2,512,768]{2,1,0:T(8,128)(2,1)S(1)}, u32[]{:S(2)}, u32[]{:S(2)}) collective-permute-start(bf16[2,512,768]{2,1,0:T(8,128)(2,1)S(1)} %get-tuple-element.144), channel_id=1, source_target_pairs={{0,16},{4,20},{8,24},{12,28},{16,0},{20,4},{24,8},{28,12},{1,17},{... | collective-permute-start | bytes 4718600 | tf_op jit(solution)/shard_map/ppermute | solution.py:316
  161.8 24.5 %collective-permute-start.25 = (bf16[1,704,768]{2,1,0:T(8,128)(2,1)S(1)}, bf16[1,704,768]{2,1,0:T(8,128)(2,1)S(1)}, u32[]{:S(2)}, u32[]{:S(2)}) collective-permute-start(bf16[1,704,768]{2,1,0:T(8,128)(2,1)S(1)} %get-tuple-element.152), channel_id=1, source_target_pairs={{0,16},{4,20},{8,24},{12,28},{16,0},{20,4},{24,8},{28,12},{1,17},{... | collective-permute-start | bytes 3244040 | tf_op jit(solution)/shard_map/ppermute | solution.py:316
  163.4 24.4 %collective-permute-start.26 = (bf16[1,704,768]{2,1,0:T(8,128)(2,1)S(1)}, bf16[1,704,768]{2,1,0:T(8,128)(2,1)S(1)}, u32[]{:S(2)}, u32[]{:S(2)}) collective-permute-start(bf16[1,704,768]{2,1,0:T(8,128)(2,1)S(1)} %get-tuple-element.154), channel_id=1, source_target_pairs={{0,8},{4,12},{8,0},{12,4},{16,24},{20,28},{24,16},{28,20},{1,9},{5... | collective-permute-start | bytes 3244040 | tf_op jit(solution)/shard_map/ppermute | solution.py:316
  (5 other events, 109.3 us)
